TPU v7x, 32 devices: a whole 2x2x4 slice. The times are simulated.
32 devices in a mesh: groups: 2 (over y), expert: 16 (over z, x, core), dp: 1.
Axes of the slice: x: 2, y: 2, z: 4, core: 2. Of those that a mesh axis runs over, the one named last changes fastest.
Arguments:
- tokens: bfloat16 [4096, 1024], P(('groups', 'expert', 'dp')), parts along dimension 0, may hold values from -6 to 6
- cotangent: bfloat16 [4096, 1024], P(('groups', 'expert', 'dp')), parts along dimension 0, may hold values from -6 to 6
- routes: int32 [4096, 8], P(('groups', 'expert', 'dp')), parts along dimension 0, may hold values from 0 to 15, all different within a row; in each aligned block of 128 rows (0 to 127, 128 to 255, ...) at most 64 rows name the same one
- combine: float32 [4096, 8], P(('groups', 'expert', 'dp')), parts along dimension 0, may hold values from 0.2 to 1
- w_gate: bfloat16 [16, 1024, 384], P('expert'), may hold values from -0.1875 to 0.1875
- w_up: bfloat16 [16, 1024, 384], P('expert'), may hold values from -0.1875 to 0.1875
- w_down: bfloat16 [16, 1024, 384], P('expert'), may hold values from -0.3125 to 0.3125
Outputs:
- mixed: bfloat16 [4096, 1024], P(('groups', 'expert', 'dp')), parts along dimension 0
- grad_tokens: bfloat16 [4096, 1024], P(('groups', 'expert', 'dp')), parts along dimension 0
- grad_gate: bfloat16 [32, 1024, 384], P(('groups', 'expert'), 'dp'), parts along dimension 0
- grad_up: bfloat16 [32, 1024, 384], P(('groups', 'expert'), 'dp'), parts along dimension 0
- grad_down: bfloat16 [32, 1024, 384], P(('groups', 'expert'), 'dp'), parts along dimension 0
There are 2 independent parts, one for each index of `groups`. A program takes and returns all parts, laid end to end along the dimension named above; an argument that names none is the same for every part. Nothing has to cross between parts.
Inputs may be any that keep to these rules, and one draw needn't show every extreme that they name: `routes`: each row names 8 different experts; within each aligned block of 128 rows no expert is named more than 64 times, a bound that some block reaches; every expert is named somewhere.
All inputs are finite; a program needn't handle non-finite values.
Results may differ from a plain program's by a relative error of at most 0.012.
Values may be sent and summed in bfloat16 or wider, within the bound.
No kernel may reach another device: no remote copies, remote signals or barrier semaphores. Data moves between devices by JAX's collectives and lax.ppermute only.
A program may use at most 64 MiB of HBM per device.

v0:
```python
import jax
import jax.numpy as jnp
from jax import lax
from jax.sharding import PartitionSpec as P


def contract_last(left, right):
    return lax.dot_general(
        left, right, (((1,), (1,)), ((), ())), preferred_element_type=jnp.float32
    )


def contract_first(left, right):
    return lax.dot_general(
        left, right, (((0,), (0,)), ((), ())), preferred_element_type=jnp.float32
    )


def per_device(tokens, cotangent, routes, combine, w_gate, w_up, w_down):
    tok_dev, width = tokens.shape
    top_count = routes.shape[1]
    experts = w_gate.shape[0] * lax.axis_size("expert")
    capacity = min(tok_dev, max(2, (tok_dev * top_count + experts - 1) // experts))
    flat = routes.reshape(-1)
    onehot = (flat[:, None] == jnp.arange(experts, dtype=jnp.int32)[None, :]).astype(jnp.int32)
    rank = jnp.cumsum(onehot, axis=0) - onehot
    place = flat * capacity + jnp.sum(rank * onehot, axis=1)
    owner = jnp.arange(tok_dev * top_count, dtype=jnp.int32) // top_count

    def fill_slots(values):
        empty = jnp.zeros((experts * capacity, width), jnp.bfloat16)
        return empty.at[place].set(values).reshape(experts, capacity, width)

    def collect(returned):
        picked = returned.reshape(-1, width)[place].astype(jnp.float32)
        return picked.reshape(tok_dev, top_count, width)

    outgoing = fill_slots(tokens[owner])
    weighted = (combine.reshape(-1)[:, None] * cotangent[owner].astype(jnp.float32)).astype(
        jnp.bfloat16
    )
    arrived = lax.all_to_all(outgoing, "expert", split_axis=0, concat_axis=0, tiled=True)
    rows = arrived.reshape(-1, width)
    gate_w = w_gate[0]
    up_w = w_up[0]
    down_w = w_down[0]
    gate = jnp.dot(rows, gate_w, preferred_element_type=jnp.float32)
    up = jnp.dot(rows, up_w, preferred_element_type=jnp.float32)
    sig = jax.nn.sigmoid(gate)
    act = gate * sig
    hidden = (act * up).astype(jnp.bfloat16)
    produced = contract_last(hidden, down_w).astype(jnp.bfloat16).reshape(arrived.shape)
    returned = lax.all_to_all(produced, "expert", split_axis=0, concat_axis=0, tiled=True)
    mixed = jnp.sum(collect(returned) * combine[:, :, None], axis=1).astype(jnp.bfloat16)
    grad_arrived = lax.all_to_all(
        fill_slots(weighted), "expert", split_axis=0, concat_axis=0, tiled=True
    )
    grad_rows = grad_arrived.reshape(-1, width)
    dhidden = jnp.dot(grad_rows, down_w, preferred_element_type=jnp.float32)
    dgate = (dhidden * up * sig * (1.0 + gate * (1.0 - sig))).astype(jnp.bfloat16)
    dup = (dhidden * act).astype(jnp.bfloat16)
    dinput = (contract_last(dgate, gate_w) + contract_last(dup, up_w)).astype(jnp.bfloat16)
    back = lax.all_to_all(
        dinput.reshape(arrived.shape), "expert", split_axis=0, concat_axis=0, tiled=True
    )
    grad_tokens = jnp.sum(collect(back), axis=1).astype(jnp.bfloat16)
    summed = lax.psum_scatter(
        jnp.concatenate(
            [
                contract_first(rows, dgate),
                contract_first(rows, dup),
                contract_first(grad_rows, hidden),
            ],
            axis=1,
        ).astype(jnp.bfloat16),
        "dp",
        scatter_dimension=0,
        tiled=True,
    ).astype(jnp.float32)
    hidden_units = gate_w.shape[1]
    grad_gate = summed[:, :hidden_units].astype(jnp.bfloat16)[None]
    grad_up = summed[:, hidden_units : 2 * hidden_units].astype(jnp.bfloat16)[None]
    grad_down = summed[:, 2 * hidden_units :].astype(jnp.bfloat16)[None]
    return (mixed, grad_tokens, grad_gate, grad_up, grad_down)


def solution(mesh):
    placed = (
        P(("groups", "expert", "dp"), None),
        P(("groups", "expert", "dp"), None),
        P(("groups", "expert", "dp"), None),
        P(("groups", "expert", "dp"), None),
        P("expert", None, None),
        P("expert", None, None),
        P("expert", None, None),
    )
    return jax.shard_map(
        per_device,
        mesh=mesh,
        in_specs=placed,
        out_specs=(
            P(("groups", "expert", "dp"), None),
            P(("groups", "expert", "dp"), None),
            P(("groups", "expert"), "dp", None),
            P(("groups", "expert"), "dp", None),
            P(("groups", "expert"), "dp", None),
        ),
        check_vma=False,
    )
```

profile of v0, /device:TPU:11, one launch (start us, length us, event | category | flops | bytes accessed | tf_op | source)
XLA Modules:
  0.0 253.0 jit_solution(2245146608314679615)
XLA Ops:
  2.6 4.5 %reduce-window.6 = s32[16,8,128]{2,1,0:T(8,128)S(1)} reduce-window(s32[16,8,128]{2,1,0:T(8,128)S(1)} %fusion.24, s32[]{:T(128)} %constant.28.clone.1), window={size=1x1x128 pad=0_0x0_0x127_0}, to_apply=%region_0.0 | reduce-window | flops 2080768 | bytes 131076 | tf_op jit(solution)/shard_map/reduce-window
  7.6 16.1 %scatter_custom_fusion = bf16[1024,1024]{1,0:T(8,128)(2,1)} fusion(s32[1024]{0:T(1024)S(1)} %bitcast.81, bf16[128,1024]{1,0:T(8,128)(2,1)} %param.7, s32[1024]{0:T(1024)S(1)} %broadcast_clamp_fusion.1, bf16[]{:T(256)} %constant.26.clone.1), kind=kCustom, calls=%fused_computation.12 | custom fusion | bytes 2097664 | tf_op jit(solution)/shard_map/scatter | solution.py:32
  23.8 6.7 %all-to-all-start = ((bf16[16,64,1024]{2,1,0:T(8,128)(2,1)}), bf16[16,64,1024]{2,1,0:T(8,128)(2,1)S(1)}, u32[]{:S(2)}, u32[]{:S(2)}) async-start(bf16[16,64,1024]{2,1,0:T(8,128)(2,1)} %bitcast.5), calls=%async_computation | async-start | bytes 4194304 | tf_op jit(solution)/shard_map/all_to_all | solution.py:42
  30.6 14.5 %scatter_custom_fusion.1 = bf16[1024,1024]{1,0:T(8,128)(2,1)} fusion(s32[1024]{0:T(1024)S(1)} %bitcast.82, f32[1024]{0:T(1024)S(1)} %mul.66, bf16[]{:T(256)} %constant.26.clone.1, bf16[128,1024]{1,0:T(8,128)(2,1)S(1)} %copy-done.8, s32[1024]{0:T(1024)S(1)} %broadcast_clamp_fusion.1), kind=kCustom, calls=%fused_computation.10 | custom fusion | flops 3145728 | bytes 2367490 | tf_op jit(solution)/shard_map/scatter | solution.py:32
  45.1 32.7 %all-to-all-done = bf16[16,64,1024]{2,1,0:T(8,128)(2,1)S(1)} async-done(((bf16[16,64,1024]{2,1,0:T(8,128)(2,1)}), bf16[16,64,1024]{2,1,0:T(8,128)(2,1)S(1)}, u32[]{:S(2)}, u32[]{:S(2)}) %all-to-all-start) | async-done | bytes 2097184 | tf_op jit(solution)/shard_map/all_to_all | solution.py:42
  77.9 4.9 %all-to-all-start.2 = ((bf16[16,64,1024]{2,1,0:T(8,128)(2,1)}), bf16[16,64,1024]{2,1,0:T(8,128)(2,1)}, u32[]{:S(2)}, u32[]{:S(2)}) async-start(bf16[16,64,1024]{2,1,0:T(8,128)(2,1)} %bitcast.13), calls=%async_computation.2 | async-start | bytes 4194304 | tf_op jit(solution)/shard_map/all_to_all | solution.py:55
  82.8 3.7 %fusion.15 = f32[1024,384]{1,0:T(8,128)} fusion(bf16[1024,1024]{1,0:T(8,128)(2,1)S(1)} %bitcast.73, bf16[1,1024,384]{2,1,0:T(8,128)(2,1)} %param.12), kind=kOutput, calls=%fused_computation.33 | convolution fusion | flops 805306368 | bytes 4456448 | tf_op jit(solution)/shard_map/dot_general | solution.py:48
  86.5 2.4 fusion.19
  88.9 41.4 %all-to-all-done.2 = bf16[16,64,1024]{2,1,0:T(8,128)(2,1)} async-done(((bf16[16,64,1024]{2,1,0:T(8,128)(2,1)}), bf16[16,64,1024]{2,1,0:T(8,128)(2,1)}, u32[]{:S(2)}, u32[]{:S(2)}) %all-to-all-start.2) | async-done | bytes 2097184 | tf_op jit(solution)/shard_map/all_to_all | solution.py:55
  130.3 5.5 %multiply_convert_fusion.2 = (bf16[1024,384]{1,0:T(8,128)(2,1)}, bf16[1024,384]{1,0:T(8,128)(2,1)}, bf16[1024,384]{1,0:T(8,128)(2,1)S(1)}) fusion(f32[1024,384]{1,0:T(8,128)} %fusion.19, f32[1024,384]{1,0:T(8,128)} %fusion.15, bf16[1024,1024]{1,0:T(8,128)(2,1)} %bitcast.14, bf16[1,1024,384]{2,1,0:T(8,128)(2,1)S(1)} %copy-done), kind=kOutput, calls=%fused_computation.16 | convolution fusion | flops 811204608 | bytes 8388608 | tf_op jit(solution)/shard_map/dot_general | solution.py:59
  136.7 2.6 %convolution_convert_fusion = bf16[1024,1024]{1,0:T(8,128)(2,1)} fusion(bf16[1024,384]{1,0:T(8,128)(2,1)S(1)} %get-tuple-element.7, bf16[1,1024,384]{2,1,0:T(8,128)(2,1)S(1)} %copy-done), kind=kOutput, calls=%fused_computation.15 | convolution fusion | flops 806354944 | bytes 3670016 | tf_op jit(solution)/shard_map/dot_general | solution.py:8
  139.3 4.9 %all-to-all-start.1 = ((bf16[16,64,1024]{2,1,0:T(8,128)(2,1)}), bf16[16,64,1024]{2,1,0:T(8,128)(2,1)S(1)}, u32[]{:S(2)}, u32[]{:S(2)}) async-start(bf16[16,64,1024]{2,1,0:T(8,128)(2,1)} %bitcast.77), calls=%async_computation.1 | async-start | bytes 4194304 | tf_op jit(solution)/shard_map/all_to_all | solution.py:53
  144.2 2.8 %fusion.17 = f32[1024,1024]{1,0:T(8,128)S(1)} fusion(bf16[1024,384]{1,0:T(8,128)(2,1)} %get-tuple-element.6, bf16[1,1024,384]{2,1,0:T(8,128)(2,1)} %param.11), kind=kOutput, calls=%fused_computation.35 | convolution fusion | flops 805306368 | bytes 5767168 | tf_op jit(solution)/shard_map/dot_general | solution.py:8
  147.0 2.6 %add_convert_fusion = bf16[1024,1024]{1,0:T(8,128)(2,1)} fusion(f32[1024,1024]{1,0:T(8,128)S(1)} %fusion.17, bf16[1024,384]{1,0:T(8,128)(2,1)S(1)} %copy-done.6, bf16[1,1024,384]{2,1,0:T(8,128)(2,1)S(1)} %copy-done.5), kind=kOutput, calls=%fused_computation.8 | convolution fusion | flops 807403520 | bytes 7864320 | tf_op jit(solution)/shard_map/dot_general | solution.py:8
  149.6 42.0 %all-to-all-done.1 = bf16[16,64,1024]{2,1,0:T(8,128)(2,1)S(1)} async-done(((bf16[16,64,1024]{2,1,0:T(8,128)(2,1)}), bf16[16,64,1024]{2,1,0:T(8,128)(2,1)S(1)}, u32[]{:S(2)}, u32[]{:S(2)}) %all-to-all-start.1) | async-done | bytes 2097184 | tf_op jit(solution)/shard_map/all_to_all | solution.py:53
  191.6 4.9 %all-to-all-start.3 = ((bf16[16,64,1024]{2,1,0:T(8,128)(2,1)}), bf16[16,64,1024]{2,1,0:T(8,128)(2,1)}, u32[]{:S(2)}, u32[]{:S(2)}) async-start(bf16[16,64,1024]{2,1,0:T(8,128)(2,1)} %bitcast.72), calls=%async_computation.3 | async-start | bytes 4194304 | tf_op jit(solution)/shard_map/all_to_all | solution.py:63
  196.6 4.1 %fusion.8 = bf16[1,1024,384]{2,1,0:T(8,128)(2,1)} fusion(bf16[1024,1024]{1,0:T(8,128)(2,1)} %bitcast.14, bf16[1024,384]{1,0:T(8,128)(2,1)} %copy-done.10), kind=kOutput, calls=%fused_computation.26 | convolution fusion | flops 805699584 | bytes 3670016 | tf_op jit(solution)/shard_map/dot_general | solution.py:14
  200.7 2.2 fusion.7
  202.8 2.2 fusion.6
  205.0 5.3 %gather_fusion = bf16[1024,1024]{1,0:T(8,128)(2,1)} fusion(bf16[1024,1024]{1,0:T(8,128)(2,1)S(1)} %bitcast.71, s32[1024]{0:T(1024)S(1)} %broadcast_clamp_fusion), kind=kCustom, calls=%fused_computation.1 | custom fusion | bytes 4198400 | tf_op jit(solution)/shard_map/gather | solution.py:35
  210.3 3.7 %fusion = bf16[128,1024]{1,0:T(8,128)(2,1)} fusion(bf16[1024,1024]{1,0:T(8,128)(2,1)} %gather_fusion, f32[128,8]{1,0:T(8,128)S(1)} %copy.20), kind=kLoop, calls=%fused_computation.7 | loop fusion | flops 3014656 | bytes 2363392 | tf_op jit(solution)/shard_map/reduce_sum | solution.py:54
  214.0 30.1 %all-to-all-done.3 = bf16[16,64,1024]{2,1,0:T(8,128)(2,1)} async-done(((bf16[16,64,1024]{2,1,0:T(8,128)(2,1)}), bf16[16,64,1024]{2,1,0:T(8,128)(2,1)}, u32[]{:S(2)}, u32[]{:S(2)}) %all-to-all-start.3) | async-done | bytes 2097184 | tf_op jit(solution)/shard_map/all_to_all | solution.py:63
  244.1 6.8 %gather_fusion.1 = bf16[1024,1024]{1,0:T(8,128)(2,1)S(1)} fusion(bf16[1024,1024]{1,0:T(8,128)(2,1)} %bitcast.16, s32[1024]{0:T(1024)S(1)} %broadcast_clamp_fusion), kind=kCustom, calls=%fused_computation.3 | custom fusion | bytes 4198400 | tf_op jit(solution)/shard_map/gather | solution.py:35
  250.9 2.1 bitcast_reduce_fusion
  (42 shorter events, 3.6 us)
Async XLA Ops:
  0.6 129.7 %copy-start = (bf16[1,1024,384]{2,1,0:T(8,128)(2,1)S(1)}, bf16[1,1024,384]{2,1,0:T(8,128)(2,1)}, u32[]{:S(2)}) copy-start(bf16[1,1024,384]{2,1,0:T(8,128)(2,1)} %param.13) | copy-start | bytes 2359300
  23.7 6.7 %copy-start.9 = (f32[128,8]{0,1:T(8,128)S(1)}, f32[128,8]{0,1:T(8,128)}, u32[]{:S(2)}) copy-start(f32[128,8]{0,1:T(8,128)} %param.10) | copy-start | bytes 12292
  23.8 6.9 %copy-start.8 = (bf16[128,1024]{1,0:T(8,128)(2,1)S(1)}, bf16[128,1024]{1,0:T(8,128)(2,1)}, u32[]{:S(2)}) copy-start(bf16[128,1024]{1,0:T(8,128)(2,1)} %param.8) | copy-start | bytes 786436
  23.8 54.1 %all-to-all-start = ((bf16[16,64,1024]{2,1,0:T(8,128)(2,1)}), bf16[16,64,1024]{2,1,0:T(8,128)(2,1)S(1)}, u32[]{:S(2)}, u32[]{:S(2)}) async-start(bf16[16,64,1024]{2,1,0:T(8,128)(2,1)} %bitcast.5), calls=%async_computation | async-start | bytes 4194304 | tf_op jit(solution)/shard_map/all_to_all | solution.py:42
  77.9 8.6 %copy-start.2 = (bf16[16,64,1024]{2,1,0:T(8,128)(2,1)}, bf16[16,64,1024]{2,1,0:T(8,128)(2,1)S(1)}, u32[]{:S(2)}) copy-start(bf16[16,64,1024]{2,1,0:T(8,128)(2,1)S(1)} %all-to-all-done) | copy-start | bytes 6291460
  77.9 52.4 %all-to-all-start.2 = ((bf16[16,64,1024]{2,1,0:T(8,128)(2,1)}), bf16[16,64,1024]{2,1,0:T(8,128)(2,1)}, u32[]{:S(2)}, u32[]{:S(2)}) async-start(bf16[16,64,1024]{2,1,0:T(8,128)(2,1)} %bitcast.13), calls=%async_computation.2 | async-start | bytes 4194304 | tf_op jit(solution)/shard_map/all_to_all | solution.py:55
  82.8 3.7 %copy-start.4 = (bf16[1,1024,384]{2,1,0:T(8,128)(2,1)S(1)}, bf16[1,1024,384]{2,1,0:T(8,128)(2,1)}, u32[]{:S(2)}) copy-start(bf16[1,1024,384]{2,1,0:T(8,128)(2,1)} %param.11) | copy-start | bytes 2359300
  135.8 0.9 copy-start.10
  139.3 52.3 %all-to-all-start.1 = ((bf16[16,64,1024]{2,1,0:T(8,128)(2,1)}), bf16[16,64,1024]{2,1,0:T(8,128)(2,1)S(1)}, u32[]{:S(2)}, u32[]{:S(2)}) async-start(bf16[16,64,1024]{2,1,0:T(8,128)(2,1)} %bitcast.77), calls=%async_computation.1 | async-start | bytes 4194304 | tf_op jit(solution)/shard_map/all_to_all | solution.py:53
  144.2 2.8 %copy-start.5 = (bf16[1,1024,384]{2,1,0:T(8,128)(2,1)S(1)}, bf16[1,1024,384]{2,1,0:T(8,128)(2,1)}, u32[]{:S(2)}) copy-start(bf16[1,1024,384]{2,1,0:T(8,128)(2,1)} %param.12) | copy-start | bytes 2359300
  144.2 2.8 %copy-start.6 = (bf16[1024,384]{1,0:T(8,128)(2,1)S(1)}, bf16[1024,384]{1,0:T(8,128)(2,1)}, u32[]{:S(2)}) copy-start(bf16[1024,384]{1,0:T(8,128)(2,1)} %get-tuple-element.5) | copy-start | bytes 2359300
  191.6 52.4 %all-to-all-start.3 = ((bf16[16,64,1024]{2,1,0:T(8,128)(2,1)}), bf16[16,64,1024]{2,1,0:T(8,128)(2,1)}, u32[]{:S(2)}, u32[]{:S(2)}) async-start(bf16[16,64,1024]{2,1,0:T(8,128)(2,1)} %bitcast.72), calls=%async_computation.3 | async-start | bytes 4194304 | tf_op jit(solution)/shard_map/all_to_all | solution.py:63
  196.6 4.1 %copy-start.3 = (bf16[16,64,1024]{2,1,0:T(8,128)(2,1)S(1)}, bf16[16,64,1024]{2,1,0:T(8,128)(2,1)}, u32[]{:S(2)}) copy-start(bf16[16,64,1024]{2,1,0:T(8,128)(2,1)} %copy-done.2) | copy-start | bytes 6291460
  196.6 4.1 %copy-start.7 = (bf16[1024,384]{1,0:T(8,128)(2,1)S(1)}, bf16[1024,384]{1,0:T(8,128)(2,1)}, u32[]{:S(2)}) copy-start(bf16[1024,384]{1,0:T(8,128)(2,1)} %get-tuple-element.5) | copy-start | bytes 2359300
  200.7 2.2 copy-start.1
where the time goes:
time: 254 us; the launch traced here: 253 us
  waiting for transfers between devices  146 us (57%)
  local copies, waits for them, and re-layouts  30.9 us (12%)
  matrix products  27.9 us (11%)
  other arithmetic  25.7 us (10%)
  starting transfers between devices  21.4 us (8%)
    all_to_all x1, waiting for transfers between devices, per_device(): lax.all_to_all(produced, 'expert', split_axis=0, concat_axis=0, tiled=True)  42 us
    all_to_all x1, waiting for transfers between devices, per_device(): lax.all_to_all(fill_slots(weighted), 'expert', split_axis=0, concat_axis=...  41.4 us
    all_to_all x1, waiting for transfers between devices, per_device(): lax.all_to_all(outgoing, 'expert', split_axis=0, concat_axis=0, tiled=True)  32.7 us
    all_to_all x1, waiting for transfers between devices, per_device(): lax.all_to_all(dinput.reshape(arrived.shape), 'expert', split_axis=0, con...  30.1 us
    scatter x1, local copies, waits for them, and re-layouts, fill_slots(): return empty.at[place].set(values).reshape(experts, capacity, width)  16.1 us
    scatter x1, other arithmetic, fill_slots(): return empty.at[place].set(values).reshape(experts, capacity, width)  14.5 us
    gather x2, local copies, waits for them, and re-layouts, collect(): picked = returned.reshape(-1, width)[place].astype(jnp.float32)  12.2 us
    dot_general x3, matrix products, contract_first(): lax.dot_general(left, right, (((0,), (0,)), ((), ())), preferred_element_...  8.41 us
  transfers between devices with their start and end apart: 4, of which 4 were waited for; matrix products, arithmetic and copies ran while one was open for 17% of the time, Pallas kernels for 0%

commit v1 on v0

--- a/solution.py
+++ b/solution.py
@@ -1,7 +1,14 @@
+import functools
+
 import jax
 import jax.numpy as jnp
 from jax import lax
+from jax.experimental import pallas as pl
+from jax.experimental.pallas import tpu as pltpu
 from jax.sharding import PartitionSpec as P
+
+F32 = jnp.float32
+BF16 = jnp.bfloat16
 
 
 def contract_last(left, right):
@@ -16,7 +23,7 @@
     )
 
 
-def per_device(tokens, cotangent, routes, combine, w_gate, w_up, w_down):
+def by_all_to_all(tokens, cotangent, routes, combine, w_gate, w_up, w_down):
     tok_dev, width = tokens.shape
     top_count = routes.shape[1]
     experts = w_gate.shape[0] * lax.axis_size("expert")
@@ -84,6 +91,314 @@
     return (mixed, grad_tokens, grad_gate, grad_up, grad_down)
 
 
+VMEM = pltpu.VMEM
+LIMIT = 20 * 1024 * 1024
+
+
+def call(body, outs, operands, flops, smem=0, scratch=(), nbytes=None):
+    specs = [pl.BlockSpec(memory_space=pltpu.SMEM)] * smem
+    specs += [pl.BlockSpec(memory_space=VMEM)] * (len(operands) - smem)
+    if nbytes is None:
+        nbytes = sum(a.size * a.dtype.itemsize for a in operands)
+        nbytes += sum(a.size * a.dtype.itemsize for a in outs)
+    return pl.pallas_call(
+        body,
+        out_shape=list(outs),
+        in_specs=specs,
+        out_specs=[pl.BlockSpec(memory_space=VMEM)] * len(outs),
+        scratch_shapes=list(scratch),
+        compiler_params=pltpu.CompilerParams(vmem_limit_bytes=LIMIT),
+        cost_estimate=pl.CostEstimate(flops=flops, bytes_accessed=nbytes, transcendentals=0),
+    )(*operands)
+
+
+def picks(place, cap):
+    slots = lax.broadcasted_iota(jnp.int32, (cap, place.shape[1]), 0).astype(F32)
+    return jnp.where(slots == place, 1.0, 0.0)
+
+
+def joined(parts):
+    return parts[0] if len(parts) == 1 else jnp.concatenate(parts, axis=0)
+
+
+def forward_body(dirs, halves, cap, top, expert_ref, *refs):
+    metas = refs[:dirs]
+    refs = refs[dirs:]
+    count = dirs * halves
+    own = refs[:count]
+    other = refs[count : 2 * count]
+    w_gate, w_up, w_down = refs[2 * count : 2 * count + 3]
+    info_ref, rows_ref, slope_ref, act_ref, hidden_ref, keep_ref, give_ref = refs[2 * count + 3 :]
+    me = expert_ref[0].astype(F32)
+    mate = expert_ref[1].astype(F32)
+    tok = metas[0].shape[1]
+    masks, weights = [], []
+    for expert, side in ((me, 0), (me, 1), (mate, 0)):
+        for d in range(dirs):
+            base = side * 2 * top
+            hit = metas[d][base : base + top] == expert
+            masks.append(jnp.sum(jnp.where(hit, 1.0, 0.0), axis=0, keepdims=True))
+            share = jnp.where(hit, metas[d][base + top : base + 2 * top], 0.0)
+            weights.append(jnp.sum(share, axis=0, keepdims=True))
+    pad = jnp.zeros((8 - len(masks), tok), F32)
+    mask = jnp.concatenate(masks + [pad], axis=0)
+    before = lax.broadcasted_iota(jnp.int32, (tok, tok), 0) < lax.broadcasted_iota(
+        jnp.int32, (tok, tok), 1
+    )
+    rank = jnp.dot(
+        mask.astype(BF16), jnp.where(before, 1.0, 0.0).astype(BF16), preferred_element_type=F32
+    )
+    place = jnp.where(mask > 0.5, rank, -1.0)
+    info_ref[0:8] = place
+    info_ref[8:16] = jnp.concatenate(weights + [pad], axis=0)
+    share = []
+    for side, blocks in enumerate((own, other)):
+        for d in range(dirs):
+            i = side * dirs + d
+            pick = picks(place[i : i + 1], cap)
+            share.append(jnp.sum(pick * weights[i], axis=1, keepdims=True))
+            block = joined([b[...] for b in blocks[d * halves : (d + 1) * halves]])
+            taken = jnp.dot(pick.astype(BF16), block, preferred_element_type=F32)
+            rows_ref[i * cap : (i + 1) * cap] = taken.astype(BF16)
+    rows = rows_ref[...]
+    gate = jnp.dot(rows, w_gate[...], preferred_element_type=F32)
+    up = jnp.dot(rows, w_up[...], preferred_element_type=F32)
+    sig = jax.nn.sigmoid(gate)
+    act = gate * sig
+    hidden = (act * up).astype(BF16)
+    hidden_ref[...] = hidden
+    act_ref[...] = act
+    slope_ref[...] = up * sig * (1.0 + gate * (1.0 - sig))
+    produced = contract_last(hidden, w_down[...]).astype(BF16).astype(F32)
+    sent = (jnp.concatenate(share, axis=0) * produced).astype(BF16)
+    keep_ref[...] = sent[: dirs * cap]
+    give_ref[...] = sent[dirs * cap :]
+
+
+def backward_body(dirs, halves, cap, *refs):
+    count = dirs * halves
+    info_ref, slope, act = refs[:3]
+    own = refs[3 : 3 + count]
+    other = refs[3 + count : 3 + 2 * count]
+    w_gate, w_up, w_down = refs[3 + 2 * count : 6 + 2 * count]
+    rows_ref, dgate_ref, dup_ref, keep_ref, give_ref = refs[6 + 2 * count :]
+    for side, blocks in enumerate((own, other)):
+        for d in range(dirs):
+            i = side * dirs + d
+            pick = picks(info_ref[i : i + 1], cap)
+            share = jnp.sum(pick * info_ref[8 + i : 9 + i], axis=1, keepdims=True)
+            block = joined([b[...] for b in blocks[d * halves : (d + 1) * halves]])
+            taken = jnp.dot(pick.astype(BF16), block, preferred_element_type=F32)
+            rows_ref[i * cap : (i + 1) * cap] = (share * taken).astype(BF16)
+    dhidden = jnp.dot(rows_ref[...], w_down[...], preferred_element_type=F32)
+    dgate = (dhidden * slope[...]).astype(BF16)
+    dup = (dhidden * act[...]).astype(BF16)
+    dgate_ref[...] = dgate
+    dup_ref[...] = dup
+    back = (contract_last(dgate, w_gate[...]) + contract_last(dup, w_up[...])).astype(BF16)
+    keep_ref[...] = back[: dirs * cap]
+    give_ref[...] = back[dirs * cap :]
+
+
+def return_body(dirs, cap, arrived, info_ref, keep, give, *refs):
+    ins = refs[: len(arrived)]
+    outs = refs[len(arrived) :]
+    sums = []
+    for d in range(dirs):
+        both = jnp.concatenate(
+            [picks(info_ref[d : d + 1], cap), picks(info_ref[2 * dirs + d : 2 * dirs + d + 1], cap)],
+            axis=0,
+        ).astype(BF16)
+        part = slice(d * cap, (d + 1) * cap)
+        values = jnp.concatenate([keep[part], give[part]], axis=0)
+        sums.append(contract_first(both, values))
+    if dirs == 1 and len(outs) == 2:
+        half = sums[0].shape[0] // 2
+        outs[0][...] = sums[0][:half].astype(BF16)
+        outs[1][...] = sums[0][half:].astype(BF16)
+        return
+    for d in range(dirs):
+        total = sums[d]
+        for ref, (which, low, high) in zip(ins, arrived):
+            if which != d:
+                continue
+            value = ref[...].astype(F32)
+            tok = total.shape[0]
+            if high - low == tok:
+                total = total + value
+            else:
+                pieces = []
+                if low:
+                    pieces.append(total[:low])
+                pieces.append(total[low:high] + value)
+                if high < tok:
+                    pieces.append(total[high:])
+                total = jnp.concatenate(pieces, axis=0)
+        outs[d][...] = total.astype(BF16)
+
+
+def weights_body(steps, cols, *refs):
+    rows = refs[:steps]
+    grads = refs[steps : 2 * steps]
+    out = refs[2 * steps]
+    right = jnp.concatenate([g[...] for g in grads], axis=0)
+    for low in range(0, out.shape[0], cols):
+        left = jnp.concatenate([r[:, low : low + cols] for r in rows], axis=0)
+        out[low : low + cols] = contract_first(left, right).astype(BF16)
+
+
+def by_ring(tokens, cotangent, routes, combine, w_gate, w_up, w_down):
+    tok, width = tokens.shape
+    top = routes.shape[1]
+    n = lax.axis_size("expert")
+    cap = (tok * top + n - 1) // n
+    units = w_gate.shape[2]
+    gate_w, up_w, down_w = w_gate[0], w_up[0], w_down[0]
+    pairs = n // 2
+    reach = pairs // 2
+    half = tok // 2
+    walk = [2 * i for i in range(reach)] + [2 * i + 1 for i in reversed(range(reach))]
+
+    def hop(value, by):
+        moves = [
+            (2 * walk[i] + core, 2 * walk[(i + by) % pairs] + core)
+            for i in range(pairs)
+            for core in range(2)
+        ]
+        return lax.ppermute(value, "expert", moves)
+
+    def swap(value):
+        return lax.ppermute(value, "expert", [(i, i ^ 1) for i in range(n)])
+
+    def spread(block, split):
+        found = [[block]]
+        back = front = block
+        for step in range(1, reach + 1):
+            if step == reach and split:
+                back, front = hop(back[:half], 1), hop(front[half:], -1)
+            elif step == reach:
+                found.append([hop(back, 1)])
+                break
+            else:
+                back, front = hop(back, 1), hop(front, -1)
+            found.append([back, front])
+        return found
+
+    here = lax.axis_index("expert").astype(jnp.int32)
+    expert = jnp.stack([here, here ^ 1])
+    meta = jnp.concatenate([routes.T.astype(F32), combine.T], axis=0)
+    metas = spread(jnp.concatenate([meta, swap(meta)], axis=0), False)
+    token_blocks = spread(tokens, True)
+    token_other = [[swap(b) for b in found] for found in token_blocks]
+    cot_blocks = spread(cotangent, True)
+    cot_other = [[swap(b) for b in found] for found in cot_blocks]
+
+    def struct(shape, dtype):
+        return jax.ShapeDtypeStruct(shape, dtype)
+
+    forward, backward = [], []
+    for step in range(reach + 1):
+        dirs = 2 if 0 < step < reach else 1
+        halves = 2 if step == reach else 1
+        m = 2 * dirs * cap
+        forward.append(
+            call(
+                functools.partial(forward_body, dirs, halves, cap, top),
+                [
+                    struct((16, tok), F32),
+                    struct((m, width), BF16),
+                    struct((m, units), F32),
+                    struct((m, units), F32),
+                    struct((m, units), BF16),
+                    struct((m // 2, width), BF16),
+                    struct((m // 2, width), BF16),
+                ],
+                [expert, *metas[step], *token_blocks[step], *token_other[step], gate_w, up_w, down_w],
+                2 * m * width * (3 * units + tok),
+                smem=1,
+            )
+        )
+    for step in range(reach + 1):
+        dirs = 2 if 0 < step < reach else 1
+        halves = 2 if step == reach else 1
+        m = 2 * dirs * cap
+        info, _, slope, act = forward[step][:4]
+        backward.append(
+            call(
+                functools.partial(backward_body, dirs, halves, cap),
+                [
+                    struct((m, width), BF16),
+                    struct((m, units), BF16),
+                    struct((m, units), BF16),
+                    struct((m // 2, width), BF16),
+                    struct((m // 2, width), BF16),
+                ],
+                [info, slope, act, *cot_blocks[step], *cot_other[step], gate_w, up_w, down_w],
+                2 * m * width * (3 * units + tok),
+            )
+        )
+
+    def gather_sums(kept, given):
+        given = [swap(g) for g in given]
+        flops = 4 * cap * tok * width
+
+        def stage(step, arrived, values, outs):
+            dirs = 2 if 0 < step < reach else 1
+            return call(
+                functools.partial(return_body, dirs, cap, arrived),
+                [struct((rows, width), BF16) for rows in outs],
+                [forward[step][0], kept[step], given[step], *values],
+                dirs * flops,
+            )
+
+        ahead, behind = stage(reach, (), (), (half, half))
+        ahead, behind = hop(ahead, 1), hop(behind, -1)
+        for step in range(reach - 1, 0, -1):
+            first = step == reach - 1
+            arrived = (
+                (0, half if first else 0, tok),
+                (1, 0, half if first else tok),
+            )
+            behind, ahead = stage(step, arrived, (behind, ahead), (tok, tok))
+            ahead, behind = hop(ahead, 1), hop(behind, -1)
+        alone = reach == 1
+        arrived = ((0, 0, half if alone else tok), (0, half if alone else 0, tok))
+        return stage(0, arrived, (ahead, behind), (tok,))[0]
+
+    mixed = gather_sums([f[5] for f in forward], [f[6] for f in forward])
+    grad_tokens = gather_sums([b[3] for b in backward], [b[4] for b in backward])
+
+    def weight_grad(lefts, rights):
+        return call(
+            functools.partial(weights_body, len(lefts), 256),
+            [struct((width, units), BF16)],
+            [*lefts, *rights],
+            2 * n * cap * width * units,
+        )[0][None]
+
+    grad_gate = weight_grad([f[1] for f in forward], [b[1] for b in backward])
+    grad_up = weight_grad([f[1] for f in forward], [b[2] for b in backward])
+    grad_down = weight_grad([b[0] for b in backward], [f[4] for f in forward])
+    return (mixed, grad_tokens, grad_gate, grad_up, grad_down)
+
+
+def per_device(tokens, cotangent, routes, combine, w_gate, w_up, w_down):
+    n = lax.axis_size("expert")
+    tok, width = tokens.shape
+    top = routes.shape[1]
+    ring = (
+        lax.axis_size("dp") == 1
+        and w_gate.shape[0] == 1
+        and n % 4 == 0
+        and n <= 2 * top
+        and tok % 128 == 0
+        and top % 8 == 0
+        and (tok * top) % (16 * n) == 0
+    )
+    plan = by_ring if ring else by_all_to_all
+    return plan(tokens, cotangent, routes, combine, w_gate, w_up, w_down)
+
+
 def solution(mesh):
     placed = (
         P(("groups", "expert", "dp"), None),

time: 254 us -> 129 us (0.51)
  the two profiles are of different devices: /device:TPU:11 before, /device:TPU:0 now
where the time goes in v1:
time: 129 us; the launch traced here: 128 us
  starting transfers between devices  49.9 us (39%)
  waiting for transfers between devices  36.3 us (28%)
  Pallas kernels  27.8 us (22%)
  local copies, waits for them, and re-layouts  12.2 us (9%)
    ppermute x39, starting transfers between devices, hop(): return lax.ppermute(value, 'expert', moves)  45.9 us
    ppermute x39, waiting for transfers between devices, hop(): return lax.ppermute(value, 'expert', moves)  36.3 us
    pallas_call x23, Pallas kernels, call(): pl.pallas_call(body, out_shape=list(outs), in_specs=specs, out_specs=[pl....  27.8 us
    unnamed x80, local copies, waits for them, and re-layouts  12.2 us
    ppermute x29, starting transfers between devices, swap(): return lax.ppermute(value, 'expert', [(i, i ^ 1) for i in range(n)])  3.95 us
  transfers between devices with their start and end apart: 68, of which 23 were waited for; matrix products, arithmetic and copies ran while one was open for 1% of the time, Pallas kernels for 21%

profile of v1, /device:TPU:0, one launch (start us, length us, event | category | flops | bytes accessed | tf_op | source)
XLA Modules:
  0.0 128.2 jit_solution(17830759576814053839)
XLA Ops:
  0.7 3.1 %collective-permute-start.5 = (bf16[128,1024]{1,0:T(8,128)(2,1)}, bf16[128,1024]{1,0:T(8,128)(2,1)S(1)}, u32[]{:S(2)}, u32[]{:S(2)}) collective-permute-start(bf16[128,1024]{1,0:T(8,128)(2,1)} %refs_1_.1), channel_id=1, source_target_pairs={{0,4},{1,5},{4,8},{5,9},{8,12},{9,13},{12,14},{13,15},{14,10},{15,... | collective-permute-start | bytes 786440 | tf_op jit(solution)/shard_map/ppermute | solution.py:268
  4.5 2.0 %collective-permute-start.40 = (bf16[128,1024]{1,0:T(8,128)(2,1)}, bf16[128,1024]{1,0:T(8,128)(2,1)S(1)}, u32[]{:S(2)}, u32[]{:S(2)}) collective-permute-start(bf16[128,1024]{1,0:T(8,128)(2,1)} %refs_3_.1), channel_id=1, source_target_pairs={{0,4},{1,5},{4,8},{5,9},{8,12},{9,13},{12,14},{13,15},{14,10},{15,... | collective-permute-start | bytes 786440 | tf_op jit(solution)/shard_map/ppermute | solution.py:268
  8.5 7.6 %collective-permute-done.3.refs_0_ = f32[32,128]{1,0:T(8,128)S(1)} collective-permute-done((f32[32,128]{1,0:T(8,128)S(1)}, f32[32,128]{1,0:T(8,128)S(1)}, u32[]{:S(2)}, u32[]{:S(2)}) %collective-permute-start.3) | collective-permute-done | bytes 16416 | tf_op jit(solution)/shard_map/ppermute | solution.py:268
  16.1 1.8 %collective-permute-start.10 = (f32[32,128]{1,0:T(8,128)S(1)}, f32[32,128]{1,0:T(8,128)S(1)}, u32[]{:S(2)}, u32[]{:S(2)}) collective-permute-start(f32[32,128]{1,0:T(8,128)S(1)} %collective-permute-done.3.refs_0_), channel_id=1, source_target_pairs={{0,4},{1,5},{4,8},{5,9},{8,12},{9,13},{12,14},{13,15},{14,10},{15,... | collective-permute-start | bytes 49160 | tf_op jit(solution)/shard_map/ppermute | solution.py:268
  19.9 1.8 %collective-permute-start.17 = (f32[32,128]{1,0:T(8,128)S(1)}, f32[32,128]{1,0:T(8,128)S(1)}, u32[]{:S(2)}, u32[]{:S(2)}) collective-permute-start(f32[32,128]{1,0:T(8,128)S(1)} %collective-permute-done.10.refs_0_), channel_id=1, source_target_pairs={{0,4},{1,5},{4,8},{5,9},{8,12},{9,13},{12,14},{13,15},{14,10},{15,... | collective-permute-start | bytes 49160 | tf_op jit(solution)/shard_map/ppermute | solution.py:268
  30.1 1.7 %collective-permute-start.45 = (bf16[128,1024]{1,0:T(8,128)(2,1)S(1)}, bf16[128,1024]{1,0:T(8,128)(2,1)S(1)}, u32[]{:S(2)}, u32[]{:S(2)}) collective-permute-start(bf16[128,1024]{1,0:T(8,128)(2,1)S(1)} %collective-permute-done.40.refs_3_), channel_id=1, source_target_pairs={{0,4},{1,5},{4,8},{5,9},{8,12},{9,13},{12,14},{13,15},{14,10},{15,... | collective-permute-start | bytes 786440 | tf_op jit(solution)/shard_map/ppermute | solution.py:268
  31.8 2.5 %collective-permute-done.41.refs_4_ = bf16[128,1024]{1,0:T(8,128)(2,1)S(1)} collective-permute-done((bf16[128,1024]{1,0:T(8,128)(2,1)}, bf16[128,1024]{1,0:T(8,128)(2,1)S(1)}, u32[]{:S(2)}, u32[]{:S(2)}) %collective-permute-start.41) | collective-permute-done | bytes 262176 | tf_op jit(solution)/shard_map/ppermute | solution.py:268
  34.6 2.6 %collective-permute-done.12.refs_2_ = bf16[128,1024]{1,0:T(8,128)(2,1)S(1)} collective-permute-done((bf16[128,1024]{1,0:T(8,128)(2,1)S(1)}, bf16[128,1024]{1,0:T(8,128)(2,1)S(1)}, u32[]{:S(2)}, u32[]{:S(2)}) %collective-permute-start.12) | collective-permute-done | bytes 262176 | tf_op jit(solution)/shard_map/ppermute | solution.py:268
  40.2 2.6 %collective-permute-done.45.refs_3_ = bf16[128,1024]{1,0:T(8,128)(2,1)S(1)} collective-permute-done((bf16[128,1024]{1,0:T(8,128)(2,1)S(1)}, bf16[128,1024]{1,0:T(8,128)(2,1)S(1)}, u32[]{:S(2)}, u32[]{:S(2)}) %collective-permute-start.45) | collective-permute-done | bytes 262176 | tf_op jit(solution)/shard_map/ppermute | solution.py:268
  46.5 2.0 %collective-permute-done.19.refs_2_ = bf16[128,1024]{1,0:T(8,128)(2,1)S(1)} collective-permute-done((bf16[128,1024]{1,0:T(8,128)(2,1)S(1)}, bf16[128,1024]{1,0:T(8,128)(2,1)S(1)}, u32[]{:S(2)}, u32[]{:S(2)}) %collective-permute-start.19) | collective-permute-done | bytes 262176 | tf_op jit(solution)/shard_map/ppermute | solution.py:268
  53.9 1.8 %collective-permute-start.25 = (bf16[64,1024]{1,0:T(8,128)(2,1)S(1)}, bf16[64,1024]{1,0:T(8,128)(2,1)}, u32[]{:S(2)}, u32[]{:S(2)}) collective-permute-start(bf16[64,1024]{1,0:T(8,128)(2,1)S(1)} %slice.16), channel_id=1, source_target_pairs={{0,4},{1,5},{4,8},{5,9},{8,12},{9,13},{12,14},{13,15},{14,10},{15,... | collective-permute-start | bytes 393224 | tf_op jit(solution)/shard_map/ppermute | solution.py:268
  68.5 2.2 %shard_map.114 = (f32[16,128]{1,0:T(8,128)S(1)}, bf16[128,1024]{1,0:T(8,128)(2,1)S(1)}, f32[128,384]{1,0:T(8,128)S(1)}, f32[128,384]{1,0:T(8,128)S(1)}, bf16[128...) custom-call(s32[2]{0:T(128)S(1)} %pad_add_fusion.expert_ref, ...), custom_call_target="tpu_custom_call" | custom-call | flops 335544320 | bytes 3923976 | tf_op jit(solution)/shard_map/pallas_call | solution.py:104
  71.3 1.9 %shard_map.124 = (bf16[128,1024]{1,0:T(8,128)(2,1)S(1)}, bf16[128,384]{1,0:T(8,128)(2,1)S(1)}, bf16[128,384]{1,0:T(8,128)(2,1)S(1)}, bf16[64,1024]{1,0:T(8,128)(2,1)S(1)}, bf16[64,1024]{1,0:T(8,128)(2,1)S(1)}) custom-call(f32[16,128]{1,0:T(8,128)S(1)} %get-tuple-element.93.info_ref.refs_0_, f32[128,384]{1,0:T(8,128)S(1)} %get-tuple-element.120.refs_1_, ...), custom_call_target="tpu_custom_call" | custom-call | flops 335544320 | bytes 4005888 | tf_op jit(solution)/shard_map/pallas_call | solution.py:104
  73.7 2.5 %shard_map.113 = (f32[16,128]{1,0:T(8,128)S(1)}, bf16[256,1024]{1,0:T(8,128)(2,1)S(1)}, f32[256,384]{1,0:T(8,128)S(1)}, f32[256,384]{1,0:T(8,128)S(1)}, bf16[256...) custom-call(s32[2]{0:T(128)S(1)} %pad_add_fusion.expert_ref, ...), custom_call_target="tpu_custom_call" | custom-call | flops 671088640 | bytes 5480456 | tf_op jit(solution)/shard_map/pallas_call | solution.py:104
  84.2 2.0 %shard_map.112 = (f32[16,128]{1,0:T(8,128)S(1)}, bf16[256,1024]{1,0:T(8,128)(2,1)S(1)}, f32[256,384]{1,0:T(8,128)S(1)}, f32[256,384]{1,0:T(8,128)S(1)}, bf16[256...) custom-call(s32[2]{0:T(128)S(1)} %pad_add_fusion.expert_ref, ...), custom_call_target="tpu_custom_call" | custom-call | flops 671088640 | bytes 5480456 | tf_op jit(solution)/shard_map/pallas_call | solution.py:104
  93.0 2.0 %shard_map.111 = (f32[16,128]{1,0:T(8,128)S(1)}, bf16[256,1024]{1,0:T(8,128)(2,1)S(1)}, f32[256,384]{1,0:T(8,128)S(1)}, f32[256,384]{1,0:T(8,128)S(1)}, bf16[256...) custom-call(s32[2]{0:T(128)S(1)} %pad_add_fusion.expert_ref, ...), custom_call_target="tpu_custom_call" | custom-call | flops 671088640 | bytes 5480456 | tf_op jit(solution)/shard_map/pallas_call | solution.py:104
  101.0 2.3 %collective-permute-start.35 = (bf16[128,1024]{1,0:T(8,128)(2,1)S(1)}, bf16[128,1024]{1,0:T(8,128)(2,1)S(1)}, u32[]{:S(2)}, u32[]{:S(2)}) collective-permute-start(bf16[128,1024]{1,0:T(8,128)(2,1)S(1)} %get-tuple-element.101), channel_id=1, source_target_pairs={{0,4},{1,5},{4,8},{5,9},{8,12},{9,13},{12,14},{13,15},{14,10},{15,... | collective-permute-start | bytes 786440 | tf_op jit(solution)/shard_map/ppermute | solution.py:268
  105.1 2.0 %collective-permute-start.65 = (bf16[128,1024]{1,0:T(8,128)(2,1)S(1)}, bf16[128,1024]{1,0:T(8,128)(2,1)S(1)}, u32[]{:S(2)}, u32[]{:S(2)}) collective-permute-start(bf16[128,1024]{1,0:T(8,128)(2,1)S(1)} %get-tuple-element.129), channel_id=1, source_target_pairs={{0,4},{1,5},{4,8},{5,9},{8,12},{9,13},{12,14},{13,15},{14,10},{15,... | collective-permute-start | bytes 786440 | tf_op jit(solution)/shard_map/ppermute | solution.py:268
  111.0 2.7 %collective-permute-done.64.refs_0_ = bf16[128,1024]{1,0:T(8,128)(2,1)S(1)} collective-permute-done((bf16[128,1024]{1,0:T(8,128)(2,1)S(1)}, bf16[128,1024]{1,0:T(8,128)(2,1)S(1)}, u32[]{:S(2)}, u32[]{:S(2)}) %collective-permute-start.64) | collective-permute-done | bytes 262176 | tf_op jit(solution)/shard_map/ppermute | solution.py:268
  114.6 2.0 %collective-permute-start.66 = (bf16[128,1024]{1,0:T(8,128)(2,1)S(1)}, bf16[128,1024]{1,0:T(8,128)(2,1)S(1)}, u32[]{:S(2)}, u32[]{:S(2)}) collective-permute-start(bf16[128,1024]{1,0:T(8,128)(2,1)S(1)} %get-tuple-element.130), channel_id=1, source_target_pairs={{0,4},{1,5},{4,8},{5,9},{8,12},{9,13},{12,14},{13,15},{14,10},{15,... | collective-permute-start | bytes 786440 | tf_op jit(solution)/shard_map/ppermute | solution.py:268
  117.7 2.2 %shard_map.130 = bf16[1024,384]{1,0:T(8,128)(2,1)} custom-call(bf16[128,1024]{1,0:T(8,128)(2,1)S(1)} %get-tuple-element.132.refs_0_, bf16[256,1024]{1,0:T(8,128)(2,1)S(1)} %get-tuple-element.133.refs_1_, bf16[256,1024]{1,0:T(8,128)(2,1)S(1)} %get-tuple-element.134.refs_2_, bf16[256,1024]{1,0:T(8,128)(2,1)S(1)} %get-tuple-element.135.refs_3_, ...), custom_call_target="tpu_custom_call" | custom-call | flops 805306368 | bytes 3670016 | tf_op jit(solution)/shard_map/pallas_call | solution.py:104
  119.9 2.2 %shard_map.131 = bf16[1024,384]{1,0:T(8,128)(2,1)} custom-call(bf16[128,1024]{1,0:T(8,128)(2,1)S(1)} %get-tuple-element.132.refs_0_, bf16[256,1024]{1,0:T(8,128)(2,1)S(1)} %get-tuple-element.133.refs_1_, bf16[256,1024]{1,0:T(8,128)(2,1)S(1)} %get-tuple-element.134.refs_2_, bf16[256,1024]{1,0:T(8,128)(2,1)S(1)} %get-tuple-element.135.refs_3_, ...), custom_call_target="tpu_custom_call" | custom-call | flops 805306368 | bytes 3670016 | tf_op jit(solution)/shard_map/pallas_call | solution.py:104
  122.1 2.2 %shard_map.132 = bf16[1024,384]{1,0:T(8,128)(2,1)} custom-call(bf16[128,1024]{1,0:T(8,128)(2,1)S(1)} %get-tuple-element.147.refs_0_, bf16[256,1024]{1,0:T(8,128)(2,1)S(1)} %get-tuple-element.148.refs_1_, bf16[256,1024]{1,0:T(8,128)(2,1)S(1)} %get-tuple-element.149.refs_2_, bf16[256,1024]{1,0:T(8,128)(2,1)S(1)} %get-tuple-element.150.refs_3_, ...), custom_call_target="tpu_custom_call" | custom-call | flops 805306368 | bytes 3670016 | tf_op jit(solution)/shard_map/pallas_call | solution.py:104
  125.3 2.0 %collective-permute-done.67.refs_1_ = bf16[128,1024]{1,0:T(8,128)(2,1)S(1)} collective-permute-done((bf16[128,1024]{1,0:T(8,128)(2,1)S(1)}, bf16[128,1024]{1,0:T(8,128)(2,1)S(1)}, u32[]{:S(2)}, u32[]{:S(2)}) %collective-permute-start.67) | collective-permute-done | bytes 262176 | tf_op jit(solution)/shard_map/ppermute | solution.py:268
  (223 shorter events, 69.4 us)
Async XLA Ops:
  0.7 26.3 %collective-permute-start.5 = (bf16[128,1024]{1,0:T(8,128)(2,1)}, bf16[128,1024]{1,0:T(8,128)(2,1)S(1)}, u32[]{:S(2)}, u32[]{:S(2)}) collective-permute-start(bf16[128,1024]{1,0:T(8,128)(2,1)} %refs_1_.1), channel_id=1, source_target_pairs={{0,4},{1,5},{4,8},{5,9},{8,12},{9,13},{12,14},{13,15},{14,10},{15,... | collective-permute-start | bytes 786440 | tf_op jit(solution)/shard_map/ppermute | solution.py:268
  4.4 25.3 %collective-permute-start.6 = (bf16[128,1024]{1,0:T(8,128)(2,1)}, bf16[128,1024]{1,0:T(8,128)(2,1)S(1)}, u32[]{:S(2)}, u32[]{:S(2)}) collective-permute-start(bf16[128,1024]{1,0:T(8,128)(2,1)} %refs_1_.1), channel_id=1, source_target_pairs={{0,2},{1,3},{4,0},{5,1},{8,4},{9,5},{12,8},{13,9},{14,12},{15,13},... | collective-permute-start | bytes 786440 | tf_op jit(solution)/shard_map/ppermute | solution.py:268
  4.5 25.6 %collective-permute-start.40 = (bf16[128,1024]{1,0:T(8,128)(2,1)}, bf16[128,1024]{1,0:T(8,128)(2,1)S(1)}, u32[]{:S(2)}, u32[]{:S(2)}) collective-permute-start(bf16[128,1024]{1,0:T(8,128)(2,1)} %refs_3_.1), channel_id=1, source_target_pairs={{0,4},{1,5},{4,8},{5,9},{8,12},{9,13},{12,14},{13,15},{14,10},{15,... | collective-permute-start | bytes 786440 | tf_op jit(solution)/shard_map/ppermute | solution.py:268
  6.5 9.6 %collective-permute-start.3 = (f32[32,128]{1,0:T(8,128)S(1)}, f32[32,128]{1,0:T(8,128)S(1)}, u32[]{:S(2)}, u32[]{:S(2)}) collective-permute-start(f32[32,128]{1,0:T(8,128)S(1)} %pad_maximum_fusion.refs_0_), channel_id=1, source_target_pairs={{0,4},{1,5},{4,8},{5,9},{8,12},{9,13},{12,14},{13,15},{14,10},{15,... | collective-permute-start | bytes 49160 | tf_op jit(solution)/shard_map/ppermute | solution.py:268
  8.1 10.5 %collective-permute-start.4 = (f32[32,128]{1,0:T(8,128)S(1)}, f32[32,128]{1,0:T(8,128)S(1)}, u32[]{:S(2)}, u32[]{:S(2)}) collective-permute-start(f32[32,128]{1,0:T(8,128)S(1)} %pad_maximum_fusion.refs_0_), channel_id=1, source_target_pairs={{0,2},{1,3},{4,0},{5,1},{8,4},{9,5},{12,8},{13,9},{14,12},{15,13},... | collective-permute-start | bytes 49160 | tf_op jit(solution)/shard_map/ppermute | solution.py:268
  29.8 10.1 %collective-permute-start.13 = (bf16[128,1024]{1,0:T(8,128)(2,1)S(1)}, bf16[128,1024]{1,0:T(8,128)(2,1)S(1)}, u32[]{:S(2)}, u32[]{:S(2)}) collective-permute-start(bf16[128,1024]{1,0:T(8,128)(2,1)S(1)} %collective-permute-done.6.refs_3_), channel_id=1, source_target_pairs={{0,2},{1,3},{4,0},{5,1},{8,4},{9,5},{12,8},{13,9},{14,12},{15,13},... | collective-permute-start | bytes 786440 | tf_op jit(solution)/shard_map/ppermute | solution.py:268
  30.1 12.8 %collective-permute-start.45 = (bf16[128,1024]{1,0:T(8,128)(2,1)S(1)}, bf16[128,1024]{1,0:T(8,128)(2,1)S(1)}, u32[]{:S(2)}, u32[]{:S(2)}) collective-permute-start(bf16[128,1024]{1,0:T(8,128)(2,1)S(1)} %collective-permute-done.40.refs_3_), channel_id=1, source_target_pairs={{0,4},{1,5},{4,8},{5,9},{8,12},{9,13},{12,14},{13,15},{14,10},{15,... | collective-permute-start | bytes 786440 | tf_op jit(solution)/shard_map/ppermute | solution.py:268
  34.3 10.3 %collective-permute-start.8 = (bf16[128,1024]{1,0:T(8,128)(2,1)S(1)}, bf16[128,1024]{1,0:T(8,128)(2,1)S(1)}, u32[]{:S(2)}, u32[]{:S(2)}) collective-permute-start(bf16[128,1024]{1,0:T(8,128)(2,1)S(1)} %collective-permute-done.6.refs_3_), channel_id=1, source_target_pairs={{0,1},{1,0},{2,3},{3,2},{4,5},{5,4},{6,7},{7,6},{8,9},{9,8},{10,11... | collective-permute-start | bytes 786440 | tf_op jit(solution)/shard_map/ppermute | solution.py:271
  34.3 11.2 %collective-permute-start.46 = (bf16[128,1024]{1,0:T(8,128)(2,1)S(1)}, bf16[128,1024]{1,0:T(8,128)(2,1)S(1)}, u32[]{:S(2)}, u32[]{:S(2)}) collective-permute-start(bf16[128,1024]{1,0:T(8,128)(2,1)S(1)} %collective-permute-done.41.refs_4_), channel_id=1, source_target_pairs={{0,2},{1,3},{4,0},{5,1},{8,4},{9,5},{12,8},{13,9},{14,12},{15,13},... | collective-permute-start | bytes 786440 | tf_op jit(solution)/shard_map/ppermute | solution.py:268
  37.2 11.2 %collective-permute-start.19 = (bf16[128,1024]{1,0:T(8,128)(2,1)S(1)}, bf16[128,1024]{1,0:T(8,128)(2,1)S(1)}, u32[]{:S(2)}, u32[]{:S(2)}) collective-permute-start(bf16[128,1024]{1,0:T(8,128)(2,1)S(1)} %collective-permute-done.12.refs_2_), channel_id=1, source_target_pairs={{0,4},{1,5},{4,8},{5,9},{8,12},{9,13},{12,14},{13,15},{14,10},{15,... | collective-permute-start | bytes 786440 | tf_op jit(solution)/shard_map/ppermute | solution.py:268
  39.9 10.9 %collective-permute-start.20 = (bf16[128,1024]{1,0:T(8,128)(2,1)S(1)}, bf16[128,1024]{1,0:T(8,128)(2,1)S(1)}, u32[]{:S(2)}, u32[]{:S(2)}) collective-permute-start(bf16[128,1024]{1,0:T(8,128)(2,1)S(1)} %collective-permute-done.13.refs_3_), channel_id=1, source_target_pairs={{0,2},{1,3},{4,0},{5,1},{8,4},{9,5},{12,8},{13,9},{14,12},{15,13},... | collective-permute-start | bytes 786440 | tf_op jit(solution)/shard_map/ppermute | solution.py:268
  42.8 10.3 %collective-permute-start.50 = (bf16[128,1024]{1,0:T(8,128)(2,1)S(1)}, bf16[128,1024]{1,0:T(8,128)(2,1)S(1)}, u32[]{:S(2)}, u32[]{:S(2)}) collective-permute-start(bf16[128,1024]{1,0:T(8,128)(2,1)S(1)} %collective-permute-done.45.refs_3_), channel_id=1, source_target_pairs={{0,4},{1,5},{4,8},{5,9},{8,12},{9,13},{12,14},{13,15},{14,10},{15,... | collective-permute-start | bytes 786440 | tf_op jit(solution)/shard_map/ppermute | solution.py:268
  45.5 10.2 %collective-permute-start.14 = (bf16[128,1024]{1,0:T(8,128)(2,1)S(1)}, bf16[128,1024]{1,0:T(8,128)(2,1)S(1)}, u32[]{:S(2)}, u32[]{:S(2)}) collective-permute-start(bf16[128,1024]{1,0:T(8,128)(2,1)S(1)} %collective-permute-done.12.refs_2_), channel_id=1, source_target_pairs={{0,1},{1,0},{2,3},{3,2},{4,5},{5,4},{6,7},{7,6},{8,9},{9,8},{10,11... | collective-permute-start | bytes 786440 | tf_op jit(solution)/shard_map/ppermute | solution.py:271
  64.8 11.8 %collective-permute-start.52 = (bf16[128,1024]{1,0:T(8,128)(2,1)S(1)}, bf16[128,1024]{1,0:T(8,128)(2,1)S(1)}, u32[]{:S(2)}, u32[]{:S(2)}) collective-permute-start(bf16[128,1024]{1,0:T(8,128)(2,1)S(1)} %collective-permute-done.50.refs_3_), channel_id=1, source_target_pairs={{0,1},{1,0},{2,3},{3,2},{4,5},{5,4},{6,7},{7,6},{8,9},{9,8},{10,11... | collective-permute-start | bytes 786440 | tf_op jit(solution)/shard_map/ppermute | solution.py:271
  64.8 13.3 %collective-permute-start.53 = (bf16[128,1024]{1,0:T(8,128)(2,1)S(1)}, bf16[128,1024]{1,0:T(8,128)(2,1)S(1)}, u32[]{:S(2)}, u32[]{:S(2)}) collective-permute-start(bf16[128,1024]{1,0:T(8,128)(2,1)S(1)} %collective-permute-done.51.refs_4_), channel_id=1, source_target_pairs={{0,1},{1,0},{2,3},{3,2},{4,5},{5,4},{6,7},{7,6},{8,9},{9,8},{10,11... | collective-permute-start | bytes 786440 | tf_op jit(solution)/shard_map/ppermute | solution.py:271
  76.2 10.0 %collective-permute-start.23 = (bf16[128,1024]{1,0:T(8,128)(2,1)S(1)}, bf16[128,1024]{1,0:T(8,128)(2,1)S(1)}, u32[]{:S(2)}, u32[]{:S(2)}) collective-permute-start(bf16[128,1024]{1,0:T(8,128)(2,1)S(1)} %get-tuple-element.92), channel_id=1, source_target_pairs={{0,1},{1,0},{2,3},{3,2},{4,5},{5,4},{6,7},{7,6},{8,9},{9,8},{10,11... | collective-permute-start | bytes 786440 | tf_op jit(solution)/shard_map/ppermute | solution.py:271
  80.1 10.4 %collective-permute-start.54 = (bf16[128,1024]{1,0:T(8,128)(2,1)S(1)}, bf16[128,1024]{1,0:T(8,128)(2,1)S(1)}, u32[]{:S(2)}, u32[]{:S(2)}) collective-permute-start(bf16[128,1024]{1,0:T(8,128)(2,1)S(1)} %get-tuple-element.119), channel_id=1, source_target_pairs={{0,1},{1,0},{2,3},{3,2},{4,5},{5,4},{6,7},{7,6},{8,9},{9,8},{10,11... | collective-permute-start | bytes 786440 | tf_op jit(solution)/shard_map/ppermute | solution.py:271
  90.9 10.1 %collective-permute-start.62 = (bf16[128,1024]{1,0:T(8,128)(2,1)S(1)}, bf16[128,1024]{1,0:T(8,128)(2,1)S(1)}, u32[]{:S(2)}, u32[]{:S(2)}) collective-permute-start(bf16[128,1024]{1,0:T(8,128)(2,1)S(1)} %get-tuple-element.126), channel_id=1, source_target_pairs={{0,2},{1,3},{4,0},{5,1},{8,4},{9,5},{12,8},{13,9},{14,12},{15,13},... | collective-permute-start | bytes 786440 | tf_op jit(solution)/shard_map/ppermute | solution.py:268
  92.1 12.4 %collective-permute-start.63 = (bf16[128,1024]{1,0:T(8,128)(2,1)S(1)}, bf16[128,1024]{1,0:T(8,128)(2,1)S(1)}, u32[]{:S(2)}, u32[]{:S(2)}) collective-permute-start(bf16[128,1024]{1,0:T(8,128)(2,1)S(1)} %get-tuple-element.127), channel_id=1, source_target_pairs={{0,4},{1,5},{4,8},{5,9},{8,12},{9,13},{12,14},{13,15},{14,10},{15,... | collective-permute-start | bytes 786440 | tf_op jit(solution)/shard_map/ppermute | solution.py:268
  108.7 11.2 %collective-permute-start.2 = (bf16[64,1024]{1,0:T(8,128)(2,1)S(1)}, bf16[64,1024]{1,0:T(8,128)(2,1)S(1)}, u32[]{:S(2)}, u32[]{:S(2)}) collective-permute-start(bf16[64,1024]{1,0:T(8,128)(2,1)S(1)} %get-tuple-element.83), channel_id=1, source_target_pairs={{0,1},{1,0},{2,3},{3,2},{4,5},{5,4},{6,7},{7,6},{8,9},{9,8},{10,11... | collective-permute-start | bytes 393224 | tf_op jit(solution)/shard_map/ppermute | solution.py:271
  109.6 14.7 %collective-permute-start.36 = (bf16[128,1024]{1,0:T(8,128)(2,1)S(1)}, bf16[128,1024]{1,0:T(8,128)(2,1)S(1)}, u32[]{:S(2)}, u32[]{:S(2)}) collective-permute-start(bf16[128,1024]{1,0:T(8,128)(2,1)S(1)} %get-tuple-element.102), channel_id=1, source_target_pairs={{0,4},{1,5},{4,8},{5,9},{8,12},{9,13},{12,14},{13,15},{14,10},{15,... | collective-permute-start | bytes 786440 | tf_op jit(solution)/shard_map/ppermute | solution.py:268
  113.7 10.6 %collective-permute-start.37 = (bf16[128,1024]{1,0:T(8,128)(2,1)S(1)}, bf16[128,1024]{1,0:T(8,128)(2,1)S(1)}, u32[]{:S(2)}, u32[]{:S(2)}) collective-permute-start(bf16[128,1024]{1,0:T(8,128)(2,1)S(1)} %get-tuple-element.103), channel_id=1, source_target_pairs={{0,2},{1,3},{4,0},{5,1},{8,4},{9,5},{12,8},{13,9},{14,12},{15,13},... | collective-permute-start | bytes 786440 | tf_op jit(solution)/shard_map/ppermute | solution.py:268
  114.6 10.6 %collective-permute-start.66 = (bf16[128,1024]{1,0:T(8,128)(2,1)S(1)}, bf16[128,1024]{1,0:T(8,128)(2,1)S(1)}, u32[]{:S(2)}, u32[]{:S(2)}) collective-permute-start(bf16[128,1024]{1,0:T(8,128)(2,1)S(1)} %get-tuple-element.130), channel_id=1, source_target_pairs={{0,4},{1,5},{4,8},{5,9},{8,12},{9,13},{12,14},{13,15},{14,10},{15,... | collective-permute-start | bytes 786440 | tf_op jit(solution)/shard_map/ppermute | solution.py:268
  116.6 10.6 %collective-permute-start.67 = (bf16[128,1024]{1,0:T(8,128)(2,1)S(1)}, bf16[128,1024]{1,0:T(8,128)(2,1)S(1)}, u32[]{:S(2)}, u32[]{:S(2)}) collective-permute-start(bf16[128,1024]{1,0:T(8,128)(2,1)S(1)} %get-tuple-element.131), channel_id=1, source_target_pairs={{0,2},{1,3},{4,0},{5,1},{8,4},{9,5},{12,8},{13,9},{14,12},{15,13},... | collective-permute-start | bytes 786440 | tf_op jit(solution)/shard_map/ppermute | solution.py:268
  (84 other events, 471.4 us)

commit v2 on v1

--- a/solution.py
+++ b/solution.py
@@ -121,25 +121,44 @@
     return parts[0] if len(parts) == 1 else jnp.concatenate(parts, axis=0)
 
 
+def payload_body(routes_ref, combine_ref, tokens_ref, out_ref):
+    top, tok = routes_ref.shape
+    exact = combine_ref[...]
+    high = exact.astype(BF16)
+    rest = exact - high.astype(F32)
+    middle = rest.astype(BF16)
+    low = (rest - middle.astype(F32)).astype(BF16)
+    blank = jnp.zeros((top, tok), F32)
+    names = jnp.concatenate([routes_ref[...].astype(F32), high.astype(F32)], axis=0)
+    out_ref[: 2 * top] = jnp.zeros((2 * top, out_ref.shape[1]), BF16)
+    out_ref[: 2 * top, :tok] = names.astype(BF16)
+    for i, term in enumerate((middle, low)):
+        padded = jnp.concatenate([blank, term.astype(F32)], axis=0)
+        out_ref[: 2 * top, (i + 1) * tok : (i + 2) * tok] = padded.astype(BF16)
+    out_ref[2 * top :] = tokens_ref[...]
+
+
 def forward_body(dirs, halves, cap, top, expert_ref, *refs):
-    metas = refs[:dirs]
-    refs = refs[dirs:]
     count = dirs * halves
-    own = refs[:count]
-    other = refs[count : 2 * count]
+    sides = (refs[:count], refs[count : 2 * count])
     w_gate, w_up, w_down = refs[2 * count : 2 * count + 3]
     info_ref, rows_ref, slope_ref, act_ref, hidden_ref, keep_ref, give_ref = refs[2 * count + 3 :]
     me = expert_ref[0].astype(F32)
     mate = expert_ref[1].astype(F32)
-    tok = metas[0].shape[1]
+    head = 2 * top
+    tok = info_ref.shape[1]
+    names, terms = [], []
+    for blocks in sides:
+        for d in range(dirs):
+            told = blocks[d * halves][:head, : 3 * tok].astype(F32)
+            names.append(told[:top, :tok])
+            told = told[top:]
+            terms.append(told[:, :tok] + (told[:, tok : 2 * tok] + told[:, 2 * tok :]))
     masks, weights = [], []
-    for expert, side in ((me, 0), (me, 1), (mate, 0)):
-        for d in range(dirs):
-            base = side * 2 * top
-            hit = metas[d][base : base + top] == expert
-            masks.append(jnp.sum(jnp.where(hit, 1.0, 0.0), axis=0, keepdims=True))
-            share = jnp.where(hit, metas[d][base + top : base + 2 * top], 0.0)
-            weights.append(jnp.sum(share, axis=0, keepdims=True))
+    for expert, which in [(me, i) for i in range(2 * dirs)] + [(mate, i) for i in range(dirs)]:
+        hit = names[which] == expert
+        masks.append(jnp.sum(jnp.where(hit, 1.0, 0.0), axis=0, keepdims=True))
+        weights.append(jnp.sum(jnp.where(hit, terms[which], 0.0), axis=0, keepdims=True))
     pad = jnp.zeros((8 - len(masks), tok), F32)
     mask = jnp.concatenate(masks + [pad], axis=0)
     before = lax.broadcasted_iota(jnp.int32, (tok, tok), 0) < lax.broadcasted_iota(
@@ -152,12 +171,13 @@
     info_ref[0:8] = place
     info_ref[8:16] = jnp.concatenate(weights + [pad], axis=0)
     share = []
-    for side, blocks in enumerate((own, other)):
+    for side, blocks in enumerate(sides):
         for d in range(dirs):
             i = side * dirs + d
             pick = picks(place[i : i + 1], cap)
             share.append(jnp.sum(pick * weights[i], axis=1, keepdims=True))
-            block = joined([b[...] for b in blocks[d * halves : (d + 1) * halves]])
+            first, *others = blocks[d * halves : (d + 1) * halves]
+            block = joined([first[head:]] + [b[...] for b in others])
             taken = jnp.dot(pick.astype(BF16), block, preferred_element_type=F32)
             rows_ref[i * cap : (i + 1) * cap] = taken.astype(BF16)
     rows = rows_ref[...]
@@ -267,76 +287,85 @@
         ]
         return lax.ppermute(value, "expert", moves)
 
+    def after(value, *others):
+        return lax.optimization_barrier((value, *others))[0] if others else value
+
     def swap(value):
         return lax.ppermute(value, "expert", [(i, i ^ 1) for i in range(n)])
 
-    def spread(block, split):
-        found = [[block]]
-        back = front = block
-        for step in range(1, reach + 1):
-            if step == reach and split:
-                back, front = hop(back[:half], 1), hop(front[half:], -1)
-            elif step == reach:
-                found.append([hop(back, 1)])
-                break
-            else:
-                back, front = hop(back, 1), hop(front, -1)
-            found.append([back, front])
-        return found
+    def struct(shape, dtype):
+        return jax.ShapeDtypeStruct(shape, dtype)
+
+    def shape_of(step):
+        return (2 if 0 < step < reach else 1), (2 if step == reach else 1)
 
     here = lax.axis_index("expert").astype(jnp.int32)
     expert = jnp.stack([here, here ^ 1])
-    meta = jnp.concatenate([routes.T.astype(F32), combine.T], axis=0)
-    metas = spread(jnp.concatenate([meta, swap(meta)], axis=0), False)
-    token_blocks = spread(tokens, True)
-    token_other = [[swap(b) for b in found] for found in token_blocks]
-    cot_blocks = spread(cotangent, True)
-    cot_other = [[swap(b) for b in found] for found in cot_blocks]
-
-    def struct(shape, dtype):
-        return jax.ShapeDtypeStruct(shape, dtype)
-
-    forward, backward = [], []
-    for step in range(reach + 1):
-        dirs = 2 if 0 < step < reach else 1
-        halves = 2 if step == reach else 1
+    head = 2 * top
+
+    def onward(found, step, cut, waits):
+        back, front = found[0], found[-1]
+        if step == reach:
+            back, front = back[: half + cut], front[half + cut :]
+        return [hop(after(back, *waits), 1), hop(after(front, *waits), -1)]
+
+    def run_forward(step):
+        dirs, halves = shape_of(step)
         m = 2 * dirs * cap
-        forward.append(
-            call(
-                functools.partial(forward_body, dirs, halves, cap, top),
-                [
-                    struct((16, tok), F32),
-                    struct((m, width), BF16),
-                    struct((m, units), F32),
-                    struct((m, units), F32),
-                    struct((m, units), BF16),
-                    struct((m // 2, width), BF16),
-                    struct((m // 2, width), BF16),
-                ],
-                [expert, *metas[step], *token_blocks[step], *token_other[step], gate_w, up_w, down_w],
-                2 * m * width * (3 * units + tok),
-                smem=1,
-            )
+        return call(
+            functools.partial(forward_body, dirs, halves, cap, top),
+            [
+                struct((16, tok), F32),
+                struct((m, width), BF16),
+                struct((m, units), F32),
+                struct((m, units), F32),
+                struct((m, units), BF16),
+                struct((m // 2, width), BF16),
+                struct((m // 2, width), BF16),
+            ],
+            [expert, *token_own[step], *token_other[step], gate_w, up_w, down_w],
+            2 * m * width * (3 * units + tok),
+            smem=1,
         )
-    for step in range(reach + 1):
-        dirs = 2 if 0 < step < reach else 1
-        halves = 2 if step == reach else 1
+
+    def run_backward(step):
+        dirs, halves = shape_of(step)
         m = 2 * dirs * cap
         info, _, slope, act = forward[step][:4]
-        backward.append(
-            call(
-                functools.partial(backward_body, dirs, halves, cap),
-                [
-                    struct((m, width), BF16),
-                    struct((m, units), BF16),
-                    struct((m, units), BF16),
-                    struct((m // 2, width), BF16),
-                    struct((m // 2, width), BF16),
-                ],
-                [info, slope, act, *cot_blocks[step], *cot_other[step], gate_w, up_w, down_w],
-                2 * m * width * (3 * units + tok),
-            )
+        return call(
+            functools.partial(backward_body, dirs, halves, cap),
+            [
+                struct((m, width), BF16),
+                struct((m, units), BF16),
+                struct((m, units), BF16),
+                struct((m // 2, width), BF16),
+                struct((m // 2, width), BF16),
+            ],
+            [info, slope, act, *cot_own[step], *cot_other[step], gate_w, up_w, down_w],
+            2 * m * width * (3 * units + tok),
         )
+
+    payload = call(
+        payload_body, [struct((head + tok, width), BF16)], [routes.T, combine.T, tokens], 0
+    )[0]
+    token_own, cot_own = [[payload]], [[cotangent]]
+    token_other, cot_other = [[swap(payload)]], []
+    forward, backward = [], []
+    for step in range(1, reach + 1):
+        waits = [forward[step - 2][0]] if step > 1 else []
+        token_own.append(onward(token_own[-1], step, head, waits))
+        waits = [token_own[step][0]]
+        if step > 1:
+            waits.append(backward[step - 2][1])
+        token_other.append([swap(b) for b in token_own[step]])
+        if step == 1:
+            cot_other.append([swap(cotangent)])
+        cot_own.append(onward(cot_own[-1], step, 0, waits))
+        cot_other.append([swap(b) for b in cot_own[step]])
+        forward.append(run_forward(step - 1))
+        backward.append(run_backward(step - 1))
+    forward.append(run_forward(reach))
+    backward.append(run_backward(reach))
 
     def gather_sums(kept, given):
         given = [swap(g) for g in given]
@@ -393,6 +422,7 @@
         and n <= 2 * top
         and tok % 128 == 0
         and top % 8 == 0
+        and width >= 3 * tok
         and (tok * top) % (16 * n) == 0
     )
     plan = by_ring if ring else by_all_to_all

time: 129 us -> 125 us (0.969)
  waiting for transfers between devices: 36.3 us -> 52 us
  starting transfers between devices: 49.9 us -> 39.8 us
  local copies, waits for them, and re-layouts: 12.2 us -> 5.77 us
  Pallas kernels: 27.8 us -> 25.9 us
    ppermute x39 -> x32, waiting for transfers between devices: 36.3 us -> 51.8 us  [hop(): return lax.ppermute(value, 'expert', moves)]
    ppermute x39 -> x32, starting transfers between devices: 45.9 us -> 34.5 us  [hop(): return lax.ppermute(value, 'expert', moves)]
    unnamed x80 -> x20, local copies, waits for them, and re-layouts: 12.2 us -> 5.73 us
    pallas_call x23 -> x24, Pallas kernels: 27.8 us -> 25.9 us  [call(): pl.pallas_call(body, out_shape=list(outs), in_specs=specs, out_specs=[pl....]
    ppermute x29 -> x28, starting transfers between devices: 3.95 us -> 5.36 us  [swap(): return lax.ppermute(value, 'expert', [(i, i ^ 1) for i in range(n)])]
  transfers between devices with their start and end apart: 68 -> 60, of which waited for: 23 -> 19; matrix products, arithmetic and copies ran while one was open for 1% -> 0% of each run, Pallas kernels for 21% -> 20%
where the time goes in v2:
time: 125 us
  waiting for transfers between devices  52 us (42%)
  starting transfers between devices  39.8 us (32%)
  Pallas kernels  25.9 us (21%)
  local copies, waits for them, and re-layouts  5.77 us (5%)
    ppermute x32, waiting for transfers between devices, hop(): return lax.ppermute(value, 'expert', moves)  51.8 us
    ppermute x32, starting transfers between devices, hop(): return lax.ppermute(value, 'expert', moves)  34.5 us
    pallas_call x24, Pallas kernels, call(): pl.pallas_call(body, out_shape=list(outs), in_specs=specs, out_specs=[pl....  25.9 us
    unnamed x20, local copies, waits for them, and re-layouts  5.73 us
    ppermute x28, starting transfers between devices, swap(): return lax.ppermute(value, 'expert', [(i, i ^ 1) for i in range(n)])  5.36 us
  transfers between devices with their start and end apart: 60, of which 19 were waited for; matrix products, arithmetic and copies ran while one was open for 0% of the time, Pallas kernels for 20%

profile of v2, /device:TPU:0, one launch (start us, length us, event | category | flops | bytes accessed | tf_op | source)
XLA Modules:
  0.0 124.5 jit_solution(8131851218212979503)
XLA Ops:
  3.0 3.1 %collective-permute-start.2 = (bf16[144,1024]{1,0:T(8,128)(2,1)S(1)}, bf16[144,1024]{1,0:T(8,128)(2,1)S(1)}, u32[]{:S(2)}, u32[]{:S(2)}) collective-permute-start(bf16[144,1024]{1,0:T(8,128)(2,1)S(1)} %shard_map.110.refs_0_), channel_id=1, source_target_pairs={{0,4},{1,5},{4,8},{5,9},{8,12},{9,13},{12,14},{13,15},{14,10},{15,... | collective-permute-start | bytes 884744 | tf_op jit(solution)/shard_map/ppermute | solution.py:288
  6.9 6.1 %collective-permute-done.2.refs_0_ = bf16[144,1024]{1,0:T(8,128)(2,1)S(1)} collective-permute-done((bf16[144,1024]{1,0:T(8,128)(2,1)S(1)}, bf16[144,1024]{1,0:T(8,128)(2,1)S(1)}, u32[]{:S(2)}, u32[]{:S(2)}) %collective-permute-start.2) | collective-permute-done | bytes 294944 | tf_op jit(solution)/shard_map/ppermute | solution.py:288
  13.0 1.8 %collective-permute-start.32 = (bf16[128,1024]{1,0:T(8,128)(2,1)S(1)}, bf16[128,1024]{1,0:T(8,128)(2,1)S(1)}, u32[]{:S(2)}, u32[]{:S(2)}) collective-permute-start(bf16[128,1024]{1,0:T(8,128)(2,1)S(1)} %copy-done.6), channel_id=1, source_target_pairs={{0,4},{1,5},{4,8},{5,9},{8,12},{9,13},{12,14},{13,15},{14,10},{15,... | collective-permute-start | bytes 786440 | tf_op jit(solution)/shard_map/ppermute | solution.py:288
  19.8 1.6 %collective-permute-start.7 = (bf16[144,1024]{1,0:T(8,128)(2,1)S(1)}, bf16[144,1024]{1,0:T(8,128)(2,1)S(1)}, u32[]{:S(2)}, u32[]{:S(2)}) collective-permute-start(bf16[144,1024]{1,0:T(8,128)(2,1)S(1)} %collective-permute-done.2.refs_0_), channel_id=1, source_target_pairs={{0,4},{1,5},{4,8},{5,9},{8,12},{9,13},{12,14},{13,15},{14,10},{15,... | collective-permute-start | bytes 884744 | tf_op jit(solution)/shard_map/ppermute | solution.py:288
  22.6 8.1 %collective-permute-done.33.refs_4_ = bf16[128,1024]{1,0:T(8,128)(2,1)S(1)} collective-permute-done((bf16[128,1024]{1,0:T(8,128)(2,1)S(1)}, bf16[128,1024]{1,0:T(8,128)(2,1)S(1)}, u32[]{:S(2)}, u32[]{:S(2)}) %collective-permute-start.33) | collective-permute-done | bytes 262176 | tf_op jit(solution)/shard_map/ppermute | solution.py:288
  32.2 1.6 %collective-permute-start.37 = (bf16[128,1024]{1,0:T(8,128)(2,1)S(1)}, bf16[128,1024]{1,0:T(8,128)(2,1)S(1)}, u32[]{:S(2)}, u32[]{:S(2)}) collective-permute-start(bf16[128,1024]{1,0:T(8,128)(2,1)S(1)} %collective-permute-done.32.refs_3_), channel_id=1, source_target_pairs={{0,4},{1,5},{4,8},{5,9},{8,12},{9,13},{12,14},{13,15},{14,10},{15,... | collective-permute-start | bytes 786440 | tf_op jit(solution)/shard_map/ppermute | solution.py:288
  34.3 2.0 %shard_map.112 = (f32[16,128]{1,0:T(8,128)S(1)}, bf16[256,1024]{1,0:T(8,128)(2,1)S(1)}, f32[256,384]{1,0:T(8,128)S(1)}, f32[256,384]{1,0:T(8,128)S(1)}, bf16[256...) custom-call(s32[2]{0:T(128)S(1)} %pad_add_fusion.expert_ref, ...), custom_call_target="tpu_custom_call" | custom-call | flops 671088640 | bytes 5578760 | tf_op jit(solution)/shard_map/pallas_call | solution.py:104
  37.3 3.2 %collective-permute-done.37.refs_3_ = bf16[128,1024]{1,0:T(8,128)(2,1)S(1)} collective-permute-done((bf16[128,1024]{1,0:T(8,128)(2,1)S(1)}, bf16[128,1024]{1,0:T(8,128)(2,1)S(1)}, u32[]{:S(2)}, u32[]{:S(2)}) %collective-permute-start.37) | collective-permute-done | bytes 262176 | tf_op jit(solution)/shard_map/ppermute | solution.py:288
  40.5 1.6 %collective-permute-start.12 = (bf16[144,1024]{1,0:T(8,128)(2,1)S(1)}, bf16[144,1024]{1,0:T(8,128)(2,1)S(1)}, u32[]{:S(2)}, u32[]{:S(2)}) collective-permute-start(bf16[144,1024]{1,0:T(8,128)(2,1)S(1)} %collective-permute-done.7.refs_0_), channel_id=1, source_target_pairs={{0,4},{1,5},{4,8},{5,9},{8,12},{9,13},{12,14},{13,15},{14,10},{15,... | collective-permute-start | bytes 884744 | tf_op jit(solution)/shard_map/ppermute | solution.py:288
  44.3 3.8 %collective-permute-done.13.refs_1_ = bf16[144,1024]{1,0:T(8,128)(2,1)S(1)} collective-permute-done((bf16[144,1024]{1,0:T(8,128)(2,1)S(1)}, bf16[144,1024]{1,0:T(8,128)(2,1)S(1)}, u32[]{:S(2)}, u32[]{:S(2)}) %collective-permute-start.13) | collective-permute-done | bytes 294944 | tf_op jit(solution)/shard_map/ppermute | solution.py:288
  48.1 2.0 %shard_map.113 = (f32[16,128]{1,0:T(8,128)S(1)}, bf16[256,1024]{1,0:T(8,128)(2,1)S(1)}, f32[256,384]{1,0:T(8,128)S(1)}, f32[256,384]{1,0:T(8,128)S(1)}, bf16[256...) custom-call(s32[2]{0:T(128)S(1)} %pad_add_fusion.expert_ref, ...), custom_call_target="tpu_custom_call" | custom-call | flops 671088640 | bytes 5578760 | tf_op jit(solution)/shard_map/pallas_call | solution.py:104
  53.8 3.5 %collective-permute-done.18.refs_1_ = bf16[64,1024]{1,0:T(8,128)(2,1)S(1)} collective-permute-done((bf16[64,1024]{1,0:T(8,128)(2,1)S(1)}, bf16[64,1024]{1,0:T(8,128)(2,1)S(1)}, u32[]{:S(2)}, u32[]{:S(2)}) %collective-permute-start.18) | collective-permute-done | bytes 131104 | tf_op jit(solution)/shard_map/ppermute | solution.py:288
  57.8 4.6 %collective-permute-done.17.refs_0_ = bf16[80,1024]{1,0:T(8,128)(2,1)S(1)} collective-permute-done((bf16[80,1024]{1,0:T(8,128)(2,1)S(1)}, bf16[80,1024]{1,0:T(8,128)(2,1)S(1)}, u32[]{:S(2)}, u32[]{:S(2)}) %collective-permute-start.17) | collective-permute-done | bytes 163872 | tf_op jit(solution)/shard_map/ppermute | solution.py:288
  69.0 2.0 %shard_map.114 = (f32[16,128]{1,0:T(8,128)S(1)}, bf16[256,1024]{1,0:T(8,128)(2,1)S(1)}, f32[256,384]{1,0:T(8,128)S(1)}, f32[256,384]{1,0:T(8,128)S(1)}, bf16[256...) custom-call(s32[2]{0:T(128)S(1)} %pad_add_fusion.expert_ref, ...), custom_call_target="tpu_custom_call" | custom-call | flops 671088640 | bytes 5578760 | tf_op jit(solution)/shard_map/pallas_call | solution.py:104
  71.6 2.4 %collective-permute-done.48.refs_4_ = bf16[64,1024]{1,0:T(8,128)(2,1)S(1)} collective-permute-done((bf16[64,1024]{1,0:T(8,128)(2,1)S(1)}, bf16[64,1024]{1,0:T(8,128)(2,1)S(1)}, u32[]{:S(2)}, u32[]{:S(2)}) %collective-permute-start.48) | collective-permute-done | bytes 131104 | tf_op jit(solution)/shard_map/ppermute | solution.py:288
  82.2 1.6 %collective-permute-start.53 = (bf16[64,1024]{1,0:T(8,128)(2,1)S(1)}, bf16[64,1024]{1,0:T(8,128)(2,1)S(1)}, u32[]{:S(2)}, u32[]{:S(2)}) collective-permute-start(bf16[64,1024]{1,0:T(8,128)(2,1)S(1)} %get-tuple-element.154), channel_id=1, source_target_pairs={{0,4},{1,5},{4,8},{5,9},{8,12},{9,13},{12,14},{13,15},{14,10},{15,... | collective-permute-start | bytes 393224 | tf_op jit(solution)/shard_map/ppermute | solution.py:288
  85.2 6.5 %collective-permute-done.52.refs_0_ = bf16[64,1024]{1,0:T(8,128)(2,1)S(1)} collective-permute-done((bf16[64,1024]{1,0:T(8,128)(2,1)S(1)}, bf16[64,1024]{1,0:T(8,128)(2,1)S(1)}, u32[]{:S(2)}, u32[]{:S(2)}) %collective-permute-start.52) | collective-permute-done | bytes 131104 | tf_op jit(solution)/shard_map/ppermute | solution.py:288
  96.5 4.6 %collective-permute-done.54.refs_0_ = bf16[128,1024]{1,0:T(8,128)(2,1)S(1)} collective-permute-done((bf16[128,1024]{1,0:T(8,128)(2,1)S(1)}, bf16[128,1024]{1,0:T(8,128)(2,1)S(1)}, u32[]{:S(2)}, u32[]{:S(2)}) %collective-permute-start.54) | collective-permute-done | bytes 262176 | tf_op jit(solution)/shard_map/ppermute | solution.py:288
  102.6 1.6 %collective-permute-start.57 = (bf16[128,1024]{1,0:T(8,128)(2,1)S(1)}, bf16[128,1024]{1,0:T(8,128)(2,1)S(1)}, u32[]{:S(2)}, u32[]{:S(2)}) collective-permute-start(bf16[128,1024]{1,0:T(8,128)(2,1)S(1)} %get-tuple-element.158), channel_id=1, source_target_pairs={{0,4},{1,5},{4,8},{5,9},{8,12},{9,13},{12,14},{13,15},{14,10},{15,... | collective-permute-start | bytes 786440 | tf_op jit(solution)/shard_map/ppermute | solution.py:288
  104.2 2.6 %collective-permute-done.26.refs_0_ = bf16[128,1024]{1,0:T(8,128)(2,1)S(1)} collective-permute-done((bf16[128,1024]{1,0:T(8,128)(2,1)S(1)}, bf16[128,1024]{1,0:T(8,128)(2,1)S(1)}, u32[]{:S(2)}, u32[]{:S(2)}) %collective-permute-start.26) | collective-permute-done | bytes 262176 | tf_op jit(solution)/shard_map/ppermute | solution.py:288
  109.8 2.6 %collective-permute-done.56.refs_0_ = bf16[128,1024]{1,0:T(8,128)(2,1)S(1)} collective-permute-done((bf16[128,1024]{1,0:T(8,128)(2,1)S(1)}, bf16[128,1024]{1,0:T(8,128)(2,1)S(1)}, u32[]{:S(2)}, u32[]{:S(2)}) %collective-permute-start.56) | collective-permute-done | bytes 262176 | tf_op jit(solution)/shard_map/ppermute | solution.py:288
  115.4 2.2 %shard_map.131 = bf16[1024,384]{1,0:T(8,128)(2,1)} custom-call(bf16[128,1024]{1,0:T(8,128)(2,1)S(1)} %get-tuple-element.161.refs_0_, bf16[256,1024]{1,0:T(8,128)(2,1)S(1)} %get-tuple-element.162.refs_1_, bf16[256,1024]{1,0:T(8,128)(2,1)S(1)} %get-tuple-element.163.refs_2_, bf16[256,1024]{1,0:T(8,128)(2,1)S(1)} %get-tuple-element.164.refs_3_, ...), custom_call_target="tpu_custom_call" | custom-call | flops 805306368 | bytes 3670016 | tf_op jit(solution)/shard_map/pallas_call | solution.py:104
  117.6 2.2 %shard_map.132 = bf16[1024,384]{1,0:T(8,128)(2,1)} custom-call(bf16[128,1024]{1,0:T(8,128)(2,1)S(1)} %get-tuple-element.161.refs_0_, bf16[256,1024]{1,0:T(8,128)(2,1)S(1)} %get-tuple-element.162.refs_1_, bf16[256,1024]{1,0:T(8,128)(2,1)S(1)} %get-tuple-element.163.refs_2_, bf16[256,1024]{1,0:T(8,128)(2,1)S(1)} %get-tuple-element.164.refs_3_, ...), custom_call_target="tpu_custom_call" | custom-call | flops 805306368 | bytes 3670016 | tf_op jit(solution)/shard_map/pallas_call | solution.py:104
  119.8 2.2 %shard_map.133 = bf16[1024,384]{1,0:T(8,128)(2,1)} custom-call(bf16[128,1024]{1,0:T(8,128)(2,1)S(1)} %get-tuple-element.173.refs_0_, bf16[256,1024]{1,0:T(8,128)(2,1)S(1)} %get-tuple-element.174.refs_1_, bf16[256,1024]{1,0:T(8,128)(2,1)S(1)} %get-tuple-element.175.refs_2_, bf16[256,1024]{1,0:T(8,128)(2,1)S(1)} %get-tuple-element.176.refs_3_, ...), custom_call_target="tpu_custom_call" | custom-call | flops 805306368 | bytes 3670016 | tf_op jit(solution)/shard_map/pallas_call | solution.py:104
  (145 shorter events, 50.1 us)
Async XLA Ops:
  6.1 15.8 %collective-permute-start.30 = (bf16[128,1024]{1,0:T(8,128)(2,1)S(1)}, bf16[128,1024]{1,0:T(8,128)(2,1)S(1)}, u32[]{:S(2)}, u32[]{:S(2)}) collective-permute-start(bf16[128,1024]{1,0:T(8,128)(2,1)S(1)} %copy-done.6), channel_id=1, source_target_pairs={{0,1},{1,0},{2,3},{3,2},{4,5},{5,4},{6,7},{7,6},{8,9},{9,8},{10,11... | collective-permute-start | bytes 786440 | tf_op jit(solution)/shard_map/ppermute | solution.py:294
  6.6 15.3 %collective-permute-start.3 = (bf16[144,1024]{1,0:T(8,128)(2,1)S(1)}, bf16[144,1024]{1,0:T(8,128)(2,1)S(1)}, u32[]{:S(2)}, u32[]{:S(2)}) collective-permute-start(bf16[144,1024]{1,0:T(8,128)(2,1)S(1)} %shard_map.110.refs_0_), channel_id=1, source_target_pairs={{0,2},{1,3},{4,0},{5,1},{8,4},{9,5},{12,8},{13,9},{14,12},{15,13},... | collective-permute-start | bytes 884744 | tf_op jit(solution)/shard_map/ppermute | solution.py:288
  19.8 10.9 %collective-permute-start.7 = (bf16[144,1024]{1,0:T(8,128)(2,1)S(1)}, bf16[144,1024]{1,0:T(8,128)(2,1)S(1)}, u32[]{:S(2)}, u32[]{:S(2)}) collective-permute-start(bf16[144,1024]{1,0:T(8,128)(2,1)S(1)} %collective-permute-done.2.refs_0_), channel_id=1, source_target_pairs={{0,4},{1,5},{4,8},{5,9},{8,12},{9,13},{12,14},{13,15},{14,10},{15,... | collective-permute-start | bytes 884744 | tf_op jit(solution)/shard_map/ppermute | solution.py:288
  21.9 10.3 %collective-permute-start.4 = (bf16[144,1024]{1,0:T(8,128)(2,1)S(1)}, bf16[144,1024]{1,0:T(8,128)(2,1)S(1)}, u32[]{:S(2)}, u32[]{:S(2)}) collective-permute-start(bf16[144,1024]{1,0:T(8,128)(2,1)S(1)} %collective-permute-done.2.refs_0_), channel_id=1, source_target_pairs={{0,1},{1,0},{2,3},{3,2},{4,5},{5,4},{6,7},{7,6},{8,9},{9,8},{10,11... | collective-permute-start | bytes 884744 | tf_op jit(solution)/shard_map/ppermute | solution.py:294
  21.9 12.0 %collective-permute-start.5 = (bf16[144,1024]{1,0:T(8,128)(2,1)S(1)}, bf16[144,1024]{1,0:T(8,128)(2,1)S(1)}, u32[]{:S(2)}, u32[]{:S(2)}) collective-permute-start(bf16[144,1024]{1,0:T(8,128)(2,1)S(1)} %collective-permute-done.3.refs_1_), channel_id=1, source_target_pairs={{0,1},{1,0},{2,3},{3,2},{4,5},{5,4},{6,7},{7,6},{8,9},{9,8},{10,11... | collective-permute-start | bytes 884744 | tf_op jit(solution)/shard_map/ppermute | solution.py:294
  22.4 13.9 %collective-permute-start.8 = (bf16[144,1024]{1,0:T(8,128)(2,1)S(1)}, bf16[144,1024]{1,0:T(8,128)(2,1)S(1)}, u32[]{:S(2)}, u32[]{:S(2)}) collective-permute-start(bf16[144,1024]{1,0:T(8,128)(2,1)S(1)} %collective-permute-done.3.refs_1_), channel_id=1, source_target_pairs={{0,2},{1,3},{4,0},{5,1},{8,4},{9,5},{12,8},{13,9},{14,12},{15,13},... | collective-permute-start | bytes 884744 | tf_op jit(solution)/shard_map/ppermute | solution.py:288
  36.3 11.8 %collective-permute-start.13 = (bf16[144,1024]{1,0:T(8,128)(2,1)S(1)}, bf16[144,1024]{1,0:T(8,128)(2,1)S(1)}, u32[]{:S(2)}, u32[]{:S(2)}) collective-permute-start(bf16[144,1024]{1,0:T(8,128)(2,1)S(1)} %collective-permute-done.8.refs_1_), channel_id=1, source_target_pairs={{0,2},{1,3},{4,0},{5,1},{8,4},{9,5},{12,8},{13,9},{14,12},{15,13},... | collective-permute-start | bytes 884744 | tf_op jit(solution)/shard_map/ppermute | solution.py:288
  36.8 11.4 %collective-permute-start.9 = (bf16[144,1024]{1,0:T(8,128)(2,1)S(1)}, bf16[144,1024]{1,0:T(8,128)(2,1)S(1)}, u32[]{:S(2)}, u32[]{:S(2)}) collective-permute-start(bf16[144,1024]{1,0:T(8,128)(2,1)S(1)} %collective-permute-done.7.refs_0_), channel_id=1, source_target_pairs={{0,1},{1,0},{2,3},{3,2},{4,5},{5,4},{6,7},{7,6},{8,9},{9,8},{10,11... | collective-permute-start | bytes 884744 | tf_op jit(solution)/shard_map/ppermute | solution.py:294
  36.8 11.4 %collective-permute-start.10 = (bf16[144,1024]{1,0:T(8,128)(2,1)S(1)}, bf16[144,1024]{1,0:T(8,128)(2,1)S(1)}, u32[]{:S(2)}, u32[]{:S(2)}) collective-permute-start(bf16[144,1024]{1,0:T(8,128)(2,1)S(1)} %collective-permute-done.8.refs_1_), channel_id=1, source_target_pairs={{0,1},{1,0},{2,3},{3,2},{4,5},{5,4},{6,7},{7,6},{8,9},{9,8},{10,11... | collective-permute-start | bytes 884744 | tf_op jit(solution)/shard_map/ppermute | solution.py:294
  43.0 19.4 %collective-permute-start.39 = (bf16[128,1024]{1,0:T(8,128)(2,1)S(1)}, bf16[128,1024]{1,0:T(8,128)(2,1)S(1)}, u32[]{:S(2)}, u32[]{:S(2)}) collective-permute-start(bf16[128,1024]{1,0:T(8,128)(2,1)S(1)} %collective-permute-done.37.refs_3_), channel_id=1, source_target_pairs={{0,1},{1,0},{2,3},{3,2},{4,5},{5,4},{6,7},{7,6},{8,9},{9,8},{10,11... | collective-permute-start | bytes 786440 | tf_op jit(solution)/shard_map/ppermute | solution.py:294
  48.1 14.8 %collective-permute-start.40 = (bf16[128,1024]{1,0:T(8,128)(2,1)S(1)}, bf16[128,1024]{1,0:T(8,128)(2,1)S(1)}, u32[]{:S(2)}, u32[]{:S(2)}) collective-permute-start(bf16[128,1024]{1,0:T(8,128)(2,1)S(1)} %collective-permute-done.38.refs_4_), channel_id=1, source_target_pairs={{0,1},{1,0},{2,3},{3,2},{4,5},{5,4},{6,7},{7,6},{8,9},{9,8},{10,11... | collective-permute-start | bytes 786440 | tf_op jit(solution)/shard_map/ppermute | solution.py:294
  50.1 12.9 %collective-permute-start.42 = (bf16[128,1024]{1,0:T(8,128)(2,1)S(1)}, bf16[128,1024]{1,0:T(8,128)(2,1)S(1)}, u32[]{:S(2)}, u32[]{:S(2)}) collective-permute-start(bf16[128,1024]{1,0:T(8,128)(2,1)S(1)} %collective-permute-done.37.refs_3_), channel_id=1, source_target_pairs={{0,4},{1,5},{4,8},{5,9},{8,12},{9,13},{12,14},{13,15},{14,10},{15,... | collective-permute-start | bytes 786440 | tf_op jit(solution)/shard_map/ppermute | solution.py:288
  52.2 10.2 %collective-permute-start.17 = (bf16[80,1024]{1,0:T(8,128)(2,1)S(1)}, bf16[80,1024]{1,0:T(8,128)(2,1)S(1)}, u32[]{:S(2)}, u32[]{:S(2)}) collective-permute-start(bf16[80,1024]{1,0:T(8,128)(2,1)S(1)} %slice.16), channel_id=1, source_target_pairs={{0,4},{1,5},{4,8},{5,9},{8,12},{9,13},{12,14},{13,15},{14,10},{15,... | collective-permute-start | bytes 491528 | tf_op jit(solution)/shard_map/ppermute | solution.py:288
  79.8 12.8 %collective-permute-start.11 = (bf16[128,1024]{1,0:T(8,128)(2,1)S(1)}, bf16[128,1024]{1,0:T(8,128)(2,1)S(1)}, u32[]{:S(2)}, u32[]{:S(2)}) collective-permute-start(bf16[128,1024]{1,0:T(8,128)(2,1)S(1)} %get-tuple-element.104), channel_id=1, source_target_pairs={{0,1},{1,0},{2,3},{3,2},{4,5},{5,4},{6,7},{7,6},{8,9},{9,8},{10,11... | collective-permute-start | bytes 786440 | tf_op jit(solution)/shard_map/ppermute | solution.py:294
  80.8 13.3 %collective-permute-start.24 = (bf16[128,1024]{1,0:T(8,128)(2,1)S(1)}, bf16[128,1024]{1,0:T(8,128)(2,1)S(1)}, u32[]{:S(2)}, u32[]{:S(2)}) collective-permute-start(bf16[128,1024]{1,0:T(8,128)(2,1)S(1)} %get-tuple-element.117), channel_id=1, source_target_pairs={{0,2},{1,3},{4,0},{5,1},{8,4},{9,5},{12,8},{13,9},{14,12},{15,13},... | collective-permute-start | bytes 786440 | tf_op jit(solution)/shard_map/ppermute | solution.py:288
  83.7 10.4 %collective-permute-start.25 = (bf16[128,1024]{1,0:T(8,128)(2,1)S(1)}, bf16[128,1024]{1,0:T(8,128)(2,1)S(1)}, u32[]{:S(2)}, u32[]{:S(2)}) collective-permute-start(bf16[128,1024]{1,0:T(8,128)(2,1)S(1)} %get-tuple-element.118), channel_id=1, source_target_pairs={{0,4},{1,5},{4,8},{5,9},{8,12},{9,13},{12,14},{13,15},{14,10},{15,... | collective-permute-start | bytes 786440 | tf_op jit(solution)/shard_map/ppermute | solution.py:288
  94.5 12.3 %collective-permute-start.26 = (bf16[128,1024]{1,0:T(8,128)(2,1)S(1)}, bf16[128,1024]{1,0:T(8,128)(2,1)S(1)}, u32[]{:S(2)}, u32[]{:S(2)}) collective-permute-start(bf16[128,1024]{1,0:T(8,128)(2,1)S(1)} %get-tuple-element.119), channel_id=1, source_target_pairs={{0,2},{1,3},{4,0},{5,1},{8,4},{9,5},{12,8},{13,9},{14,12},{15,13},... | collective-permute-start | bytes 786440 | tf_op jit(solution)/shard_map/ppermute | solution.py:288
  95.1 12.3 %collective-permute-start.27 = (bf16[128,1024]{1,0:T(8,128)(2,1)S(1)}, bf16[128,1024]{1,0:T(8,128)(2,1)S(1)}, u32[]{:S(2)}, u32[]{:S(2)}) collective-permute-start(bf16[128,1024]{1,0:T(8,128)(2,1)S(1)} %get-tuple-element.120), channel_id=1, source_target_pairs={{0,4},{1,5},{4,8},{5,9},{8,12},{9,13},{12,14},{13,15},{14,10},{15,... | collective-permute-start | bytes 786440 | tf_op jit(solution)/shard_map/ppermute | solution.py:288
  102.1 10.3 %collective-permute-start.56 = (bf16[128,1024]{1,0:T(8,128)(2,1)S(1)}, bf16[128,1024]{1,0:T(8,128)(2,1)S(1)}, u32[]{:S(2)}, u32[]{:S(2)}) collective-permute-start(bf16[128,1024]{1,0:T(8,128)(2,1)S(1)} %get-tuple-element.157), channel_id=1, source_target_pairs={{0,2},{1,3},{4,0},{5,1},{8,4},{9,5},{12,8},{13,9},{14,12},{15,13},... | collective-permute-start | bytes 786440 | tf_op jit(solution)/shard_map/ppermute | solution.py:288
  102.6 10.4 %collective-permute-start.57 = (bf16[128,1024]{1,0:T(8,128)(2,1)S(1)}, bf16[128,1024]{1,0:T(8,128)(2,1)S(1)}, u32[]{:S(2)}, u32[]{:S(2)}) collective-permute-start(bf16[128,1024]{1,0:T(8,128)(2,1)S(1)} %get-tuple-element.158), channel_id=1, source_target_pairs={{0,4},{1,5},{4,8},{5,9},{8,12},{9,13},{12,14},{13,15},{14,10},{15,... | collective-permute-start | bytes 786440 | tf_op jit(solution)/shard_map/ppermute | solution.py:288
  106.8 10.8 %collective-permute-start.1 = (bf16[64,1024]{1,0:T(8,128)(2,1)S(1)}, bf16[64,1024]{1,0:T(8,128)(2,1)S(1)}, u32[]{:S(2)}, u32[]{:S(2)}) collective-permute-start(bf16[64,1024]{1,0:T(8,128)(2,1)S(1)} %get-tuple-element.96), channel_id=1, source_target_pairs={{0,1},{1,0},{2,3},{3,2},{4,5},{5,4},{6,7},{7,6},{8,9},{9,8},{10,11... | collective-permute-start | bytes 393224 | tf_op jit(solution)/shard_map/ppermute | solution.py:294
  107.7 14.3 %collective-permute-start.28 = (bf16[128,1024]{1,0:T(8,128)(2,1)S(1)}, bf16[128,1024]{1,0:T(8,128)(2,1)S(1)}, u32[]{:S(2)}, u32[]{:S(2)}) collective-permute-start(bf16[128,1024]{1,0:T(8,128)(2,1)S(1)} %get-tuple-element.121), channel_id=1, source_target_pairs={{0,4},{1,5},{4,8},{5,9},{8,12},{9,13},{12,14},{13,15},{14,10},{15,... | collective-permute-start | bytes 786440 | tf_op jit(solution)/shard_map/ppermute | solution.py:288
  109.3 12.8 %collective-permute-start.29 = (bf16[128,1024]{1,0:T(8,128)(2,1)S(1)}, bf16[128,1024]{1,0:T(8,128)(2,1)S(1)}, u32[]{:S(2)}, u32[]{:S(2)}) collective-permute-start(bf16[128,1024]{1,0:T(8,128)(2,1)S(1)} %get-tuple-element.122), channel_id=1, source_target_pairs={{0,2},{1,3},{4,0},{5,1},{8,4},{9,5},{12,8},{13,9},{14,12},{15,13},... | collective-permute-start | bytes 786440 | tf_op jit(solution)/shard_map/ppermute | solution.py:288
  113.3 10.2 %collective-permute-start.58 = (bf16[128,1024]{1,0:T(8,128)(2,1)S(1)}, bf16[128,1024]{1,0:T(8,128)(2,1)S(1)}, u32[]{:S(2)}, u32[]{:S(2)}) collective-permute-start(bf16[128,1024]{1,0:T(8,128)(2,1)S(1)} %get-tuple-element.159), channel_id=1, source_target_pairs={{0,4},{1,5},{4,8},{5,9},{8,12},{9,13},{12,14},{13,15},{14,10},{15,... | collective-permute-start | bytes 786440 | tf_op jit(solution)/shard_map/ppermute | solution.py:288
  (46 other events, 298.4 us)

commit v3 on v0

--- a/solution.py
+++ b/solution.py
@@ -1,7 +1,14 @@
+import functools
+
 import jax
 import jax.numpy as jnp
 from jax import lax
+from jax.experimental import pallas as pl
+from jax.experimental.pallas import tpu as pltpu
 from jax.sharding import PartitionSpec as P
+
+F32 = jnp.float32
+BF16 = jnp.bfloat16
 
 
 def contract_last(left, right):
@@ -16,7 +23,7 @@
     )
 
 
-def per_device(tokens, cotangent, routes, combine, w_gate, w_up, w_down):
+def by_all_to_all(tokens, cotangent, routes, combine, w_gate, w_up, w_down):
     tok_dev, width = tokens.shape
     top_count = routes.shape[1]
     experts = w_gate.shape[0] * lax.axis_size("expert")
@@ -84,6 +91,387 @@
     return (mixed, grad_tokens, grad_gate, grad_up, grad_down)
 
 
+VMEM = pltpu.VMEM
+LIMIT = 20 * 1024 * 1024
+
+
+def call(body, outs, operands, flops, smem=0, scratch=(), nbytes=None, far=False):
+    specs = [pl.BlockSpec(memory_space=pltpu.SMEM)] * smem
+    specs += [pl.BlockSpec(memory_space=pltpu.HBM if far else VMEM)] * (len(operands) - smem)
+    if far:
+        operands = [pltpu.with_memory_space_constraint(a, pltpu.HBM) for a in operands]
+    return pl.pallas_call(
+        body,
+        out_shape=list(outs),
+        in_specs=specs,
+        out_specs=[pl.BlockSpec(memory_space=VMEM)] * len(outs),
+        scratch_shapes=list(scratch),
+        compiler_params=pltpu.CompilerParams(vmem_limit_bytes=LIMIT),
+        cost_estimate=pl.CostEstimate(flops=0, bytes_accessed=1 << 20, transcendentals=0),
+    )(*operands)
+
+
+def picks(place, cap):
+    slots = lax.broadcasted_iota(jnp.int32, (cap, place.shape[1]), 0).astype(F32)
+    return jnp.where(slots == place, 1.0, 0.0)
+
+
+def joined(parts):
+    return parts[0] if len(parts) == 1 else jnp.concatenate(parts, axis=0)
+
+
+def payload_body(routes_hbm, combine_hbm, tokens_hbm, out_ref, routes_ref, combine_ref, sems):
+    top, tok = routes_ref.shape
+    head = 2 * top
+    body = pltpu.make_async_copy(tokens_hbm, out_ref.at[pl.ds(head, tok)], sems.at[0])
+    names = pltpu.make_async_copy(routes_hbm, routes_ref, sems.at[1])
+    shares = pltpu.make_async_copy(combine_hbm, combine_ref, sems.at[2])
+    names.start()
+    shares.start()
+    body.start()
+    out_ref[:head] = jnp.zeros((head, out_ref.shape[1]), BF16)
+    names.wait()
+    shares.wait()
+    exact = combine_ref[...]
+    high = exact.astype(BF16)
+    rest = exact - high.astype(F32)
+    middle = rest.astype(BF16)
+    low = (rest - middle.astype(F32)).astype(BF16)
+    blank = jnp.zeros((top, tok), F32)
+    named = jnp.concatenate([routes_ref[...].astype(F32), high.astype(F32)], axis=0)
+    out_ref[:head, :tok] = named.astype(BF16)
+    for i, term in enumerate((middle, low)):
+        padded = jnp.concatenate([blank, term.astype(F32)], axis=0)
+        out_ref[:head, (i + 1) * tok : (i + 2) * tok] = padded.astype(BF16)
+    body.wait()
+
+
+def stage_body(*refs):
+    *pairs, sems = refs
+    half = len(pairs) // 2
+    copies = [
+        pltpu.make_async_copy(pairs[i], pairs[half + i], sems.at[i]) for i in range(half)
+    ]
+    for copy in copies:
+        copy.start()
+    for copy in copies:
+        copy.wait()
+
+
+def forward_body(cap, top, kept, expert_ref, near, far, w_gate, w_up, w_down, *outs):
+    info_ref, rows_ref, slope_ref, act_ref, hidden_ref, keep_ref, give_ref = outs
+    me = expert_ref[0].astype(F32)
+    mate = expert_ref[1].astype(F32)
+    head = 2 * top
+    tok = info_ref.shape[1]
+    tall = head + tok
+    blocks = [(side, low) for side in (near, far) for low in range(0, side.shape[0], tall)]
+    names, terms = [], []
+    for side, low in blocks:
+        told = side[low : low + head, : 3 * tok].astype(F32)
+        names.append(told[:top, :tok])
+        told = told[top:]
+        terms.append(told[:, :tok] + (told[:, tok : 2 * tok] + told[:, 2 * tok :]))
+    masks, weights = [], []
+    for expert, which in [(me, i) for i in range(len(blocks))] + [(mate, i) for i in kept]:
+        hit = names[which] == expert
+        masks.append(jnp.sum(jnp.where(hit, 1.0, 0.0), axis=0, keepdims=True))
+        weights.append(jnp.sum(jnp.where(hit, terms[which], 0.0), axis=0, keepdims=True))
+    pad = jnp.zeros((8 - len(masks), tok), F32)
+    mask = jnp.concatenate(masks + [pad], axis=0)
+    before = lax.broadcasted_iota(jnp.int32, (tok, tok), 0) < lax.broadcasted_iota(
+        jnp.int32, (tok, tok), 1
+    )
+    rank = jnp.dot(
+        mask.astype(BF16), jnp.where(before, 1.0, 0.0).astype(BF16), preferred_element_type=F32
+    )
+    place = jnp.where(mask > 0.5, rank, -1.0)
+    info_ref[0:8] = place
+    info_ref[8:16] = jnp.concatenate(weights + [pad], axis=0)
+    share = []
+    for i, (side, low) in enumerate(blocks):
+        pick = picks(place[i : i + 1], cap)
+        share.append(jnp.sum(pick * weights[i], axis=1, keepdims=True))
+        taken = jnp.dot(
+            pick.astype(BF16), side[low + head : low + tall], preferred_element_type=F32
+        )
+        rows_ref[i * cap : (i + 1) * cap] = taken.astype(BF16)
+    rows = rows_ref[...]
+    gate = jnp.dot(rows, w_gate[...], preferred_element_type=F32)
+    up = jnp.dot(rows, w_up[...], preferred_element_type=F32)
+    sig = jax.nn.sigmoid(gate)
+    act = gate * sig
+    hidden = (act * up).astype(BF16)
+    hidden_ref[...] = hidden
+    act_ref[...] = act
+    slope_ref[...] = up * sig * (1.0 + gate * (1.0 - sig))
+    produced = contract_last(hidden, w_down[...]).astype(BF16).astype(F32)
+    split(kept, cap, (jnp.concatenate(share, axis=0) * produced).astype(BF16), keep_ref, give_ref)
+
+
+def split(kept, cap, rows, keep_ref, give_ref):
+    cut = rows.shape[0] // 2
+    first, second = (keep_ref, give_ref) if kept[0] == 0 else (give_ref, keep_ref)
+    first[...] = rows[:cut]
+    second[...] = rows[cut:]
+
+
+def backward_body(cap, kept, info_ref, slope, act, near, far, w_gate, w_up, w_down, *outs):
+    rows_ref, dgate_ref, dup_ref, keep_ref, give_ref = outs
+    tok = info_ref.shape[1]
+    blocks = [(side, low) for side in (near, far) for low in range(0, side.shape[0], tok)]
+    for i, (side, low) in enumerate(blocks):
+        pick = picks(info_ref[i : i + 1], cap)
+        share = jnp.sum(pick * info_ref[8 + i : 9 + i], axis=1, keepdims=True)
+        taken = jnp.dot(pick.astype(BF16), side[low : low + tok], preferred_element_type=F32)
+        rows_ref[i * cap : (i + 1) * cap] = (share * taken).astype(BF16)
+    dhidden = jnp.dot(rows_ref[...], w_down[...], preferred_element_type=F32)
+    dgate = (dhidden * slope[...]).astype(BF16)
+    dup = (dhidden * act[...]).astype(BF16)
+    dgate_ref[...] = dgate
+    dup_ref[...] = dup
+    back = contract_last(dgate, w_gate[...]) + contract_last(dup, w_up[...])
+    split(kept, cap, back.astype(BF16), keep_ref, give_ref)
+
+
+def return_body(cap, kept, count, info_ref, keep, give, *refs):
+    arrived, outs = refs[: len(refs) - count], refs[len(refs) - count :]
+    tok = info_ref.shape[1]
+    sums = []
+    for j in reversed(range(len(kept))):
+        i = kept[j]
+        mate = 2 * len(kept) + j
+        both = jnp.concatenate(
+            [picks(info_ref[i : i + 1], cap), picks(info_ref[mate : mate + 1], cap)], axis=0
+        ).astype(BF16)
+        part = slice(j * cap, (j + 1) * cap)
+        sums.append(contract_first(both, jnp.concatenate([keep[part], give[part]], axis=0)))
+    for ref in arrived:
+        for j in range(ref.shape[0] // tok):
+            sums[j] = sums[j] + ref[j * tok : (j + 1) * tok].astype(F32)
+    for out, total in zip(outs, sums if count > 1 else [joined(sums)]):
+        out[...] = total.astype(BF16)
+
+
+def weights_body(steps, cols, *refs):
+    rows = refs[:steps]
+    grads = refs[steps : 2 * steps]
+    out = refs[2 * steps]
+    right = jnp.concatenate([g[...] for g in grads], axis=0)
+    for low in range(0, out.shape[0], cols):
+        left = jnp.concatenate([r[:, low : low + cols] for r in rows], axis=0)
+        out[low : low + cols] = contract_first(left, right).astype(BF16)
+
+
+def by_ring(tokens, cotangent, routes, combine, w_gate, w_up, w_down):
+    tok, width = tokens.shape
+    top = routes.shape[1]
+    n = lax.axis_size("expert")
+    cap = (tok * top + n - 1) // n
+    units = w_gate.shape[2]
+    gate_w, up_w, down_w = w_gate[0], w_up[0], w_down[0]
+    pairs = n // 2
+    reach = pairs // 2
+    walk = [2 * i for i in range(reach)] + [2 * i + 1 for i in reversed(range(reach))]
+    straight = [
+        (2 * walk[i] + core, 2 * walk[(i + 1 - 2 * core) % pairs] + core)
+        for i in range(pairs)
+        for core in range(2)
+    ]
+    crossing = [
+        (2 * walk[i] + core, 2 * walk[(i - 1 + 2 * core) % pairs] + 1 - core)
+        for i in range(pairs)
+        for core in range(2)
+    ]
+    crossing_back = [(a, b ^ 1) for a, b in straight]
+
+    def hop(value, what, moves=straight):
+        with jax.named_scope(what):
+            return lax.ppermute(value, "expert", moves)
+
+    def swap(value, what):
+        return hop(value, what, [(i, i ^ 1) for i in range(n)])
+
+    def after(value, *others):
+        return lax.optimization_barrier((value, *others))[0] if others else value
+
+    def land(values, *before):
+        return list(lax.optimization_barrier((*values, *before))[: len(values)])
+
+    def struct(shape, dtype):
+        return jax.ShapeDtypeStruct(shape, dtype)
+
+    here = lax.axis_index("expert").astype(jnp.int32)
+    expert = jnp.stack([here, here ^ 1])
+    head = 2 * top
+
+    def blocks_of(step):
+        return (4, (2, 3)) if 0 < step < reach else (2, (0,))
+
+    def run_forward(step):
+        count, kept = blocks_of(step)
+        m = count * cap
+        return call(
+            functools.partial(forward_body, cap, top, kept),
+            [
+                struct((16, tok), F32),
+                struct((m, width), BF16),
+                struct((m, units), F32),
+                struct((m, units), F32),
+                struct((m, units), BF16),
+                struct((m // 2, width), BF16),
+                struct((m // 2, width), BF16),
+            ],
+            [expert, token_near[step], token_far[step], gate_w, up_w, down_w],
+            0,
+            smem=1,
+        )
+
+    def run_backward(step):
+        count, kept = blocks_of(step)
+        m = count * cap
+        info, _, slope, act = forward[step][:4]
+        return call(
+            functools.partial(backward_body, cap, kept),
+            [
+                struct((m, width), BF16),
+                struct((m, units), BF16),
+                struct((m, units), BF16),
+                struct((m // 2, width), BF16),
+                struct((m // 2, width), BF16),
+            ],
+            [info, slope, act, cot_near[step], cot_far[step], gate_w, up_w, down_w],
+            0,
+        )
+
+    payload = call(
+        payload_body,
+        [struct((head + tok, width), BF16)],
+        [routes.T, combine.T, tokens],
+        0,
+        scratch=[VMEM((top, tok), jnp.int32), VMEM((top, tok), F32), pltpu.SemaphoreType.DMA((3,))],
+        far=True,
+    )[0]
+    staged = after((gate_w, up_w, down_w), payload)
+    gate_w, up_w, down_w = call(
+        stage_body,
+        [struct(w.shape, BF16) for w in staged],
+        staged,
+        0,
+        scratch=[pltpu.SemaphoreType.DMA((3,))],
+        far=True,
+    )
+
+    def depart(block, what):
+        return [hop(block, what + "_1"), hop(block, what + "_1_crossing", crossing)]
+
+    def onward(near, step, what):
+        if step == reach:
+            near = near[: near.shape[0] // 2]
+        return [hop(near, f"{what}_{step}")]
+
+    cot = after(cotangent, payload)
+    token_near, cot_near = [payload], [cot]
+    token_fly, cot_fly = depart(payload, "tokens"), depart(cot, "cotangent")
+    token_far, cot_far = [swap(payload, "tokens_0_swap")], [swap(cot, "cotangent_0_swap")]
+    forward, backward = [], []
+    for step in range(1, reach + 1):
+        before = [b[1] for b in backward[-1:]] or [gate_w]
+        *arrived, token_near[-1] = land([*token_fly, token_near[-1]], *before)
+        token_near.append(joined(arrived))
+        if step < reach:
+            token_fly = onward(token_near[-1], step + 1, "tokens")
+        token_far.append(swap(token_near[-1], f"tokens_{step}_swap"))
+        forward.append(run_forward(step - 1))
+        if step == reach:
+            forward.append(run_forward(reach))
+        before = [f[5] for f in forward[step - 1 :]]
+        *arrived, cot_near[-1] = land([*cot_fly, cot_near[-1]], *before)
+        cot_near.append(joined(arrived))
+        if step < reach:
+            cot_fly = onward(cot_near[-1], step + 1, "cotangent")
+        cot_far.append(swap(cot_near[-1], f"cotangent_{step}_swap"))
+        backward.append(run_backward(step - 1))
+    backward.append(run_backward(reach))
+
+    def back_from(step, kept, given, values):
+        outs = {0: (tok,), 1: (tok, tok), reach: (tok,)}.get(step, (2 * tok,))
+        return call(
+            functools.partial(return_body, cap, blocks_of(step)[1], len(outs)),
+            [struct((rows, width), BF16) for rows in outs],
+            [forward[step][0], kept[step], given[step], *values],
+            0,
+        )
+
+    def send_back(sums, step, what):
+        if step == 1:
+            return [hop(sums[0], what + "_1"), hop(sums[1], what + "_1_crossing", crossing_back)]
+        return [hop(sums[0], f"{what}_{step}")]
+
+    def weight_grad(lefts, rights):
+        return call(
+            functools.partial(weights_body, len(lefts), 256),
+            [struct((width, units), BF16)],
+            [*lefts, *rights],
+            0,
+        )[0]
+
+    mixed_kept = [f[5] for f in forward]
+    mixed_given = [swap(f[6], f"mixed_{i}_swap") for i, f in enumerate(forward)]
+    grad_kept = [b[3] for b in backward]
+    grad_given = [swap(b[4], f"grad_{i}_swap") for i, b in enumerate(backward)]
+
+    token_rows = [f[1] for f in forward]
+    jobs = [
+        (token_rows, [b[1] for b in backward]),
+        (token_rows, [b[2] for b in backward]),
+        ([b[0] for b in backward], [f[4] for f in forward]),
+    ]
+    grads = []
+
+    def some_job():
+        if len(grads) < len(jobs):
+            grads.append(weight_grad(*jobs[len(grads)]))
+            return grads[-1:]
+        return []
+
+    left = back_from(reach, mixed_kept, mixed_given, ())
+    mixed_fly = send_back(left, reach, "mixed")
+    left = back_from(reach, grad_kept, grad_given, ())
+    grad_fly = send_back(left, reach, "grad")
+    for step in range(reach - 1, 0, -1):
+        arrived = land(mixed_fly, *left, *(some_job() if step < reach - 1 else []))
+        left = back_from(step, mixed_kept, mixed_given, arrived)
+        mixed_fly = send_back(left, step, "mixed")
+        arrived = land(grad_fly, *left, *(some_job() if step < reach - 1 else []))
+        left = back_from(step, grad_kept, grad_given, arrived)
+        grad_fly = send_back(left, step, "grad")
+    while len(grads) < len(jobs):
+        some_job()
+    mixed = back_from(0, mixed_kept, mixed_given, land(mixed_fly, *left, *grads))[0]
+    grad_tokens = back_from(0, grad_kept, grad_given, land(grad_fly, mixed))[0]
+    return (mixed, grad_tokens, *[g[None] for g in grads])
+
+
+def per_device(tokens, cotangent, routes, combine, w_gate, w_up, w_down):
+    n = lax.axis_size("expert")
+    tok, width = tokens.shape
+    top = routes.shape[1]
+    ring = (
+        lax.axis_size("dp") == 1
+        and w_gate.shape[0] == 1
+        and n % 4 == 0
+        and n >= 8
+        and n <= 2 * top
+        and tok % 128 == 0
+        and top % 8 == 0
+        and width >= 3 * tok
+        and (tok * top) % (16 * n) == 0
+    )
+    plan = by_ring if ring else by_all_to_all
+    return plan(tokens, cotangent, routes, combine, w_gate, w_up, w_down)
+
+
 def solution(mesh):
     placed = (
         P(("groups", "expert", "dp"), None),

time: 254 us -> 99.3 us (0.39)
  the two profiles are of different devices: /device:TPU:11 before, /device:TPU:0 now
where the time goes in v3:
time: 99.3 us; the launch traced here: 98.8 us
  starting transfers between devices  33.7 us (34%)
  waiting for transfers between devices  32.2 us (32%)
  Pallas kernels  30.1 us (30%)
  local copies, waits for them, and re-layouts  2.02 us (2%)
    ppermute x40, starting transfers between devices, hop(): return lax.ppermute(value, 'expert', moves)  33.7 us
    ppermute x40, waiting for transfers between devices, hop(): return lax.ppermute(value, 'expert', moves)  32.2 us
    pallas_call x25, Pallas kernels, call(): pl.pallas_call(body, out_shape=list(outs), in_specs=specs, out_specs=[pl....  30.1 us
  transfers between devices with their start and end apart: 40, of which 21 were waited for; matrix products, arithmetic and copies ran while one was open for 2% of the time, Pallas kernels for 28%

profile of v3, /device:TPU:0, one launch (start us, length us, event | category | flops | bytes accessed | tf_op | source)
XLA Modules:
  0.0 98.8 jit_solution(8340668967883128360)
XLA Ops:
  1.6 2.4 %collective-permute-start.1 = (bf16[144,1024]{1,0:T(8,128)(2,1)S(1)}, bf16[144,1024]{1,0:T(8,128)(2,1)S(1)}, u32[]{:S(2)}, u32[]{:S(2)}) collective-permute-start(bf16[144,1024]{1,0:T(8,128)(2,1)S(1)} %shard_map.110.near), channel_id=1, source_target_pairs={{0,3},{1,4},{4,1},{5,8},{8,5},{9,12},{12,9},{13,14},{14,13},{15,10... | collective-permute-start | bytes 884744 | tf_op jit(solution)/shard_map/tokens_1_crossing/ppermute | solution.py:290
  8.3 3.1 %collective-permute-done.1 = bf16[144,1024]{1,0:T(8,128)(2,1)S(1)} collective-permute-done((bf16[144,1024]{1,0:T(8,128)(2,1)S(1)}, bf16[144,1024]{1,0:T(8,128)(2,1)S(1)}, u32[]{:S(2)}, u32[]{:S(2)}) %collective-permute-start.1) | collective-permute-done | bytes 294944 | tf_op jit(solution)/shard_map/tokens_1_crossing/ppermute | solution.py:290
  11.4 2.6 %collective-permute-done = bf16[144,1024]{1,0:T(8,128)(2,1)S(1)} collective-permute-done((bf16[144,1024]{1,0:T(8,128)(2,1)S(1)}, bf16[144,1024]{1,0:T(8,128)(2,1)S(1)}, u32[]{:S(2)}, u32[]{:S(2)}) %collective-permute-start) | collective-permute-done | bytes 294944 | tf_op jit(solution)/shard_map/tokens_1/ppermute | solution.py:290
  19.3 2.4 %collective-permute-start.11 = (bf16[256,1024]{1,0:T(8,128)(2,1)S(1)}, bf16[256,1024]{1,0:T(8,128)(2,1)S(1)}, u32[]{:S(2)}, u32[]{:S(2)}) collective-permute-start(bf16[256,1024]{1,0:T(8,128)(2,1)S(1)} %constant_dynamic-update-slice_fusion.2.near), channel_id=1, source_target_pairs={{0,4},{1,3},{4,8},{5,1},{8,12},{9,5},{12,14},{13,9},{14,10},{15,13... | collective-permute-start | bytes 1572872 | tf_op jit(solution)/shard_map/cotangent_2/ppermute | solution.py:290
  21.8 2.0 %shard_map.113 = (bf16[128,1024]{1,0:T(8,128)(2,1)S(1)}, bf16[128,384]{1,0:T(8,128)(2,1)S(1)}, bf16[128,384]{1,0:T(8,128)(2,1)S(1)}, bf16[64,1024]{1,0:T(8,128)(2,1)S(1)}, bf16[64,1024]{1,0:T(8,128)(2,1)S(1)}) custom-call(f32[16,128]{1,0:T(8,128)S(1)} %get-tuple-element.111.info_ref, f32[128,384]{1,0:T(8,128)S(1)} %get-tuple-element.116.slope, ...), custom_call_target="tpu_custom_call" | custom-call | bytes 1048576 | tf_op jit(solution)/shard_map/pallas_call | solution.py:103
  24.1 2.0 %collective-permute-start.10 = (bf16[288,1024]{1,0:T(8,128)(2,1)}, bf16[288,1024]{1,0:T(8,128)(2,1)S(1)}, u32[]{:S(2)}, u32[]{:S(2)}) collective-permute-start(bf16[288,1024]{1,0:T(8,128)(2,1)} %collective-permute-done.4.near), channel_id=1, source_target_pairs={{0,4},{1,3},{4,8},{5,1},{8,12},{9,5},{12,14},{13,9},{14,10},{15,13... | collective-permute-start | bytes 1769480 | tf_op jit(solution)/shard_map/tokens_3/ppermute | solution.py:290
  26.6 2.0 %shard_map.114 = (f32[16,128]{1,0:T(8,128)S(1)}, bf16[256,1024]{1,0:T(8,128)(2,1)S(1)}, f32[256,384]{1,0:T(8,128)S(1)}, f32[256,384]{1,0:T(8,128)S(1)}, bf16[256...) custom-call(s32[2]{0:T(128)S(1)} %pad_add_fusion.expert_ref, ...), custom_call_target="tpu_custom_call" | custom-call | bytes 1048576 | tf_op jit(solution)/shard_map/pallas_call | solution.py:103
  29.6 2.0 %collective-permute-start.16 = (bf16[256,1024]{1,0:T(8,128)(2,1)S(1)}, bf16[256,1024]{1,0:T(8,128)(2,1)S(1)}, u32[]{:S(2)}, u32[]{:S(2)}) collective-permute-start(bf16[256,1024]{1,0:T(8,128)(2,1)S(1)} %collective-permute-done.11.near), channel_id=1, source_target_pairs={{0,4},{1,3},{4,8},{5,1},{8,12},{9,5},{12,14},{13,9},{14,10},{15,13... | collective-permute-start | bytes 1572872 | tf_op jit(solution)/shard_map/cotangent_3/ppermute | solution.py:290
  32.9 3.1 %collective-permute-done.10.near = bf16[288,1024]{1,0:T(8,128)(2,1)S(1)} collective-permute-done((bf16[288,1024]{1,0:T(8,128)(2,1)}, bf16[288,1024]{1,0:T(8,128)(2,1)S(1)}, u32[]{:S(2)}, u32[]{:S(2)}) %collective-permute-start.10) | collective-permute-done | bytes 589856 | tf_op jit(solution)/shard_map/tokens_3/ppermute | solution.py:290
  36.0 2.0 %collective-permute-start.15 = (bf16[144,1024]{1,0:T(8,128)(2,1)S(1)}, bf16[144,1024]{1,0:T(8,128)(2,1)S(1)}, u32[]{:S(2)}, u32[]{:S(2)}) collective-permute-start(bf16[144,1024]{1,0:T(8,128)(2,1)S(1)} %slice.6), channel_id=1, source_target_pairs={{0,4},{1,3},{4,8},{5,1},{8,12},{9,5},{12,14},{13,9},{14,10},{15,13... | collective-permute-start | bytes 884744 | tf_op jit(solution)/shard_map/tokens_4/ppermute | solution.py:290
  38.0 2.5 %shard_map.116 = (f32[16,128]{1,0:T(8,128)S(1)}, bf16[256,1024]{1,0:T(8,128)(2,1)S(1)}, f32[256,384]{1,0:T(8,128)S(1)}, f32[256,384]{1,0:T(8,128)S(1)}, bf16[256...) custom-call(s32[2]{0:T(128)S(1)} %pad_add_fusion.expert_ref, ...), custom_call_target="tpu_custom_call" | custom-call | bytes 1048576 | tf_op jit(solution)/shard_map/pallas_call | solution.py:103
  42.9 1.9 %collective-permute-done.15.near = bf16[144,1024]{1,0:T(8,128)(2,1)S(1)} collective-permute-done((bf16[144,1024]{1,0:T(8,128)(2,1)S(1)}, bf16[144,1024]{1,0:T(8,128)(2,1)S(1)}, u32[]{:S(2)}, u32[]{:S(2)}) %collective-permute-start.15) | collective-permute-done | bytes 294944 | tf_op jit(solution)/shard_map/tokens_4/ppermute | solution.py:290
  45.1 1.8 %collective-permute-start.23 = (bf16[128,1024]{1,0:T(8,128)(2,1)S(1)}, bf16[128,1024]{1,0:T(8,128)(2,1)S(1)}, u32[]{:S(2)}, u32[]{:S(2)}) collective-permute-start(bf16[128,1024]{1,0:T(8,128)(2,1)S(1)} %slice.7), channel_id=1, source_target_pairs={{0,4},{1,3},{4,8},{5,1},{8,12},{9,5},{12,14},{13,9},{14,10},{15,13... | collective-permute-start | bytes 786440 | tf_op jit(solution)/shard_map/cotangent_4/ppermute | solution.py:290
  48.5 2.0 %shard_map.118 = (f32[16,128]{1,0:T(8,128)S(1)}, bf16[256,1024]{1,0:T(8,128)(2,1)S(1)}, f32[256,384]{1,0:T(8,128)S(1)}, f32[256,384]{1,0:T(8,128)S(1)}, bf16[256...) custom-call(s32[2]{0:T(128)S(1)} %pad_add_fusion.expert_ref, ...), custom_call_target="tpu_custom_call" | custom-call | bytes 1048576 | tf_op jit(solution)/shard_map/pallas_call | solution.py:103
  54.5 1.8 %collective-permute-start.22 = (bf16[128,1024]{1,0:T(8,128)(2,1)S(1)}, bf16[128,1024]{1,0:T(8,128)(2,1)S(1)}, u32[]{:S(2)}, u32[]{:S(2)}) collective-permute-start(bf16[128,1024]{1,0:T(8,128)(2,1)S(1)} %shard_map.120), channel_id=1, source_target_pairs={{0,4},{1,3},{4,8},{5,1},{8,12},{9,5},{12,14},{13,9},{14,10},{15,13... | collective-permute-start | bytes 786440 | tf_op jit(solution)/shard_map/mixed_4/ppermute | solution.py:290
  56.6 1.8 %collective-permute-start.29 = (bf16[128,1024]{1,0:T(8,128)(2,1)S(1)}, bf16[128,1024]{1,0:T(8,128)(2,1)S(1)}, u32[]{:S(2)}, u32[]{:S(2)}) collective-permute-start(bf16[128,1024]{1,0:T(8,128)(2,1)S(1)} %shard_map.122), channel_id=1, source_target_pairs={{0,4},{1,3},{4,8},{5,1},{8,12},{9,5},{12,14},{13,9},{14,10},{15,13... | collective-permute-start | bytes 786440 | tf_op jit(solution)/shard_map/grad_4/ppermute | solution.py:290
  66.4 2.2 %shard_map.126 = bf16[1024,384]{1,0:T(8,128)(2,1)} custom-call(bf16[128,1024]{1,0:T(8,128)(2,1)S(1)} %get-tuple-element.163.refs_0_, bf16[256,1024]{1,0:T(8,128)(2,1)S(1)} %get-tuple-element.164.refs_1_, bf16[256,1024]{1,0:T(8,128)(2,1)S(1)} %get-tuple-element.165.refs_2_, bf16[256,1024]{1,0:T(8,128)(2,1)S(1)} %get-tuple-element.166.refs_3_, ...), custom_call_target="tpu_custom_call" | custom-call | bytes 1048576 | tf_op jit(solution)/shard_map/pallas_call | solution.py:103
  68.6 1.9 %collective-permute-done.26.refs_0_ = bf16[256,1024]{1,0:T(8,128)(2,1)S(1)} collective-permute-done((bf16[256,1024]{1,0:T(8,128)(2,1)S(1)}, bf16[256,1024]{1,0:T(8,128)(2,1)S(1)}, u32[]{:S(2)}, u32[]{:S(2)}) %collective-permute-start.26) | collective-permute-done | bytes 524320 | tf_op jit(solution)/shard_map/mixed_3/ppermute | solution.py:290
  72.7 2.2 %shard_map.128 = bf16[1024,384]{1,0:T(8,128)(2,1)} custom-call(bf16[128,1024]{1,0:T(8,128)(2,1)S(1)} %get-tuple-element.163.refs_0_, bf16[256,1024]{1,0:T(8,128)(2,1)S(1)} %get-tuple-element.164.refs_1_, bf16[256,1024]{1,0:T(8,128)(2,1)S(1)} %get-tuple-element.165.refs_2_, bf16[256,1024]{1,0:T(8,128)(2,1)S(1)} %get-tuple-element.166.refs_3_, ...), custom_call_target="tpu_custom_call" | custom-call | bytes 1048576 | tf_op jit(solution)/shard_map/pallas_call | solution.py:103
  78.8 2.2 %shard_map.130 = bf16[1024,384]{1,0:T(8,128)(2,1)} custom-call(bf16[128,1024]{1,0:T(8,128)(2,1)S(1)} %get-tuple-element.179.refs_0_, bf16[256,1024]{1,0:T(8,128)(2,1)S(1)} %get-tuple-element.180.refs_1_, bf16[256,1024]{1,0:T(8,128)(2,1)S(1)} %get-tuple-element.181.refs_2_, bf16[256,1024]{1,0:T(8,128)(2,1)S(1)} %get-tuple-element.182.refs_3_, ...), custom_call_target="tpu_custom_call" | custom-call | bytes 1048576 | tf_op jit(solution)/shard_map/pallas_call | solution.py:103
  83.9 3.5 %collective-permute-done.36.refs_0_ = bf16[256,1024]{1,0:T(8,128)(2,1)S(1)} collective-permute-done((bf16[256,1024]{1,0:T(8,128)(2,1)S(1)}, bf16[256,1024]{1,0:T(8,128)(2,1)S(1)}, u32[]{:S(2)}, u32[]{:S(2)}) %collective-permute-start.36) | collective-permute-done | bytes 524320 | tf_op jit(solution)/shard_map/grad_2/ppermute | solution.py:290
  90.2 2.1 %collective-permute-done.34.refs_1_ = bf16[128,1024]{1,0:T(8,128)(2,1)S(1)} collective-permute-done((bf16[128,1024]{1,0:T(8,128)(2,1)S(1)}, bf16[128,1024]{1,0:T(8,128)(2,1)S(1)}, u32[]{:S(2)}, u32[]{:S(2)}) %collective-permute-start.34) | collective-permute-done | bytes 262176 | tf_op jit(solution)/shard_map/mixed_1_crossing/ppermute | solution.py:290
  93.2 2.6 %collective-permute-done.38.refs_0_ = bf16[128,1024]{1,0:T(8,128)(2,1)S(1)} collective-permute-done((bf16[128,1024]{1,0:T(8,128)(2,1)S(1)}, bf16[128,1024]{1,0:T(8,128)(2,1)S(1)}, u32[]{:S(2)}, u32[]{:S(2)}) %collective-permute-start.38) | collective-permute-done | bytes 262176 | tf_op jit(solution)/shard_map/grad_1/ppermute | solution.py:290
  95.8 2.1 %collective-permute-done.39.refs_1_ = bf16[128,1024]{1,0:T(8,128)(2,1)S(1)} collective-permute-done((bf16[128,1024]{1,0:T(8,128)(2,1)S(1)}, bf16[128,1024]{1,0:T(8,128)(2,1)S(1)}, u32[]{:S(2)}, u32[]{:S(2)}) %collective-permute-start.39) | collective-permute-done | bytes 262176 | tf_op jit(solution)/shard_map/grad_1_crossing/ppermute | solution.py:290
  (88 shorter events, 44.0 us)
Async XLA Ops:
  1.6 9.8 %collective-permute-start.1 = (bf16[144,1024]{1,0:T(8,128)(2,1)S(1)}, bf16[144,1024]{1,0:T(8,128)(2,1)S(1)}, u32[]{:S(2)}, u32[]{:S(2)}) collective-permute-start(bf16[144,1024]{1,0:T(8,128)(2,1)S(1)} %shard_map.110.near), channel_id=1, source_target_pairs={{0,3},{1,4},{4,1},{5,8},{8,5},{9,12},{12,9},{13,14},{14,13},{15,10... | collective-permute-start | bytes 884744 | tf_op jit(solution)/shard_map/tokens_1_crossing/ppermute | solution.py:290
  4.1 9.9 %collective-permute-start = (bf16[144,1024]{1,0:T(8,128)(2,1)S(1)}, bf16[144,1024]{1,0:T(8,128)(2,1)S(1)}, u32[]{:S(2)}, u32[]{:S(2)}) collective-permute-start(bf16[144,1024]{1,0:T(8,128)(2,1)S(1)} %shard_map.110.near), channel_id=1, source_target_pairs={{0,4},{1,3},{4,8},{5,1},{8,12},{9,5},{12,14},{13,9},{14,10},{15,13... | collective-permute-start | bytes 884744 | tf_op jit(solution)/shard_map/tokens_1/ppermute | solution.py:290
  4.8 12.3 %collective-permute-start.6 = (bf16[128,1024]{1,0:T(8,128)(2,1)}, bf16[128,1024]{1,0:T(8,128)(2,1)}, u32[]{:S(2)}, u32[]{:S(2)}) collective-permute-start(bf16[128,1024]{1,0:T(8,128)(2,1)} %near), channel_id=1, source_target_pairs={{0,3},{1,4},{4,1},{5,8},{8,5},{9,12},{12,9},{13,14},{14,13},{15,10... | collective-permute-start | bytes 786440 | tf_op jit(solution)/shard_map/cotangent_1_crossing/ppermute | solution.py:290
  6.1 11.3 %collective-permute-start.5 = (bf16[128,1024]{1,0:T(8,128)(2,1)}, bf16[128,1024]{1,0:T(8,128)(2,1)}, u32[]{:S(2)}, u32[]{:S(2)}) collective-permute-start(bf16[128,1024]{1,0:T(8,128)(2,1)} %near), channel_id=1, source_target_pairs={{0,4},{1,3},{4,8},{5,1},{8,12},{9,5},{12,14},{13,9},{14,10},{15,13... | collective-permute-start | bytes 786440 | tf_op jit(solution)/shard_map/cotangent_1/ppermute | solution.py:290
  6.5 8.3 %collective-permute-start.2 = (bf16[144,1024]{1,0:T(8,128)(2,1)S(1)}, bf16[144,1024]{1,0:T(8,128)(2,1)S(1)}, u32[]{:S(2)}, u32[]{:S(2)}) collective-permute-start(bf16[144,1024]{1,0:T(8,128)(2,1)S(1)} %shard_map.110.near), channel_id=1, source_target_pairs={{0,1},{1,0},{2,3},{3,2},{4,5},{5,4},{6,7},{7,6},{8,9},{9,8},{10,11... | collective-permute-start | bytes 884744 | tf_op jit(solution)/shard_map/tokens_0_swap/ppermute | solution.py:290
  14.1 10.0 %collective-permute-start.4 = (bf16[288,1024]{1,0:T(8,128)(2,1)S(1)}, bf16[288,1024]{1,0:T(8,128)(2,1)}, u32[]{:S(2)}, u32[]{:S(2)}) collective-permute-start(bf16[288,1024]{1,0:T(8,128)(2,1)S(1)} %constant_dynamic-update-slice_fusion.near), channel_id=1, source_target_pairs={{0,4},{1,3},{4,8},{5,1},{8,12},{9,5},{12,14},{13,9},{14,10},{15,13... | collective-permute-start | bytes 1769480 | tf_op jit(solution)/shard_map/tokens_2/ppermute | solution.py:290
  14.8 11.8 %collective-permute-start.8 = (bf16[288,1024]{1,0:T(8,128)(2,1)S(1)}, bf16[288,1024]{1,0:T(8,128)(2,1)S(1)}, u32[]{:S(2)}, u32[]{:S(2)}) collective-permute-start(bf16[288,1024]{1,0:T(8,128)(2,1)S(1)} %constant_dynamic-update-slice_fusion.near), channel_id=1, source_target_pairs={{0,1},{1,0},{2,3},{3,2},{4,5},{5,4},{6,7},{7,6},{8,9},{9,8},{10,11... | collective-permute-start | bytes 1769480 | tf_op jit(solution)/shard_map/tokens_1_swap/ppermute | solution.py:290
  19.3 10.3 %collective-permute-start.11 = (bf16[256,1024]{1,0:T(8,128)(2,1)S(1)}, bf16[256,1024]{1,0:T(8,128)(2,1)S(1)}, u32[]{:S(2)}, u32[]{:S(2)}) collective-permute-start(bf16[256,1024]{1,0:T(8,128)(2,1)S(1)} %constant_dynamic-update-slice_fusion.2.near), channel_id=1, source_target_pairs={{0,4},{1,3},{4,8},{5,1},{8,12},{9,5},{12,14},{13,9},{14,10},{15,13... | collective-permute-start | bytes 1572872 | tf_op jit(solution)/shard_map/cotangent_2/ppermute | solution.py:290
  24.1 11.8 %collective-permute-start.10 = (bf16[288,1024]{1,0:T(8,128)(2,1)}, bf16[288,1024]{1,0:T(8,128)(2,1)S(1)}, u32[]{:S(2)}, u32[]{:S(2)}) collective-permute-start(bf16[288,1024]{1,0:T(8,128)(2,1)} %collective-permute-done.4.near), channel_id=1, source_target_pairs={{0,4},{1,3},{4,8},{5,1},{8,12},{9,5},{12,14},{13,9},{14,10},{15,13... | collective-permute-start | bytes 1769480 | tf_op jit(solution)/shard_map/tokens_3/ppermute | solution.py:290
  26.1 11.9 %collective-permute-start.13 = (bf16[288,1024]{1,0:T(8,128)(2,1)}, bf16[288,1024]{1,0:T(8,128)(2,1)S(1)}, u32[]{:S(2)}, u32[]{:S(2)}) collective-permute-start(bf16[288,1024]{1,0:T(8,128)(2,1)} %collective-permute-done.4.near), channel_id=1, source_target_pairs={{0,1},{1,0},{2,3},{3,2},{4,5},{5,4},{6,7},{7,6},{8,9},{9,8},{10,11... | collective-permute-start | bytes 1769480 | tf_op jit(solution)/shard_map/tokens_2_swap/ppermute | solution.py:290
  29.6 11.9 %collective-permute-start.16 = (bf16[256,1024]{1,0:T(8,128)(2,1)S(1)}, bf16[256,1024]{1,0:T(8,128)(2,1)S(1)}, u32[]{:S(2)}, u32[]{:S(2)}) collective-permute-start(bf16[256,1024]{1,0:T(8,128)(2,1)S(1)} %collective-permute-done.11.near), channel_id=1, source_target_pairs={{0,4},{1,3},{4,8},{5,1},{8,12},{9,5},{12,14},{13,9},{14,10},{15,13... | collective-permute-start | bytes 1572872 | tf_op jit(solution)/shard_map/cotangent_3/ppermute | solution.py:290
  31.6 10.0 %collective-permute-start.17 = (bf16[256,1024]{1,0:T(8,128)(2,1)S(1)}, bf16[256,1024]{1,0:T(8,128)(2,1)S(1)}, u32[]{:S(2)}, u32[]{:S(2)}) collective-permute-start(bf16[256,1024]{1,0:T(8,128)(2,1)S(1)} %collective-permute-done.11.near), channel_id=1, source_target_pairs={{0,1},{1,0},{2,3},{3,2},{4,5},{5,4},{6,7},{7,6},{8,9},{9,8},{10,11... | collective-permute-start | bytes 1572872 | tf_op jit(solution)/shard_map/cotangent_2_swap/ppermute | solution.py:290
  36.0 8.8 %collective-permute-start.15 = (bf16[144,1024]{1,0:T(8,128)(2,1)S(1)}, bf16[144,1024]{1,0:T(8,128)(2,1)S(1)}, u32[]{:S(2)}, u32[]{:S(2)}) collective-permute-start(bf16[144,1024]{1,0:T(8,128)(2,1)S(1)} %slice.6), channel_id=1, source_target_pairs={{0,4},{1,3},{4,8},{5,1},{8,12},{9,5},{12,14},{13,9},{14,10},{15,13... | collective-permute-start | bytes 884744 | tf_op jit(solution)/shard_map/tokens_4/ppermute | solution.py:290
  38.0 10.5 %collective-permute-start.18 = (bf16[288,1024]{1,0:T(8,128)(2,1)S(1)}, bf16[288,1024]{1,0:T(8,128)(2,1)S(1)}, u32[]{:S(2)}, u32[]{:S(2)}) collective-permute-start(bf16[288,1024]{1,0:T(8,128)(2,1)S(1)} %collective-permute-done.10.near), channel_id=1, source_target_pairs={{0,1},{1,0},{2,3},{3,2},{4,5},{5,4},{6,7},{7,6},{8,9},{9,8},{10,11... | collective-permute-start | bytes 1769480 | tf_op jit(solution)/shard_map/tokens_3_swap/ppermute | solution.py:290
  46.9 11.5 %collective-permute-start.27 = (bf16[256,1024]{1,0:T(8,128)(2,1)S(1)}, bf16[256,1024]{1,0:T(8,128)(2,1)S(1)}, u32[]{:S(2)}, u32[]{:S(2)}) collective-permute-start(bf16[256,1024]{1,0:T(8,128)(2,1)S(1)} %collective-permute-done.16.near), channel_id=1, source_target_pairs={{0,1},{1,0},{2,3},{3,2},{4,5},{5,4},{6,7},{7,6},{8,9},{9,8},{10,11... | collective-permute-start | bytes 1572872 | tf_op jit(solution)/shard_map/cotangent_3_swap/ppermute | solution.py:290
  61.3 9.2 %collective-permute-start.26 = (bf16[256,1024]{1,0:T(8,128)(2,1)S(1)}, bf16[256,1024]{1,0:T(8,128)(2,1)S(1)}, u32[]{:S(2)}, u32[]{:S(2)}) collective-permute-start(bf16[256,1024]{1,0:T(8,128)(2,1)S(1)} %shard_map.123), channel_id=1, source_target_pairs={{0,4},{1,3},{4,8},{5,1},{8,12},{9,5},{12,14},{13,9},{14,10},{15,13... | collective-permute-start | bytes 1572872 | tf_op jit(solution)/shard_map/mixed_3/ppermute | solution.py:290
  64.1 12.0 %collective-permute-start.32 = (bf16[256,1024]{1,0:T(8,128)(2,1)S(1)}, bf16[256,1024]{1,0:T(8,128)(2,1)S(1)}, u32[]{:S(2)}, u32[]{:S(2)}) collective-permute-start(bf16[256,1024]{1,0:T(8,128)(2,1)S(1)} %shard_map.125), channel_id=1, source_target_pairs={{0,4},{1,3},{4,8},{5,1},{8,12},{9,5},{12,14},{13,9},{14,10},{15,13... | collective-permute-start | bytes 1572872 | tf_op jit(solution)/shard_map/grad_3/ppermute | solution.py:290
  65.9 10.2 %collective-permute-start.31 = (bf16[128,1024]{1,0:T(8,128)(2,1)S(1)}, bf16[128,1024]{1,0:T(8,128)(2,1)S(1)}, u32[]{:S(2)}, u32[]{:S(2)}) collective-permute-start(bf16[128,1024]{1,0:T(8,128)(2,1)S(1)} %get-tuple-element.172), channel_id=1, source_target_pairs={{0,1},{1,0},{2,3},{3,2},{4,5},{5,4},{6,7},{7,6},{8,9},{9,8},{10,11... | collective-permute-start | bytes 786440 | tf_op jit(solution)/shard_map/grad_2_swap/ppermute | solution.py:290
  70.9 10.9 %collective-permute-start.30 = (bf16[256,1024]{1,0:T(8,128)(2,1)S(1)}, bf16[256,1024]{1,0:T(8,128)(2,1)S(1)}, u32[]{:S(2)}, u32[]{:S(2)}) collective-permute-start(bf16[256,1024]{1,0:T(8,128)(2,1)S(1)} %shard_map.127), channel_id=1, source_target_pairs={{0,4},{1,3},{4,8},{5,1},{8,12},{9,5},{12,14},{13,9},{14,10},{15,13... | collective-permute-start | bytes 1572872 | tf_op jit(solution)/shard_map/mixed_2/ppermute | solution.py:290
  76.5 10.9 %collective-permute-start.36 = (bf16[256,1024]{1,0:T(8,128)(2,1)S(1)}, bf16[256,1024]{1,0:T(8,128)(2,1)S(1)}, u32[]{:S(2)}, u32[]{:S(2)}) collective-permute-start(bf16[256,1024]{1,0:T(8,128)(2,1)S(1)} %shard_map.129), channel_id=1, source_target_pairs={{0,4},{1,3},{4,8},{5,1},{8,12},{9,5},{12,14},{13,9},{14,10},{15,13... | collective-permute-start | bytes 1572872 | tf_op jit(solution)/shard_map/grad_2/ppermute | solution.py:290
  78.3 9.1 %collective-permute-start.35 = (bf16[128,1024]{1,0:T(8,128)(2,1)S(1)}, bf16[128,1024]{1,0:T(8,128)(2,1)S(1)}, u32[]{:S(2)}, u32[]{:S(2)}) collective-permute-start(bf16[128,1024]{1,0:T(8,128)(2,1)S(1)} %get-tuple-element.193), channel_id=1, source_target_pairs={{0,1},{1,0},{2,3},{3,2},{4,5},{5,4},{6,7},{7,6},{8,9},{9,8},{10,11... | collective-permute-start | bytes 786440 | tf_op jit(solution)/shard_map/grad_1_swap/ppermute | solution.py:290
  82.1 8.1 %collective-permute-start.33 = (bf16[128,1024]{1,0:T(8,128)(2,1)S(1)}, bf16[128,1024]{1,0:T(8,128)(2,1)S(1)}, u32[]{:S(2)}, u32[]{:S(2)}) collective-permute-start(bf16[128,1024]{1,0:T(8,128)(2,1)S(1)} %get-tuple-element.190), channel_id=1, source_target_pairs={{0,4},{1,3},{4,8},{5,1},{8,12},{9,5},{12,14},{13,9},{14,10},{15,13... | collective-permute-start | bytes 786440 | tf_op jit(solution)/shard_map/mixed_1/ppermute | solution.py:290
  83.9 8.4 %collective-permute-start.34 = (bf16[128,1024]{1,0:T(8,128)(2,1)S(1)}, bf16[128,1024]{1,0:T(8,128)(2,1)S(1)}, u32[]{:S(2)}, u32[]{:S(2)}) collective-permute-start(bf16[128,1024]{1,0:T(8,128)(2,1)S(1)} %get-tuple-element.191), channel_id=1, source_target_pairs={{0,5},{1,2},{4,9},{5,0},{8,13},{9,4},{12,15},{13,8},{14,11},{15,12... | collective-permute-start | bytes 786440 | tf_op jit(solution)/shard_map/mixed_1_crossing/ppermute | solution.py:290
  89.5 8.4 %collective-permute-start.39 = (bf16[128,1024]{1,0:T(8,128)(2,1)S(1)}, bf16[128,1024]{1,0:T(8,128)(2,1)S(1)}, u32[]{:S(2)}, u32[]{:S(2)}) collective-permute-start(bf16[128,1024]{1,0:T(8,128)(2,1)S(1)} %get-tuple-element.196), channel_id=1, source_target_pairs={{0,5},{1,2},{4,9},{5,0},{8,13},{9,4},{12,15},{13,8},{14,11},{15,12... | collective-permute-start | bytes 786440 | tf_op jit(solution)/shard_map/grad_1_crossing/ppermute | solution.py:290
  (16 other events, 76.7 us)

commit v4 on v3

--- a/solution.py
+++ b/solution.py
@@ -95,19 +95,19 @@
 LIMIT = 20 * 1024 * 1024
 
 
-def call(body, outs, operands, flops, smem=0, scratch=(), nbytes=None, far=False):
+def call(body, outs, operands, flops, smem=0, scratch=(), near=True, far=False):
     specs = [pl.BlockSpec(memory_space=pltpu.SMEM)] * smem
     specs += [pl.BlockSpec(memory_space=pltpu.HBM if far else VMEM)] * (len(operands) - smem)
     if far:
         operands = [pltpu.with_memory_space_constraint(a, pltpu.HBM) for a in operands]
     return pl.pallas_call(
         body,
-        out_shape=list(outs),
+        out_shape=[pltpu.VMEM(a.shape, a.dtype) if near else a for a in outs],
         in_specs=specs,
         out_specs=[pl.BlockSpec(memory_space=VMEM)] * len(outs),
         scratch_shapes=list(scratch),
         compiler_params=pltpu.CompilerParams(vmem_limit_bytes=LIMIT),
-        cost_estimate=pl.CostEstimate(flops=0, bytes_accessed=1 << 20, transcendentals=0),
+        cost_estimate=pl.CostEstimate(flops=1 << 20, bytes_accessed=1 << 10, transcendentals=0),
     )(*operands)
 
 
@@ -146,6 +146,15 @@
     body.wait()
 
 
+def join_body(head, tok, first, second, out):
+    if head:
+        reach = 3 * tok
+        out[:head] = first[:head]
+        out[:head, 4 * tok : 4 * tok + reach] = second[:head, :reach]
+    out[head : head + tok] = first[head:]
+    out[head + tok :] = second[head:]
+
+
 def stage_body(*refs):
     *pairs, sems = refs
     half = len(pairs) // 2
@@ -164,11 +173,10 @@
     mate = expert_ref[1].astype(F32)
     head = 2 * top
     tok = info_ref.shape[1]
-    tall = head + tok
-    blocks = [(side, low) for side in (near, far) for low in range(0, side.shape[0], tall)]
+    blocks = [(side, j) for side in (near, far) for j in range((side.shape[0] - head) // tok)]
     names, terms = [], []
-    for side, low in blocks:
-        told = side[low : low + head, : 3 * tok].astype(F32)
+    for side, j in blocks:
+        told = side[:head, 4 * tok * j : 4 * tok * j + 3 * tok].astype(F32)
         names.append(told[:top, :tok])
         told = told[top:]
         terms.append(told[:, :tok] + (told[:, tok : 2 * tok] + told[:, 2 * tok :]))
@@ -189,11 +197,12 @@
     info_ref[0:8] = place
     info_ref[8:16] = jnp.concatenate(weights + [pad], axis=0)
     share = []
-    for i, (side, low) in enumerate(blocks):
+    for i, (side, j) in enumerate(blocks):
+        low = head + j * tok
         pick = picks(place[i : i + 1], cap)
         share.append(jnp.sum(pick * weights[i], axis=1, keepdims=True))
         taken = jnp.dot(
-            pick.astype(BF16), side[low + head : low + tall], preferred_element_type=F32
+            pick.astype(BF16), side[low : low + tok], preferred_element_type=F32
         )
         rows_ref[i * cap : (i + 1) * cap] = taken.astype(BF16)
     rows = rows_ref[...]
@@ -362,51 +371,66 @@
         far=True,
     )
 
-    def depart(block, what):
-        return [hop(block, what + "_1"), hop(block, what + "_1_crossing", crossing)]
-
-    def onward(near, step, what):
+    def join(arrived, top_rows):
+        if len(arrived) == 1:
+            return arrived[0]
+        return call(
+            functools.partial(join_body, top_rows, tok),
+            [struct((top_rows + 2 * tok, width), BF16)],
+            arrived,
+            0,
+        )[0]
+
+    def onward(near, step, top_rows, what):
         if step == reach:
-            near = near[: near.shape[0] // 2]
+            near = near[: top_rows + tok]
         return [hop(near, f"{what}_{step}")]
 
-    cot = after(cotangent, payload)
-    token_near, cot_near = [payload], [cot]
-    token_fly, cot_fly = depart(payload, "tokens"), depart(cot, "cotangent")
-    token_far, cot_far = [swap(payload, "tokens_0_swap")], [swap(cot, "cotangent_0_swap")]
+    token_near, cot_near = [payload], [cotangent]
+    token_fly = [hop(payload, "tokens_1"), hop(payload, "tokens_1_crossing", crossing)]
+    token_far, cot_far = [swap(payload, "tokens_0_swap")], [swap(cotangent, "cotangent_0_swap")]
+    cot_fly = [hop(join([cotangent, cot_far[0]], 0), "cotangent_1")]
     forward, backward = [], []
     for step in range(1, reach + 1):
         before = [b[1] for b in backward[-1:]] or [gate_w]
         *arrived, token_near[-1] = land([*token_fly, token_near[-1]], *before)
-        token_near.append(joined(arrived))
+        token_near.append(join(arrived, head))
         if step < reach:
-            token_fly = onward(token_near[-1], step + 1, "tokens")
+            token_fly = onward(token_near[-1], step + 1, head, "tokens")
         token_far.append(swap(token_near[-1], f"tokens_{step}_swap"))
         forward.append(run_forward(step - 1))
-        if step == reach:
-            forward.append(run_forward(reach))
-        before = [f[5] for f in forward[step - 1 :]]
-        *arrived, cot_near[-1] = land([*cot_fly, cot_near[-1]], *before)
-        cot_near.append(joined(arrived))
+        *arrived, cot_near[-1] = land([*cot_fly, cot_near[-1]], forward[-1][5])
+        cot_near.append(join(arrived, 0))
         if step < reach:
-            cot_fly = onward(cot_near[-1], step + 1, "cotangent")
+            cot_fly = onward(cot_near[-1], step + 1, 0, "cotangent")
         cot_far.append(swap(cot_near[-1], f"cotangent_{step}_swap"))
-        backward.append(run_backward(step - 1))
-    backward.append(run_backward(reach))
+        if step < reach:
+            backward.append(run_backward(step - 1))
+    token_near[reach] = after(token_near[reach], cot_near[reach])
+    forward.append(run_forward(reach))
+    backward.append(run_backward(reach - 1))
 
     def back_from(step, kept, given, values):
         outs = {0: (tok,), 1: (tok, tok), reach: (tok,)}.get(step, (2 * tok,))
         return call(
             functools.partial(return_body, cap, blocks_of(step)[1], len(outs)),
             [struct((rows, width), BF16) for rows in outs],
-            [forward[step][0], kept[step], given[step], *values],
+            [forward[step][0], kept, given, *values],
             0,
+            near=step > 0,
         )
 
     def send_back(sums, step, what):
         if step == 1:
             return [hop(sums[0], what + "_1"), hop(sums[1], what + "_1_crossing", crossing_back)]
         return [hop(sums[0], f"{what}_{step}")]
+
+    def mixed_swap(step):
+        return swap(forward[step][6], f"mixed_{step}_swap")
+
+    def grad_swap(step):
+        return swap(backward[step][4], f"grad_{step}_swap")
+
 
     def weight_grad(lefts, rights):
         return call(
@@ -414,12 +438,16 @@
             [struct((width, units), BF16)],
             [*lefts, *rights],
             0,
+            near=False,
         )[0]
 
-    mixed_kept = [f[5] for f in forward]
-    mixed_given = [swap(f[6], f"mixed_{i}_swap") for i, f in enumerate(forward)]
-    grad_kept = [b[3] for b in backward]
-    grad_given = [swap(b[4], f"grad_{i}_swap") for i, b in enumerate(backward)]
+    mixed_kept = after(forward[reach][5], backward[reach - 1][1])
+    mixed_left = back_from(reach, mixed_kept, mixed_swap(reach), ())
+    mixed_fly = send_back(mixed_left, reach, "mixed")
+    cot_near[reach] = after(cot_near[reach], *mixed_left)
+    backward.append(run_backward(reach))
+    grad_left = back_from(reach, backward[reach][3], grad_swap(reach), ())
+    grad_fly = send_back(grad_left, reach, "grad")
 
     token_rows = [f[1] for f in forward]
     jobs = [
@@ -435,21 +463,19 @@
             return grads[-1:]
         return []
 
-    left = back_from(reach, mixed_kept, mixed_given, ())
-    mixed_fly = send_back(left, reach, "mixed")
-    left = back_from(reach, grad_kept, grad_given, ())
-    grad_fly = send_back(left, reach, "grad")
     for step in range(reach - 1, 0, -1):
-        arrived = land(mixed_fly, *left, *(some_job() if step < reach - 1 else []))
-        left = back_from(step, mixed_kept, mixed_given, arrived)
-        mixed_fly = send_back(left, step, "mixed")
-        arrived = land(grad_fly, *left, *(some_job() if step < reach - 1 else []))
-        left = back_from(step, grad_kept, grad_given, arrived)
-        grad_fly = send_back(left, step, "grad")
+        arrived = land(mixed_fly, *grad_left, *(some_job() if step < reach - 1 else []))
+        mixed_left = back_from(step, forward[step][5], mixed_swap(step), arrived)
+        mixed_fly = send_back(mixed_left, step, "mixed")
+        arrived = land(grad_fly, *mixed_left, *(some_job() if step < reach - 1 else []))
+        grad_left = back_from(step, backward[step][3], grad_swap(step), arrived)
+        grad_fly = send_back(grad_left, step, "grad")
     while len(grads) < len(jobs):
         some_job()
-    mixed = back_from(0, mixed_kept, mixed_given, land(mixed_fly, *left, *grads))[0]
-    grad_tokens = back_from(0, grad_kept, grad_given, land(grad_fly, mixed))[0]
+    arrived = land(mixed_fly, *grad_left, *grads)
+    mixed = back_from(0, forward[0][5], mixed_swap(0), arrived)[0]
+    arrived = land(grad_fly, mixed)
+    grad_tokens = back_from(0, backward[0][3], grad_swap(0), arrived)[0]
     return (mixed, grad_tokens, *[g[None] for g in grads])
 
 
@@ -465,7 +491,7 @@
         and n <= 2 * top
         and tok % 128 == 0
         and top % 8 == 0
-        and width >= 3 * tok
+        and width >= 8 * tok
         and (tok * top) % (16 * n) == 0
     )
     plan = by_ring if ring else by_all_to_all

time: 99.3 us -> 97.6 us (0.983)
  waiting for transfers between devices: 32.2 us -> 27.8 us
  starting transfers between devices: 33.7 us -> 37 us
  local copies, waits for them, and re-layouts: 2.02 us -> 0.05 us
  Pallas kernels: 30.1 us -> 31.5 us
    ppermute x40 -> x39, waiting for transfers between devices: 32.2 us -> 27.8 us  [hop(): return lax.ppermute(value, 'expert', moves)]
    ppermute x40 -> x39, starting transfers between devices: 33.7 us -> 37 us  [hop(): return lax.ppermute(value, 'expert', moves)]
    pallas_call x25 -> x27, Pallas kernels: 30.1 us -> 31.5 us  [call(): pl.pallas_call(body, out_shape=[pltpu.VMEM(a.shape, a.dtype) if near else...]
  transfers between devices with their start and end apart: 40 -> 39, of which waited for: 21 -> 18; matrix products, arithmetic and copies ran while one was open for 2% -> 0% of each run, Pallas kernels for 28% -> 30%
where the time goes in v4:
time: 97.6 us; the launch traced here: 97.3 us
  starting transfers between devices  37 us (38%)
  Pallas kernels  31.5 us (32%)
  waiting for transfers between devices  27.8 us (28%)
    ppermute x39, starting transfers between devices, hop(): return lax.ppermute(value, 'expert', moves)  37 us
    pallas_call x27, Pallas kernels, call(): pl.pallas_call(body, out_shape=[pltpu.VMEM(a.shape, a.dtype) if near else...  31.5 us
    ppermute x39, waiting for transfers between devices, hop(): return lax.ppermute(value, 'expert', moves)  27.8 us
  transfers between devices with their start and end apart: 39, of which 18 were waited for; matrix products, arithmetic and copies ran while one was open for 0% of the time, Pallas kernels for 30%

profile of v4, /device:TPU:0, one launch (start us, length us, event | category | flops | bytes accessed | tf_op | source)
XLA Modules:
  0.0 97.3 jit_solution(7541371115376746120)
XLA Ops:
  2.2 2.6 %collective-permute-start = (bf16[144,1024]{1,0:T(8,128)(2,1)S(1)}, bf16[144,1024]{1,0:T(8,128)(2,1)S(1)}, u32[]{:S(2)}, u32[]{:S(2)}) collective-permute-start(bf16[144,1024]{1,0:T(8,128)(2,1)S(1)} %shard_map.110.near), channel_id=1, source_target_pairs={{0,4},{1,3},{4,8},{5,1},{8,12},{9,5},{12,14},{13,9},{14,10},{15,13... | collective-permute-start | bytes 884744 | tf_op jit(solution)/shard_map/tokens_1/ppermute | solution.py:299
  9.1 2.1 %collective-permute-done.first = bf16[144,1024]{1,0:T(8,128)(2,1)S(1)} collective-permute-done((bf16[144,1024]{1,0:T(8,128)(2,1)S(1)}, bf16[144,1024]{1,0:T(8,128)(2,1)S(1)}, u32[]{:S(2)}, u32[]{:S(2)}) %collective-permute-start) | collective-permute-done | bytes 294944 | tf_op jit(solution)/shard_map/tokens_1/ppermute | solution.py:299
  11.3 3.0 %collective-permute-done.1.second = bf16[144,1024]{1,0:T(8,128)(2,1)S(1)} collective-permute-done((bf16[144,1024]{1,0:T(8,128)(2,1)S(1)}, bf16[144,1024]{1,0:T(8,128)(2,1)S(1)}, u32[]{:S(2)}, u32[]{:S(2)}) %collective-permute-start.1) | collective-permute-done | bytes 294944 | tf_op jit(solution)/shard_map/tokens_1_crossing/ppermute | solution.py:299
  24.3 2.1 %collective-permute-start.9 = (bf16[272,1024]{1,0:T(8,128)(2,1)}, bf16[272,1024]{1,0:T(8,128)(2,1)S(1)}, u32[]{:S(2)}, u32[]{:S(2)}) collective-permute-start(bf16[272,1024]{1,0:T(8,128)(2,1)} %collective-permute-done.4.near), channel_id=1, source_target_pairs={{0,4},{1,3},{4,8},{5,1},{8,12},{9,5},{12,14},{13,9},{14,10},{15,13... | collective-permute-start | bytes 1671176 | tf_op jit(solution)/shard_map/tokens_3/ppermute | solution.py:299
  29.8 2.1 %collective-permute-start.15 = (bf16[256,1024]{1,0:T(8,128)(2,1)S(1)}, bf16[256,1024]{1,0:T(8,128)(2,1)S(1)}, u32[]{:S(2)}, u32[]{:S(2)}) collective-permute-start(bf16[256,1024]{1,0:T(8,128)(2,1)S(1)} %collective-permute-done.10.near), channel_id=1, source_target_pairs={{0,4},{1,3},{4,8},{5,1},{8,12},{9,5},{12,14},{13,9},{14,10},{15,13... | collective-permute-start | bytes 1572872 | tf_op jit(solution)/shard_map/cotangent_3/ppermute | solution.py:299
  31.9 2.3 %shard_map.117 = (bf16[256,1024]{1,0:T(8,128)(2,1)S(1)}, bf16[256,384]{1,0:T(8,128)(2,1)S(1)}, bf16[256,384]{1,0:T(8,128)(2,1)S(1)}, bf16[128,1024]{1,0:T(8,128)(2,1)S(1)}, bf16[128,1024]{1,0:T(8,128)(2,1)S(1)}) custom-call(f32[16,128]{1,0:T(8,128)S(1)} %get-tuple-element.122.info_ref, f32[256,384]{1,0:T(8,128)S(1)} %get-tuple-element.126.slope, ...), custom_call_target="tpu_custom_call" | custom-call | flops 1048576 | bytes 1024 | tf_op jit(solution)/shard_map/pallas_call | solution.py:103
  35.8 2.2 %collective-permute-start.14 = (bf16[144,1024]{1,0:T(8,128)(2,1)S(1)}, bf16[144,1024]{1,0:T(8,128)(2,1)S(1)}, u32[]{:S(2)}, u32[]{:S(2)}) collective-permute-start(bf16[144,1024]{1,0:T(8,128)(2,1)S(1)} %slice.6), channel_id=1, source_target_pairs={{0,4},{1,3},{4,8},{5,1},{8,12},{9,5},{12,14},{13,9},{14,10},{15,13... | collective-permute-start | bytes 884744 | tf_op jit(solution)/shard_map/tokens_4/ppermute | solution.py:299
  38.0 2.5 %shard_map.118 = (f32[16,128]{1,0:T(8,128)S(1)}, bf16[256,1024]{1,0:T(8,128)(2,1)S(1)}, f32[256,384]{1,0:T(8,128)S(1)}, f32[256,384]{1,0:T(8,128)S(1)}, bf16[256...) custom-call(s32[2]{0:T(128)S(1)} %pad_add_fusion.expert_ref, ...), custom_call_target="tpu_custom_call" | custom-call | flops 1048576 | bytes 1024 | tf_op jit(solution)/shard_map/pallas_call | solution.py:103
  41.5 2.2 %collective-permute-start.19 = (bf16[128,1024]{1,0:T(8,128)(2,1)S(1)}, bf16[128,1024]{1,0:T(8,128)(2,1)S(1)}, u32[]{:S(2)}, u32[]{:S(2)}) collective-permute-start(bf16[128,1024]{1,0:T(8,128)(2,1)S(1)} %slice.7), channel_id=1, source_target_pairs={{0,4},{1,3},{4,8},{5,1},{8,12},{9,5},{12,14},{13,9},{14,10},{15,13... | collective-permute-start | bytes 786440 | tf_op jit(solution)/shard_map/cotangent_4/ppermute | solution.py:299
  52.7 2.1 %collective-permute-start.23 = (bf16[128,1024]{1,0:T(8,128)(2,1)S(1)}, bf16[128,1024]{1,0:T(8,128)(2,1)S(1)}, u32[]{:S(2)}, u32[]{:S(2)}) collective-permute-start(bf16[128,1024]{1,0:T(8,128)(2,1)S(1)} %shard_map.123), channel_id=1, source_target_pairs={{0,4},{1,3},{4,8},{5,1},{8,12},{9,5},{12,14},{13,9},{14,10},{15,13... | collective-permute-start | bytes 786440 | tf_op jit(solution)/shard_map/mixed_4/ppermute | solution.py:299
  56.9 2.2 %collective-permute-done.23.refs_0_ = bf16[128,1024]{1,0:T(8,128)(2,1)S(1)} collective-permute-done((bf16[128,1024]{1,0:T(8,128)(2,1)S(1)}, bf16[128,1024]{1,0:T(8,128)(2,1)S(1)}, u32[]{:S(2)}, u32[]{:S(2)}) %collective-permute-start.23) | collective-permute-done | bytes 262176 | tf_op jit(solution)/shard_map/mixed_4/ppermute | solution.py:299
  59.4 2.1 %collective-permute-start.26 = (bf16[256,1024]{1,0:T(8,128)(2,1)S(1)}, bf16[256,1024]{1,0:T(8,128)(2,1)S(1)}, u32[]{:S(2)}, u32[]{:S(2)}) collective-permute-start(bf16[256,1024]{1,0:T(8,128)(2,1)S(1)} %shard_map.126), channel_id=1, source_target_pairs={{0,4},{1,3},{4,8},{5,1},{8,12},{9,5},{12,14},{13,9},{14,10},{15,13... | collective-permute-start | bytes 1572872 | tf_op jit(solution)/shard_map/mixed_3/ppermute | solution.py:299
  62.2 2.1 %collective-permute-start.31 = (bf16[256,1024]{1,0:T(8,128)(2,1)S(1)}, bf16[256,1024]{1,0:T(8,128)(2,1)S(1)}, u32[]{:S(2)}, u32[]{:S(2)}) collective-permute-start(bf16[256,1024]{1,0:T(8,128)(2,1)S(1)} %shard_map.127), channel_id=1, source_target_pairs={{0,4},{1,3},{4,8},{5,1},{8,12},{9,5},{12,14},{13,9},{14,10},{15,13... | collective-permute-start | bytes 1572872 | tf_op jit(solution)/shard_map/grad_3/ppermute | solution.py:299
  64.9 2.2 %shard_map.128 = bf16[1024,384]{1,0:T(8,128)(2,1)} custom-call(bf16[128,1024]{1,0:T(8,128)(2,1)S(1)} %get-tuple-element.166.refs_0_, bf16[256,1024]{1,0:T(8,128)(2,1)S(1)} %get-tuple-element.167.refs_1_, bf16[256,1024]{1,0:T(8,128)(2,1)S(1)} %get-tuple-element.168.refs_2_, bf16[256,1024]{1,0:T(8,128)(2,1)S(1)} %get-tuple-element.169.refs_3_, ...), custom_call_target="tpu_custom_call" | custom-call | flops 1048576 | bytes 1024 | tf_op jit(solution)/shard_map/pallas_call | solution.py:103
  69.0 2.1 %collective-permute-start.29 = (bf16[256,1024]{1,0:T(8,128)(2,1)S(1)}, bf16[256,1024]{1,0:T(8,128)(2,1)S(1)}, u32[]{:S(2)}, u32[]{:S(2)}) collective-permute-start(bf16[256,1024]{1,0:T(8,128)(2,1)S(1)} %shard_map.129), channel_id=1, source_target_pairs={{0,4},{1,3},{4,8},{5,1},{8,12},{9,5},{12,14},{13,9},{14,10},{15,13... | collective-permute-start | bytes 1572872 | tf_op jit(solution)/shard_map/mixed_2/ppermute | solution.py:299
  71.1 2.2 %shard_map.130 = bf16[1024,384]{1,0:T(8,128)(2,1)} custom-call(bf16[128,1024]{1,0:T(8,128)(2,1)S(1)} %get-tuple-element.166.refs_0_, bf16[256,1024]{1,0:T(8,128)(2,1)S(1)} %get-tuple-element.167.refs_1_, bf16[256,1024]{1,0:T(8,128)(2,1)S(1)} %get-tuple-element.168.refs_2_, bf16[256,1024]{1,0:T(8,128)(2,1)S(1)} %get-tuple-element.169.refs_3_, ...), custom_call_target="tpu_custom_call" | custom-call | flops 1048576 | bytes 1024 | tf_op jit(solution)/shard_map/pallas_call | solution.py:103
  74.6 2.1 %collective-permute-start.35 = (bf16[256,1024]{1,0:T(8,128)(2,1)S(1)}, bf16[256,1024]{1,0:T(8,128)(2,1)S(1)}, u32[]{:S(2)}, u32[]{:S(2)}) collective-permute-start(bf16[256,1024]{1,0:T(8,128)(2,1)S(1)} %shard_map.131), channel_id=1, source_target_pairs={{0,4},{1,3},{4,8},{5,1},{8,12},{9,5},{12,14},{13,9},{14,10},{15,13... | collective-permute-start | bytes 1572872 | tf_op jit(solution)/shard_map/grad_2/ppermute | solution.py:299
  77.3 2.2 %shard_map.132 = bf16[1024,384]{1,0:T(8,128)(2,1)} custom-call(bf16[128,1024]{1,0:T(8,128)(2,1)S(1)} %get-tuple-element.181.refs_0_, bf16[256,1024]{1,0:T(8,128)(2,1)S(1)} %get-tuple-element.182.refs_1_, bf16[256,1024]{1,0:T(8,128)(2,1)S(1)} %get-tuple-element.183.refs_2_, bf16[256,1024]{1,0:T(8,128)(2,1)S(1)} %get-tuple-element.184.refs_3_, ...), custom_call_target="tpu_custom_call" | custom-call | flops 1048576 | bytes 1024 | tf_op jit(solution)/shard_map/pallas_call | solution.py:103
  80.2 2.1 %collective-permute-start.32 = (bf16[128,1024]{1,0:T(8,128)(2,1)S(1)}, bf16[128,1024]{1,0:T(8,128)(2,1)S(1)}, u32[]{:S(2)}, u32[]{:S(2)}) collective-permute-start(bf16[128,1024]{1,0:T(8,128)(2,1)S(1)} %get-tuple-element.192), channel_id=1, source_target_pairs={{0,4},{1,3},{4,8},{5,1},{8,12},{9,5},{12,14},{13,9},{14,10},{15,13... | collective-permute-start | bytes 786440 | tf_op jit(solution)/shard_map/mixed_1/ppermute | solution.py:299
  82.4 3.1 %collective-permute-done.35.refs_0_ = bf16[256,1024]{1,0:T(8,128)(2,1)S(1)} collective-permute-done((bf16[256,1024]{1,0:T(8,128)(2,1)S(1)}, bf16[256,1024]{1,0:T(8,128)(2,1)S(1)}, u32[]{:S(2)}, u32[]{:S(2)}) %collective-permute-start.35) | collective-permute-done | bytes 524320 | tf_op jit(solution)/shard_map/grad_2/ppermute | solution.py:299
  85.9 2.1 %collective-permute-start.37 = (bf16[128,1024]{1,0:T(8,128)(2,1)S(1)}, bf16[128,1024]{1,0:T(8,128)(2,1)S(1)}, u32[]{:S(2)}, u32[]{:S(2)}) collective-permute-start(bf16[128,1024]{1,0:T(8,128)(2,1)S(1)} %get-tuple-element.197), channel_id=1, source_target_pairs={{0,4},{1,3},{4,8},{5,1},{8,12},{9,5},{12,14},{13,9},{14,10},{15,13... | collective-permute-start | bytes 786440 | tf_op jit(solution)/shard_map/grad_1/ppermute | solution.py:299
  88.5 2.2 %collective-permute-done.33.refs_1_ = bf16[128,1024]{1,0:T(8,128)(2,1)S(1)} collective-permute-done((bf16[128,1024]{1,0:T(8,128)(2,1)S(1)}, bf16[128,1024]{1,0:T(8,128)(2,1)S(1)}, u32[]{:S(2)}, u32[]{:S(2)}) %collective-permute-start.33) | collective-permute-done | bytes 262176 | tf_op jit(solution)/shard_map/mixed_1_crossing/ppermute | solution.py:299
  91.7 2.2 %collective-permute-done.37.refs_0_ = bf16[128,1024]{1,0:T(8,128)(2,1)S(1)} collective-permute-done((bf16[128,1024]{1,0:T(8,128)(2,1)S(1)}, bf16[128,1024]{1,0:T(8,128)(2,1)S(1)}, u32[]{:S(2)}, u32[]{:S(2)}) %collective-permute-start.37) | collective-permute-done | bytes 262176 | tf_op jit(solution)/shard_map/grad_1/ppermute | solution.py:299
  93.9 2.4 %collective-permute-done.38.refs_1_ = bf16[128,1024]{1,0:T(8,128)(2,1)S(1)} collective-permute-done((bf16[128,1024]{1,0:T(8,128)(2,1)S(1)}, bf16[128,1024]{1,0:T(8,128)(2,1)S(1)}, u32[]{:S(2)}, u32[]{:S(2)}) %collective-permute-start.38) | collective-permute-done | bytes 262176 | tf_op jit(solution)/shard_map/grad_1_crossing/ppermute | solution.py:299
  (90 shorter events, 41.6 us)
Async XLA Ops:
  2.2 9.0 %collective-permute-start = (bf16[144,1024]{1,0:T(8,128)(2,1)S(1)}, bf16[144,1024]{1,0:T(8,128)(2,1)S(1)}, u32[]{:S(2)}, u32[]{:S(2)}) collective-permute-start(bf16[144,1024]{1,0:T(8,128)(2,1)S(1)} %shard_map.110.near), channel_id=1, source_target_pairs={{0,4},{1,3},{4,8},{5,1},{8,12},{9,5},{12,14},{13,9},{14,10},{15,13... | collective-permute-start | bytes 884744 | tf_op jit(solution)/shard_map/tokens_1/ppermute | solution.py:299
  4.9 9.4 %collective-permute-start.1 = (bf16[144,1024]{1,0:T(8,128)(2,1)S(1)}, bf16[144,1024]{1,0:T(8,128)(2,1)S(1)}, u32[]{:S(2)}, u32[]{:S(2)}) collective-permute-start(bf16[144,1024]{1,0:T(8,128)(2,1)S(1)} %shard_map.110.near), channel_id=1, source_target_pairs={{0,3},{1,4},{4,1},{5,8},{8,5},{9,12},{12,9},{13,14},{14,13},{15,10... | collective-permute-start | bytes 884744 | tf_op jit(solution)/shard_map/tokens_1_crossing/ppermute | solution.py:299
  7.1 12.5 %collective-permute-start.6 = (bf16[256,1024]{1,0:T(8,128)(2,1)}, bf16[256,1024]{1,0:T(8,128)(2,1)}, u32[]{:S(2)}, u32[]{:S(2)}) collective-permute-start(bf16[256,1024]{1,0:T(8,128)(2,1)} %shard_map.114), channel_id=1, source_target_pairs={{0,4},{1,3},{4,8},{5,1},{8,12},{9,5},{12,14},{13,9},{14,10},{15,13... | collective-permute-start | bytes 1572872 | tf_op jit(solution)/shard_map/cotangent_1/ppermute | solution.py:299
  14.3 10.1 %collective-permute-start.4 = (bf16[272,1024]{1,0:T(8,128)(2,1)S(1)}, bf16[272,1024]{1,0:T(8,128)(2,1)}, u32[]{:S(2)}, u32[]{:S(2)}) collective-permute-start(bf16[272,1024]{1,0:T(8,128)(2,1)S(1)} %shard_map.113.near), channel_id=1, source_target_pairs={{0,4},{1,3},{4,8},{5,1},{8,12},{9,5},{12,14},{13,9},{14,10},{15,13... | collective-permute-start | bytes 1671176 | tf_op jit(solution)/shard_map/tokens_2/ppermute | solution.py:299
  16.1 10.8 %collective-permute-start.7 = (bf16[272,1024]{1,0:T(8,128)(2,1)S(1)}, bf16[272,1024]{1,0:T(8,128)(2,1)S(1)}, u32[]{:S(2)}, u32[]{:S(2)}) collective-permute-start(bf16[272,1024]{1,0:T(8,128)(2,1)S(1)} %shard_map.113.near), channel_id=1, source_target_pairs={{0,1},{1,0},{2,3},{3,2},{4,5},{5,4},{6,7},{7,6},{8,9},{9,8},{10,11... | collective-permute-start | bytes 1671176 | tf_op jit(solution)/shard_map/tokens_1_swap/ppermute | solution.py:299
  19.6 10.2 %collective-permute-start.10 = (bf16[256,1024]{1,0:T(8,128)(2,1)}, bf16[256,1024]{1,0:T(8,128)(2,1)S(1)}, u32[]{:S(2)}, u32[]{:S(2)}) collective-permute-start(bf16[256,1024]{1,0:T(8,128)(2,1)} %collective-permute-done.6.near), channel_id=1, source_target_pairs={{0,4},{1,3},{4,8},{5,1},{8,12},{9,5},{12,14},{13,9},{14,10},{15,13... | collective-permute-start | bytes 1572872 | tf_op jit(solution)/shard_map/cotangent_2/ppermute | solution.py:299
  24.3 11.5 %collective-permute-start.9 = (bf16[272,1024]{1,0:T(8,128)(2,1)}, bf16[272,1024]{1,0:T(8,128)(2,1)S(1)}, u32[]{:S(2)}, u32[]{:S(2)}) collective-permute-start(bf16[272,1024]{1,0:T(8,128)(2,1)} %collective-permute-done.4.near), channel_id=1, source_target_pairs={{0,4},{1,3},{4,8},{5,1},{8,12},{9,5},{12,14},{13,9},{14,10},{15,13... | collective-permute-start | bytes 1671176 | tf_op jit(solution)/shard_map/tokens_3/ppermute | solution.py:299
  26.4 11.6 %collective-permute-start.12 = (bf16[272,1024]{1,0:T(8,128)(2,1)}, bf16[272,1024]{1,0:T(8,128)(2,1)S(1)}, u32[]{:S(2)}, u32[]{:S(2)}) collective-permute-start(bf16[272,1024]{1,0:T(8,128)(2,1)} %collective-permute-done.4.near), channel_id=1, source_target_pairs={{0,1},{1,0},{2,3},{3,2},{4,5},{5,4},{6,7},{7,6},{8,9},{9,8},{10,11... | collective-permute-start | bytes 1671176 | tf_op jit(solution)/shard_map/tokens_2_swap/ppermute | solution.py:299
  29.8 11.6 %collective-permute-start.15 = (bf16[256,1024]{1,0:T(8,128)(2,1)S(1)}, bf16[256,1024]{1,0:T(8,128)(2,1)S(1)}, u32[]{:S(2)}, u32[]{:S(2)}) collective-permute-start(bf16[256,1024]{1,0:T(8,128)(2,1)S(1)} %collective-permute-done.10.near), channel_id=1, source_target_pairs={{0,4},{1,3},{4,8},{5,1},{8,12},{9,5},{12,14},{13,9},{14,10},{15,13... | collective-permute-start | bytes 1572872 | tf_op jit(solution)/shard_map/cotangent_3/ppermute | solution.py:299
  31.9 11.7 %collective-permute-start.16 = (bf16[256,1024]{1,0:T(8,128)(2,1)S(1)}, bf16[256,1024]{1,0:T(8,128)(2,1)S(1)}, u32[]{:S(2)}, u32[]{:S(2)}) collective-permute-start(bf16[256,1024]{1,0:T(8,128)(2,1)S(1)} %collective-permute-done.10.near), channel_id=1, source_target_pairs={{0,1},{1,0},{2,3},{3,2},{4,5},{5,4},{6,7},{7,6},{8,9},{9,8},{10,11... | collective-permute-start | bytes 1572872 | tf_op jit(solution)/shard_map/cotangent_2_swap/ppermute | solution.py:299
  35.8 9.3 %collective-permute-start.17 = (bf16[272,1024]{1,0:T(8,128)(2,1)S(1)}, bf16[272,1024]{1,0:T(8,128)(2,1)S(1)}, u32[]{:S(2)}, u32[]{:S(2)}) collective-permute-start(bf16[272,1024]{1,0:T(8,128)(2,1)S(1)} %collective-permute-done.9.near), channel_id=1, source_target_pairs={{0,1},{1,0},{2,3},{3,2},{4,5},{5,4},{6,7},{7,6},{8,9},{9,8},{10,11... | collective-permute-start | bytes 1671176 | tf_op jit(solution)/shard_map/tokens_3_swap/ppermute | solution.py:299
  35.8 9.1 %collective-permute-start.14 = (bf16[144,1024]{1,0:T(8,128)(2,1)S(1)}, bf16[144,1024]{1,0:T(8,128)(2,1)S(1)}, u32[]{:S(2)}, u32[]{:S(2)}) collective-permute-start(bf16[144,1024]{1,0:T(8,128)(2,1)S(1)} %slice.6), channel_id=1, source_target_pairs={{0,4},{1,3},{4,8},{5,1},{8,12},{9,5},{12,14},{13,9},{14,10},{15,13... | collective-permute-start | bytes 884744 | tf_op jit(solution)/shard_map/tokens_4/ppermute | solution.py:299
  41.4 8.6 %collective-permute-start.21 = (bf16[256,1024]{1,0:T(8,128)(2,1)S(1)}, bf16[256,1024]{1,0:T(8,128)(2,1)S(1)}, u32[]{:S(2)}, u32[]{:S(2)}) collective-permute-start(bf16[256,1024]{1,0:T(8,128)(2,1)S(1)} %collective-permute-done.15.near), channel_id=1, source_target_pairs={{0,1},{1,0},{2,3},{3,2},{4,5},{5,4},{6,7},{7,6},{8,9},{9,8},{10,11... | collective-permute-start | bytes 1572872 | tf_op jit(solution)/shard_map/cotangent_3_swap/ppermute | solution.py:299
  59.4 9.2 %collective-permute-start.26 = (bf16[256,1024]{1,0:T(8,128)(2,1)S(1)}, bf16[256,1024]{1,0:T(8,128)(2,1)S(1)}, u32[]{:S(2)}, u32[]{:S(2)}) collective-permute-start(bf16[256,1024]{1,0:T(8,128)(2,1)S(1)} %shard_map.126), channel_id=1, source_target_pairs={{0,4},{1,3},{4,8},{5,1},{8,12},{9,5},{12,14},{13,9},{14,10},{15,13... | collective-permute-start | bytes 1572872 | tf_op jit(solution)/shard_map/mixed_3/ppermute | solution.py:299
  62.2 12.0 %collective-permute-start.31 = (bf16[256,1024]{1,0:T(8,128)(2,1)S(1)}, bf16[256,1024]{1,0:T(8,128)(2,1)S(1)}, u32[]{:S(2)}, u32[]{:S(2)}) collective-permute-start(bf16[256,1024]{1,0:T(8,128)(2,1)S(1)} %shard_map.127), channel_id=1, source_target_pairs={{0,4},{1,3},{4,8},{5,1},{8,12},{9,5},{12,14},{13,9},{14,10},{15,13... | collective-permute-start | bytes 1572872 | tf_op jit(solution)/shard_map/grad_3/ppermute | solution.py:299
  64.4 9.9 %collective-permute-start.30 = (bf16[128,1024]{1,0:T(8,128)(2,1)S(1)}, bf16[128,1024]{1,0:T(8,128)(2,1)S(1)}, u32[]{:S(2)}, u32[]{:S(2)}) collective-permute-start(bf16[128,1024]{1,0:T(8,128)(2,1)S(1)} %get-tuple-element.174), channel_id=1, source_target_pairs={{0,1},{1,0},{2,3},{3,2},{4,5},{5,4},{6,7},{7,6},{8,9},{9,8},{10,11... | collective-permute-start | bytes 786440 | tf_op jit(solution)/shard_map/grad_2_swap/ppermute | solution.py:299
  69.0 10.9 %collective-permute-start.29 = (bf16[256,1024]{1,0:T(8,128)(2,1)S(1)}, bf16[256,1024]{1,0:T(8,128)(2,1)S(1)}, u32[]{:S(2)}, u32[]{:S(2)}) collective-permute-start(bf16[256,1024]{1,0:T(8,128)(2,1)S(1)} %shard_map.129), channel_id=1, source_target_pairs={{0,4},{1,3},{4,8},{5,1},{8,12},{9,5},{12,14},{13,9},{14,10},{15,13... | collective-permute-start | bytes 1572872 | tf_op jit(solution)/shard_map/mixed_2/ppermute | solution.py:299
  74.6 10.9 %collective-permute-start.35 = (bf16[256,1024]{1,0:T(8,128)(2,1)S(1)}, bf16[256,1024]{1,0:T(8,128)(2,1)S(1)}, u32[]{:S(2)}, u32[]{:S(2)}) collective-permute-start(bf16[256,1024]{1,0:T(8,128)(2,1)S(1)} %shard_map.131), channel_id=1, source_target_pairs={{0,4},{1,3},{4,8},{5,1},{8,12},{9,5},{12,14},{13,9},{14,10},{15,13... | collective-permute-start | bytes 1572872 | tf_op jit(solution)/shard_map/grad_2/ppermute | solution.py:299
  76.8 8.8 %collective-permute-start.34 = (bf16[128,1024]{1,0:T(8,128)(2,1)S(1)}, bf16[128,1024]{1,0:T(8,128)(2,1)S(1)}, u32[]{:S(2)}, u32[]{:S(2)}) collective-permute-start(bf16[128,1024]{1,0:T(8,128)(2,1)S(1)} %get-tuple-element.195), channel_id=1, source_target_pairs={{0,1},{1,0},{2,3},{3,2},{4,5},{5,4},{6,7},{7,6},{8,9},{9,8},{10,11... | collective-permute-start | bytes 786440 | tf_op jit(solution)/shard_map/grad_1_swap/ppermute | solution.py:299
  80.2 8.1 %collective-permute-start.32 = (bf16[128,1024]{1,0:T(8,128)(2,1)S(1)}, bf16[128,1024]{1,0:T(8,128)(2,1)S(1)}, u32[]{:S(2)}, u32[]{:S(2)}) collective-permute-start(bf16[128,1024]{1,0:T(8,128)(2,1)S(1)} %get-tuple-element.192), channel_id=1, source_target_pairs={{0,4},{1,3},{4,8},{5,1},{8,12},{9,5},{12,14},{13,9},{14,10},{15,13... | collective-permute-start | bytes 786440 | tf_op jit(solution)/shard_map/mixed_1/ppermute | solution.py:299
  82.4 8.4 %collective-permute-start.33 = (bf16[128,1024]{1,0:T(8,128)(2,1)S(1)}, bf16[128,1024]{1,0:T(8,128)(2,1)S(1)}, u32[]{:S(2)}, u32[]{:S(2)}) collective-permute-start(bf16[128,1024]{1,0:T(8,128)(2,1)S(1)} %get-tuple-element.193), channel_id=1, source_target_pairs={{0,5},{1,2},{4,9},{5,0},{8,13},{9,4},{12,15},{13,8},{14,11},{15,12... | collective-permute-start | bytes 786440 | tf_op jit(solution)/shard_map/mixed_1_crossing/ppermute | solution.py:299
  85.9 8.1 %collective-permute-start.37 = (bf16[128,1024]{1,0:T(8,128)(2,1)S(1)}, bf16[128,1024]{1,0:T(8,128)(2,1)S(1)}, u32[]{:S(2)}, u32[]{:S(2)}) collective-permute-start(bf16[128,1024]{1,0:T(8,128)(2,1)S(1)} %get-tuple-element.197), channel_id=1, source_target_pairs={{0,4},{1,3},{4,8},{5,1},{8,12},{9,5},{12,14},{13,9},{14,10},{15,13... | collective-permute-start | bytes 786440 | tf_op jit(solution)/shard_map/grad_1/ppermute | solution.py:299
  88.0 8.4 %collective-permute-start.38 = (bf16[128,1024]{1,0:T(8,128)(2,1)S(1)}, bf16[128,1024]{1,0:T(8,128)(2,1)S(1)}, u32[]{:S(2)}, u32[]{:S(2)}) collective-permute-start(bf16[128,1024]{1,0:T(8,128)(2,1)S(1)} %get-tuple-element.198), channel_id=1, source_target_pairs={{0,5},{1,2},{4,9},{5,0},{8,13},{9,4},{12,15},{13,8},{14,11},{15,12... | collective-permute-start | bytes 786440 | tf_op jit(solution)/shard_map/grad_1_crossing/ppermute | solution.py:299
  88.3 8.0 %collective-permute-start.36 = (bf16[64,1024]{1,0:T(8,128)(2,1)S(1)}, bf16[64,1024]{1,0:T(8,128)(2,1)S(1)}, u32[]{:S(2)}, u32[]{:S(2)}) collective-permute-start(bf16[64,1024]{1,0:T(8,128)(2,1)S(1)} %get-tuple-element.202), channel_id=1, source_target_pairs={{0,1},{1,0},{2,3},{3,2},{4,5},{5,4},{6,7},{7,6},{8,9},{9,8},{10,11... | collective-permute-start | bytes 393224 | tf_op jit(solution)/shard_map/grad_0_swap/ppermute | solution.py:299
  (18 other events, 72.6 us)

commit v5 on v4

--- a/solution.py
+++ b/solution.py
@@ -92,23 +92,30 @@
 
 
 VMEM = pltpu.VMEM
-LIMIT = 20 * 1024 * 1024
-
-
-def call(body, outs, operands, flops, smem=0, scratch=(), near=True, far=False):
+LIMIT = 14 * 1024 * 1024
+
+
+K = {'far0': 0, 'mate': 'T3', 'mate_after': 'T1', 'f3': 't4', 'b2': 'm3', 'b3': 'm4', 'force': 0, 'cot1': 'join'}
+COST = {'pair_forward': 30, 'forward_0': 31, 'forward_4': 32, 'backward_0': 31, 'grad_sums_0': 29, 'forward_2': 31, 'grad_sums_1': 30, 'stage': 30, 'mixed_sums_2': 29, 'backward_1': 30, 'join_1': 30}
+
+
+def call(name, body, outs, operands, smem=0, scratch=(), near=True, far=False):
     specs = [pl.BlockSpec(memory_space=pltpu.SMEM)] * smem
     specs += [pl.BlockSpec(memory_space=pltpu.HBM if far else VMEM)] * (len(operands) - smem)
     if far:
         operands = [pltpu.with_memory_space_constraint(a, pltpu.HBM) for a in operands]
-    return pl.pallas_call(
-        body,
-        out_shape=[pltpu.VMEM(a.shape, a.dtype) if near else a for a in outs],
-        in_specs=specs,
-        out_specs=[pl.BlockSpec(memory_space=VMEM)] * len(outs),
-        scratch_shapes=list(scratch),
-        compiler_params=pltpu.CompilerParams(vmem_limit_bytes=LIMIT),
-        cost_estimate=pl.CostEstimate(flops=1 << 20, bytes_accessed=1 << 10, transcendentals=0),
-    )(*operands)
+    with jax.named_scope(name):
+        return pl.pallas_call(
+            body,
+            out_shape=[pltpu.VMEM(a.shape, a.dtype) if near else a for a in outs],
+            in_specs=specs,
+            out_specs=[pl.BlockSpec(memory_space=VMEM)] * len(outs),
+            scratch_shapes=list(scratch),
+            compiler_params=pltpu.CompilerParams(vmem_limit_bytes=LIMIT),
+            cost_estimate=pl.CostEstimate(
+                flops=1 << COST.get(name, 20), bytes_accessed=1 << 10, transcendentals=0
+            ),
+        )(*operands)
 
 
 def picks(place, cap):
@@ -167,55 +174,103 @@
         copy.wait()
 
 
-def forward_body(cap, top, kept, expert_ref, near, far, w_gate, w_up, w_down, *outs):
-    info_ref, rows_ref, slope_ref, act_ref, hidden_ref, keep_ref, give_ref = outs
+def told_of(side, j, head, tok):
+    told = side[:head, 4 * tok * j : 4 * tok * j + 3 * tok].astype(F32)
+    names, told = told[: head // 2, :tok], told[head // 2 :]
+    return names, told[:, :tok] + (told[:, tok : 2 * tok] + told[:, 2 * tok :])
+
+
+def places_of(wanted, info_ref):
+    masks, weights = [], []
+    for names, terms, expert in wanted:
+        hit = names == expert
+        masks.append(jnp.sum(jnp.where(hit, 1.0, 0.0), axis=0, keepdims=True))
+        weights.append(jnp.sum(jnp.where(hit, terms, 0.0), axis=0, keepdims=True))
+    tok = info_ref.shape[1]
+    pad = jnp.zeros((8 - len(masks), tok), F32)
+    mask = jnp.concatenate(masks + [pad], axis=0)
+    before = lax.broadcasted_iota(jnp.int32, (tok, tok), 0) < lax.broadcasted_iota(
+        jnp.int32, (tok, tok), 1
+    )
+    rank = jnp.dot(
+        mask.astype(BF16), jnp.where(before, 1.0, 0.0).astype(BF16), preferred_element_type=F32
+    )
+    place = jnp.where(mask > 0.5, rank, -1.0)
+    info_ref[0:8] = place
+    info_ref[8:16] = jnp.concatenate(weights + [pad], axis=0)
+    return place, weights
+
+
+def hidden_of(rows, w_gate, w_up):
+    gate = jnp.dot(rows, w_gate[...], preferred_element_type=F32)
+    up = jnp.dot(rows, w_up[...], preferred_element_type=F32)
+    sig = jax.nn.sigmoid(gate)
+    act = gate * sig
+    return (act * up).astype(BF16), up * sig * (1.0 + gate * (1.0 - sig)), act
+
+
+def forward_body(cap, top, kept, sums, expert_ref, near, far, w_gate, w_up, w_down, *outs):
+    info_ref, rows_ref, slope_ref, act_ref, hidden_ref = outs[:5]
     me = expert_ref[0].astype(F32)
     mate = expert_ref[1].astype(F32)
     head = 2 * top
     tok = info_ref.shape[1]
     blocks = [(side, j) for side in (near, far) for j in range((side.shape[0] - head) // tok)]
-    names, terms = [], []
-    for side, j in blocks:
-        told = side[:head, 4 * tok * j : 4 * tok * j + 3 * tok].astype(F32)
-        names.append(told[:top, :tok])
-        told = told[top:]
-        terms.append(told[:, :tok] + (told[:, tok : 2 * tok] + told[:, 2 * tok :]))
-    masks, weights = [], []
-    for expert, which in [(me, i) for i in range(len(blocks))] + [(mate, i) for i in kept]:
-        hit = names[which] == expert
-        masks.append(jnp.sum(jnp.where(hit, 1.0, 0.0), axis=0, keepdims=True))
-        weights.append(jnp.sum(jnp.where(hit, terms[which], 0.0), axis=0, keepdims=True))
-    pad = jnp.zeros((8 - len(masks), tok), F32)
-    mask = jnp.concatenate(masks + [pad], axis=0)
-    before = lax.broadcasted_iota(jnp.int32, (tok, tok), 0) < lax.broadcasted_iota(
-        jnp.int32, (tok, tok), 1
-    )
-    rank = jnp.dot(
-        mask.astype(BF16), jnp.where(before, 1.0, 0.0).astype(BF16), preferred_element_type=F32
-    )
-    place = jnp.where(mask > 0.5, rank, -1.0)
-    info_ref[0:8] = place
-    info_ref[8:16] = jnp.concatenate(weights + [pad], axis=0)
+    told = [told_of(side, j, head, tok) for side, j in blocks]
+    wanted = [(*t, me) for t in told] + [(*told[i], mate) for i in kept]
+    place, weights = places_of(wanted, info_ref)
     share = []
     for i, (side, j) in enumerate(blocks):
         low = head + j * tok
         pick = picks(place[i : i + 1], cap)
         share.append(jnp.sum(pick * weights[i], axis=1, keepdims=True))
-        taken = jnp.dot(
-            pick.astype(BF16), side[low : low + tok], preferred_element_type=F32
-        )
+        taken = jnp.dot(pick.astype(BF16), side[low : low + tok], preferred_element_type=F32)
         rows_ref[i * cap : (i + 1) * cap] = taken.astype(BF16)
-    rows = rows_ref[...]
-    gate = jnp.dot(rows, w_gate[...], preferred_element_type=F32)
-    up = jnp.dot(rows, w_up[...], preferred_element_type=F32)
-    sig = jax.nn.sigmoid(gate)
-    act = gate * sig
-    hidden = (act * up).astype(BF16)
+    hidden, slope, act = hidden_of(rows_ref[...], w_gate, w_up)
     hidden_ref[...] = hidden
+    slope_ref[...] = slope
     act_ref[...] = act
-    slope_ref[...] = up * sig * (1.0 + gate * (1.0 - sig))
-    produced = contract_last(hidden, w_down[...]).astype(BF16).astype(F32)
-    split(kept, cap, (jnp.concatenate(share, axis=0) * produced).astype(BF16), keep_ref, give_ref)
+    if sums:
+        produced = contract_last(hidden, w_down[...]).astype(BF16).astype(F32)
+        split(kept, cap, (jnp.concatenate(share, axis=0) * produced).astype(BF16), *outs[5:])
+
+
+def pair_forward_body(cap, top, expert_ref, near, *refs):
+    weights, (info_ref, slope_ref, act_ref, out) = refs[:6], refs[6:]
+    head = 2 * top
+    tok = info_ref.shape[1]
+    told = told_of(near, 0, head, tok)
+    place, share = places_of([(*told, expert_ref[i].astype(F32)) for i in range(2)], info_ref)
+    pick = jnp.concatenate([picks(place[i : i + 1], cap) for i in range(2)], axis=0).astype(BF16)
+    rows = jnp.dot(pick, near[head : head + tok], preferred_element_type=F32).astype(BF16)
+    sent = []
+    for i in range(2):
+        w_gate, w_up, w_down = weights[3 * i : 3 * i + 3]
+        part = slice(i * cap, (i + 1) * cap)
+        hidden, slope_ref[part], act_ref[part] = hidden_of(rows[part], w_gate, w_up)
+        produced = contract_last(hidden, w_down[...]).astype(BF16).astype(F32)
+        column = jnp.sum(picks(place[i : i + 1], cap) * share[i], axis=1, keepdims=True)
+        sent.append((column * produced).astype(BF16))
+    out[...] = contract_first(pick, jnp.concatenate(sent, axis=0)).astype(BF16)
+
+
+def pair_backward_body(cap, info_ref, slope_ref, act_ref, near, *refs):
+    weights, out = refs[:6], refs[6]
+    pick = [picks(info_ref[i : i + 1], cap) for i in range(2)]
+    both = jnp.concatenate(pick, axis=0).astype(BF16)
+    taken = jnp.dot(both, near[...], preferred_element_type=F32)
+    sent = []
+    for i in range(2):
+        w_gate, w_up, w_down = weights[3 * i : 3 * i + 3]
+        part = slice(i * cap, (i + 1) * cap)
+        column = jnp.sum(pick[i] * info_ref[8 + i : 9 + i], axis=1, keepdims=True)
+        rows = (column * taken[part]).astype(BF16)
+        dhidden = jnp.dot(rows, w_down[...], preferred_element_type=F32)
+        dgate = (dhidden * slope_ref[part]).astype(BF16)
+        dup = (dhidden * act_ref[part]).astype(BF16)
+        back = contract_last(dgate, w_gate[...]) + contract_last(dup, w_up[...])
+        sent.append(back.astype(BF16))
+    out[...] = contract_first(both, jnp.concatenate(sent, axis=0)).astype(BF16)
 
 
 def split(kept, cap, rows, keep_ref, give_ref):
@@ -225,8 +280,8 @@
     second[...] = rows[cut:]
 
 
-def backward_body(cap, kept, info_ref, slope, act, near, far, w_gate, w_up, w_down, *outs):
-    rows_ref, dgate_ref, dup_ref, keep_ref, give_ref = outs
+def backward_body(cap, kept, sums, info_ref, slope, act, near, far, w_gate, w_up, w_down, *outs):
+    rows_ref, dgate_ref, dup_ref = outs[:3]
     tok = info_ref.shape[1]
     blocks = [(side, low) for side in (near, far) for low in range(0, side.shape[0], tok)]
     for i, (side, low) in enumerate(blocks):
@@ -239,8 +294,9 @@
     dup = (dhidden * act[...]).astype(BF16)
     dgate_ref[...] = dgate
     dup_ref[...] = dup
-    back = contract_last(dgate, w_gate[...]) + contract_last(dup, w_up[...])
-    split(kept, cap, back.astype(BF16), keep_ref, give_ref)
+    if sums:
+        back = contract_last(dgate, w_gate[...]) + contract_last(dup, w_up[...])
+        split(kept, cap, back.astype(BF16), *outs[3:])
 
 
 def return_body(cap, kept, count, info_ref, keep, give, *refs):
@@ -317,68 +373,76 @@
     def blocks_of(step):
         return (4, (2, 3)) if 0 < step < reach else (2, (0,))
 
+    forward, backward = {}, {}
+
     def run_forward(step):
         count, kept = blocks_of(step)
         m = count * cap
-        return call(
-            functools.partial(forward_body, cap, top, kept),
+        sums = step < reach
+        forward[step] = call(
+            f"forward_{step}",
+            functools.partial(forward_body, cap, top, kept, sums),
             [
                 struct((16, tok), F32),
                 struct((m, width), BF16),
                 struct((m, units), F32),
                 struct((m, units), F32),
                 struct((m, units), BF16),
-                struct((m // 2, width), BF16),
-                struct((m // 2, width), BF16),
-            ],
+            ]
+            + [struct((m // 2, width), BF16)] * 2 * sums,
             [expert, token_near[step], token_far[step], gate_w, up_w, down_w],
-            0,
             smem=1,
         )
+        return forward[step][4]
 
     def run_backward(step):
         count, kept = blocks_of(step)
         m = count * cap
+        sums = step < reach
         info, _, slope, act = forward[step][:4]
-        return call(
-            functools.partial(backward_body, cap, kept),
+        backward[step] = call(
+            f"backward_{step}",
+            functools.partial(backward_body, cap, kept, sums),
             [
                 struct((m, width), BF16),
                 struct((m, units), BF16),
                 struct((m, units), BF16),
-                struct((m // 2, width), BF16),
-                struct((m // 2, width), BF16),
-            ],
+            ]
+            + [struct((m // 2, width), BF16)] * 2 * sums,
             [info, slope, act, cot_near[step], cot_far[step], gate_w, up_w, down_w],
-            0,
         )
+        return backward[step][1]
+
+    def run_after(run, near, step, *others):
+        near[step] = after(near[step], *others)
+        return run(step)
 
     payload = call(
+        "payload",
         payload_body,
         [struct((head + tok, width), BF16)],
         [routes.T, combine.T, tokens],
-        0,
         scratch=[VMEM((top, tok), jnp.int32), VMEM((top, tok), F32), pltpu.SemaphoreType.DMA((3,))],
         far=True,
     )[0]
     staged = after((gate_w, up_w, down_w), payload)
     gate_w, up_w, down_w = call(
+        "stage",
         stage_body,
         [struct(w.shape, BF16) for w in staged],
         staged,
-        0,
         scratch=[pltpu.SemaphoreType.DMA((3,))],
         far=True,
     )
 
-    def join(arrived, top_rows):
+    def join(arrived, top_rows, name):
         if len(arrived) == 1:
             return arrived[0]
         return call(
+            name,
             functools.partial(join_body, top_rows, tok),
             [struct((top_rows + 2 * tok, width), BF16)],
             arrived,
-            0,
         )[0]
 
     def onward(near, step, top_rows, what):
@@ -386,37 +450,100 @@
             near = near[: top_rows + tok]
         return [hop(near, f"{what}_{step}")]
 
-    token_near, cot_near = [payload], [cotangent]
+    token_near, cot_near = {0: payload}, {0: cotangent}
     token_fly = [hop(payload, "tokens_1"), hop(payload, "tokens_1_crossing", crossing)]
-    token_far, cot_far = [swap(payload, "tokens_0_swap")], [swap(cotangent, "cotangent_0_swap")]
-    cot_fly = [hop(join([cotangent, cot_far[0]], 0), "cotangent_1")]
-    forward, backward = [], []
-    for step in range(1, reach + 1):
-        before = [b[1] for b in backward[-1:]] or [gate_w]
-        *arrived, token_near[-1] = land([*token_fly, token_near[-1]], *before)
-        token_near.append(join(arrived, head))
-        if step < reach:
-            token_fly = onward(token_near[-1], step + 1, head, "tokens")
-        token_far.append(swap(token_near[-1], f"tokens_{step}_swap"))
-        forward.append(run_forward(step - 1))
-        *arrived, cot_near[-1] = land([*cot_fly, cot_near[-1]], forward[-1][5])
-        cot_near.append(join(arrived, 0))
-        if step < reach:
-            cot_fly = onward(cot_near[-1], step + 1, 0, "cotangent")
-        cot_far.append(swap(cot_near[-1], f"cotangent_{step}_swap"))
-        if step < reach:
-            backward.append(run_backward(step - 1))
-    token_near[reach] = after(token_near[reach], cot_near[reach])
-    forward.append(run_forward(reach))
-    backward.append(run_backward(reach - 1))
-
-    def back_from(step, kept, given, values):
-        outs = {0: (tok,), 1: (tok, tok), reach: (tok,)}.get(step, (2 * tok,))
+    token_far = {0: swap(payload, "tokens_0_swap")}
+    cot_far = {0: swap(after(cotangent, payload), "cotangent_0_swap")}
+    if K["cot1"] == "join":
+        cot_fly = [hop(join([cotangent, cot_far[0]], 0, "join_0"), "cotangent_1")]
+    else:
+        late = after(cotangent, payload)
+        cot_fly = [hop(late, "cotangent_1"), hop(late, "cotangent_1_crossing", crossing)]
+
+    def mates(where):
+        return mate_w if K["mate"] == where else []
+
+    mate_w = []
+    for step in range(1, reach):
+        before = [backward[step - 2][1]] if step > 1 else [gate_w]
+        if step == 1 and K["far0"]:
+            before.append(token_far[0])
+        if K["force"] and step > 1:
+            before.append(cot_far[step - 1])
+        *arrived, token_near[step - 1] = land(
+            [*token_fly, token_near[step - 1]], *before, *mates(f"T{step}")
+        )
+        token_near[step] = join(arrived, head, "join_1")
+        token_fly = onward(token_near[step], step + 1, head, "tokens")
+        token_far[step] = swap(token_near[step], f"tokens_{step}_swap")
+        if step == 1:
+            first = {"T1": token_near[1], "P": payload, "T0": token_far[0]}[K["mate_after"]]
+            mate_w = [swap(after(w, first), "weights_swap") for w in (gate_w, up_w, down_w)]
+        before = [run_forward(step - 1)]
+        if step == reach - 1 and K["f3"] == "c3":
+            before.append(run_forward(step))
+        if K["force"]:
+            before.append(token_far[step])
+        *arrived, cot_near[step - 1] = land(
+            [*cot_fly, cot_near[step - 1]], *before, *mates(f"C{step}")
+        )
+        cot_near[step] = join(arrived, 0, "join_2")
+        cot_fly = onward(cot_near[step], step + 1, 0, "cotangent")
+        cot_far[step] = swap(cot_near[step], f"cotangent_{step}_swap")
+        if step < reach - 1:
+            run_backward(step - 1)
+
+    last = reach - 1
+    both_w = [gate_w, up_w, down_w, *mate_w]
+    before = []
+    if K["b2"] == "t4":
+        before.append(run_backward(last - 1))
+    if K["f3"] == "t4":
+        before.append(run_after(run_forward, token_near, last, cot_near[last]))
+    if K["force"]:
+        before.append(cot_far[last])
+    token_near[reach] = land(token_fly, *(before or [cot_near[last]]), *mates(f"T{reach}"))[0]
+    info, slope, act, mixed_left = call(
+        "pair_forward",
+        functools.partial(pair_forward_body, cap, top),
+        [
+            struct((16, tok), F32),
+            struct((2 * cap, units), F32),
+            struct((2 * cap, units), F32),
+            struct((tok, width), BF16),
+        ],
+        [expert, token_near[reach], *both_w],
+        smem=1,
+    )
+    mixed_left, mixed_fly = [mixed_left], [hop(mixed_left, f"mixed_{reach}")]
+    before = [mixed_left[0]]
+    if K["f3"] == "late":
+        before.append(run_after(run_forward, token_near, last, *mixed_left))
+    if K["b2"] == "c4":
+        before.append(run_after(run_backward, cot_near, last - 1, *mixed_left))
+    cot_near[reach] = land(cot_fly, *before)[0]
+    grad_left = call(
+        "pair_backward",
+        functools.partial(pair_backward_body, cap),
+        [struct((tok, width), BF16)],
+        [info, slope, act, cot_near[reach], *both_w],
+    )
+    grad_fly = [hop(grad_left[0], f"grad_{reach}")]
+    before = [*grad_left]
+    if K["f3"] == "y":
+        before.append(run_after(run_forward, token_near, last, *grad_left))
+    if K["b2"] == "m4":
+        before.append(run_after(run_backward, cot_near, last - 1, *grad_left))
+    if K["b3"] == "m4":
+        before.append(run_after(run_backward, cot_near, last, *grad_left))
+
+    def back_from(step, what, kept, given, values):
+        outs = {0: (tok,), 1: (tok, tok)}.get(step, (2 * tok,))
         return call(
+            f"{what}_sums_{step}",
             functools.partial(return_body, cap, blocks_of(step)[1], len(outs)),
             [struct((rows, width), BF16) for rows in outs],
             [forward[step][0], kept, given, *values],
-            0,
             near=step > 0,
         )
 
@@ -425,57 +552,67 @@
             return [hop(sums[0], what + "_1"), hop(sums[1], what + "_1_crossing", crossing_back)]
         return [hop(sums[0], f"{what}_{step}")]
 
-    def mixed_swap(step):
-        return swap(forward[step][6], f"mixed_{step}_swap")
-
-    def grad_swap(step):
-        return swap(backward[step][4], f"grad_{step}_swap")
-
-
-    def weight_grad(lefts, rights):
-        return call(
+    def mixed_back(step, values):
+        given = swap(forward[step][6], f"mixed_{step}_swap")
+        return back_from(step, "mixed", forward[step][5], given, values)
+
+    def grad_back(step, values):
+        given = swap(backward[step][4], f"grad_{step}_swap")
+        return back_from(step, "grad", backward[step][3], given, values)
+
+    grads = []
+
+    def some_job():
+        steps = range(reach + 1)
+        token_rows = [forward[i][1] for i in steps]
+        jobs = [
+            (token_rows, [backward[i][1] for i in steps]),
+            (token_rows, [backward[i][2] for i in steps]),
+            ([backward[i][0] for i in steps], [forward[i][4] for i in steps]),
+        ]
+        if len(grads) == len(jobs):
+            return []
+        lefts, rights = jobs[len(grads)]
+        grads.extend(call(
+            f"weights_{len(grads)}",
             functools.partial(weights_body, len(lefts), 256),
             [struct((width, units), BF16)],
             [*lefts, *rights],
-            0,
             near=False,
-        )[0]
-
-    mixed_kept = after(forward[reach][5], backward[reach - 1][1])
-    mixed_left = back_from(reach, mixed_kept, mixed_swap(reach), ())
-    mixed_fly = send_back(mixed_left, reach, "mixed")
-    cot_near[reach] = after(cot_near[reach], *mixed_left)
-    backward.append(run_backward(reach))
-    grad_left = back_from(reach, backward[reach][3], grad_swap(reach), ())
-    grad_fly = send_back(grad_left, reach, "grad")
-
-    token_rows = [f[1] for f in forward]
-    jobs = [
-        (token_rows, [b[1] for b in backward]),
-        (token_rows, [b[2] for b in backward]),
-        ([b[0] for b in backward], [f[4] for f in forward]),
-    ]
-    grads = []
-
-    def some_job():
-        if len(grads) < len(jobs):
-            grads.append(weight_grad(*jobs[len(grads)]))
-            return grads[-1:]
-        return []
-
-    for step in range(reach - 1, 0, -1):
-        arrived = land(mixed_fly, *grad_left, *(some_job() if step < reach - 1 else []))
-        mixed_left = back_from(step, forward[step][5], mixed_swap(step), arrived)
+        ))
+        return grads[-1:]
+
+    for step in range(last, 0, -1):
+        arrived = land(mixed_fly, *before)
+        mixed_left = mixed_back(step, arrived)
         mixed_fly = send_back(mixed_left, step, "mixed")
-        arrived = land(grad_fly, *mixed_left, *(some_job() if step < reach - 1 else []))
-        grad_left = back_from(step, backward[step][3], grad_swap(step), arrived)
+        before = [*mixed_left]
+        if step == last:
+            if K["b3"] == "m3":
+                before.append(run_after(run_backward, cot_near, last, *mixed_left))
+            if K["b2"] == "m3":
+                before.append(run_after(run_backward, cot_near, last - 1, *mixed_left))
+            token_near[reach] = after(token_near[reach], *mixed_left)
+            token_far[reach] = swap(token_near[reach], f"tokens_{reach}_swap")
+            cot_far[reach] = swap(after(cot_near[reach], *mixed_left), f"cotangent_{reach}_swap")
+        else:
+            before += some_job()
+        arrived = land(grad_fly, *before)
+        grad_left = grad_back(step, arrived)
         grad_fly = send_back(grad_left, step, "grad")
-    while len(grads) < len(jobs):
-        some_job()
-    arrived = land(mixed_fly, *grad_left, *grads)
-    mixed = back_from(0, forward[0][5], mixed_swap(0), arrived)[0]
+        before = [*grad_left]
+        if step == last:
+            if K["b2"] == "g3":
+                before.append(run_after(run_backward, cot_near, last - 1, *grad_left))
+            cot_near[reach] = after(cot_near[reach], *grad_left)
+            before += [run_forward(reach), run_backward(reach)]
+        before += some_job()
+    while some_job():
+        pass
+    arrived = land(mixed_fly, *before, *grads)
+    mixed = mixed_back(0, arrived)[0]
     arrived = land(grad_fly, mixed)
-    grad_tokens = back_from(0, backward[0][3], grad_swap(0), arrived)[0]
+    grad_tokens = grad_back(0, arrived)[0]
     return (mixed, grad_tokens, *[g[None] for g in grads])
 
 

time: 97.6 us -> 93.7 us (0.960)
  waiting for transfers between devices: 27.8 us -> 22.7 us
  Pallas kernels: 31.5 us -> 35.7 us
  starting transfers between devices: 37 us -> 33.9 us
    ppermute x39 -> x40, waiting for transfers between devices: 27.8 us -> 22.7 us  [hop(): return lax.ppermute(value, 'expert', moves)]
    pallas_call x27, Pallas kernels: 31.5 us -> 35.7 us  [call(): pl.pallas_call(body, out_shape=[pltpu.VMEM(a.shape, a.dtype) if near else...]
    ppermute x39 -> x40, starting transfers between devices: 37 us -> 33.9 us  [hop(): return lax.ppermute(value, 'expert', moves)]
  transfers between devices with their start and end apart: 39 -> 40, of which waited for: 18 -> 14; matrix products, arithmetic and copies ran while one was open for 0% -> 0% of each run, Pallas kernels for 30% -> 36%
where the time goes in v5:
time: 93.7 us; the launch traced here: 93.3 us
  Pallas kernels  35.7 us (38%)
  starting transfers between devices  33.9 us (36%)
  waiting for transfers between devices  22.7 us (24%)
    pallas_call x27, Pallas kernels, call(): pl.pallas_call(body, out_shape=[pltpu.VMEM(a.shape, a.dtype) if near else...  35.7 us
    ppermute x40, starting transfers between devices, hop(): return lax.ppermute(value, 'expert', moves)  33.9 us
    ppermute x40, waiting for transfers between devices, hop(): return lax.ppermute(value, 'expert', moves)  22.7 us
  transfers between devices with their start and end apart: 40, of which 14 were waited for; matrix products, arithmetic and copies ran while one was open for 0% of the time, Pallas kernels for 36%

profile of v5, /device:TPU:0, one launch (start us, length us, event | category | flops | bytes accessed | tf_op | source)
XLA Modules:
  0.0 93.3 jit_solution(11778530057620612093)
XLA Ops:
  1.7 3.1 %collective-permute-start = (bf16[144,1024]{1,0:T(8,128)(2,1)S(1)}, bf16[144,1024]{1,0:T(8,128)(2,1)S(1)}, u32[]{:S(2)}, u32[]{:S(2)}) collective-permute-start(bf16[144,1024]{1,0:T(8,128)(2,1)S(1)} %payload.1.near), channel_id=1, source_target_pairs={{0,4},{1,3},{4,8},{5,1},{8,12},{9,5},{12,14},{13,9},{14,10},{15,13... | collective-permute-start | bytes 884744 | tf_op jit(solution)/shard_map/tokens_1/ppermute | solution.py:355
  6.5 1.6 %stage.1 = (bf16[1024,384]{1,0:T(8,128)(2,1)S(1)}, bf16[1024,384]{1,0:T(8,128)(2,1)S(1)}, bf16[1024,384]{1,0:T(8,128)(2,1)S(1)}) custom-call(bf16[1024,384]{1,0:T(8,128)(2,1)} %bitcast.15, bf16[1024,384]{1,0:T(8,128)(2,1)} %bitcast.16, bf16[1024,384]{1,0:T(8,128)(2,1)} %bitcast.17), custom_call_target="tpu_custom_call" | custom-call | flops 1073741824 | bytes 1024 | tf_op jit(solution)/shard_map/stage/pallas_call | solution.py:108
  13.4 2.3 %collective-permute-start.4 = (bf16[272,1024]{1,0:T(8,128)(2,1)}, bf16[272,1024]{1,0:T(8,128)(2,1)}, u32[]{:S(2)}, u32[]{:S(2)}) collective-permute-start(bf16[272,1024]{1,0:T(8,128)(2,1)} %join_1.1.near), channel_id=1, source_target_pairs={{0,4},{1,3},{4,8},{5,1},{8,12},{9,5},{12,14},{13,9},{14,10},{15,13... | collective-permute-start | bytes 1671176 | tf_op jit(solution)/shard_map/tokens_2/ppermute | solution.py:355
  16.3 2.0 %forward_0.1 = (f32[16,128]{1,0:T(8,128)S(1)}, bf16[128,1024]{1,0:T(8,128)(2,1)S(1)}, f32[128,384]{1,0:T(8,128)S(1)}, f32[128,384]{1,0:T(8,128)S(1)}, bf16[128,3...) custom-call(s32[2]{0:T(128)S(1)} %pad_add_fusion.expert_ref, ...), custom_call_target="tpu_custom_call" | custom-call | flops 2147483648 | bytes 1024 | tf_op jit(solution)/shard_map/forward_0/pallas_call | solution.py:108
  18.5 1.9 %collective-permute-start.10 = (bf16[256,1024]{1,0:T(8,128)(2,1)}, bf16[256,1024]{1,0:T(8,128)(2,1)S(1)}, u32[]{:S(2)}, u32[]{:S(2)}) collective-permute-start(bf16[256,1024]{1,0:T(8,128)(2,1)} %collective-permute-done.6.near), channel_id=1, source_target_pairs={{0,4},{1,3},{4,8},{5,1},{8,12},{9,5},{12,14},{13,9},{14,10},{15,13... | collective-permute-start | bytes 1572872 | tf_op jit(solution)/shard_map/cotangent_2/ppermute | solution.py:355
  20.4 4.1 %collective-permute-done.4.near = bf16[272,1024]{1,0:T(8,128)(2,1)} collective-permute-done((bf16[272,1024]{1,0:T(8,128)(2,1)}, bf16[272,1024]{1,0:T(8,128)(2,1)}, u32[]{:S(2)}, u32[]{:S(2)}) %collective-permute-start.4) | collective-permute-done | bytes 557088 | tf_op jit(solution)/shard_map/tokens_2/ppermute | solution.py:355
  26.0 1.9 %collective-permute-start.9 = (bf16[272,1024]{1,0:T(8,128)(2,1)}, bf16[272,1024]{1,0:T(8,128)(2,1)S(1)}, u32[]{:S(2)}, u32[]{:S(2)}) collective-permute-start(bf16[272,1024]{1,0:T(8,128)(2,1)} %collective-permute-done.4.near), channel_id=1, source_target_pairs={{0,4},{1,3},{4,8},{5,1},{8,12},{9,5},{12,14},{13,9},{14,10},{15,13... | collective-permute-start | bytes 1671176 | tf_op jit(solution)/shard_map/tokens_3/ppermute | solution.py:355
  28.0 2.0 %collective-permute-done.10.near = bf16[256,1024]{1,0:T(8,128)(2,1)S(1)} collective-permute-done((bf16[256,1024]{1,0:T(8,128)(2,1)}, bf16[256,1024]{1,0:T(8,128)(2,1)S(1)}, u32[]{:S(2)}, u32[]{:S(2)}) %collective-permute-start.10) | collective-permute-done | bytes 524320 | tf_op jit(solution)/shard_map/cotangent_2/ppermute | solution.py:355
  30.0 2.7 %forward_1.1 = (f32[16,128]{1,0:T(8,128)S(1)}, bf16[256,1024]{1,0:T(8,128)(2,1)S(1)}, f32[256,384]{1,0:T(8,128)S(1)}, f32[256,384]{1,0:T(8,128)S(1)}, bf16[256,3...) custom-call(s32[2]{0:T(128)S(1)} %pad_add_fusion.expert_ref, ...), custom_call_target="tpu_custom_call" | custom-call | flops 1048576 | bytes 1024 | tf_op jit(solution)/shard_map/forward_1/pallas_call | solution.py:108
  32.7 1.9 %collective-permute-start.17 = (bf16[256,1024]{1,0:T(8,128)(2,1)S(1)}, bf16[256,1024]{1,0:T(8,128)(2,1)S(1)}, u32[]{:S(2)}, u32[]{:S(2)}) collective-permute-start(bf16[256,1024]{1,0:T(8,128)(2,1)S(1)} %collective-permute-done.10.near), channel_id=1, source_target_pairs={{0,4},{1,3},{4,8},{5,1},{8,12},{9,5},{12,14},{13,9},{14,10},{15,13... | collective-permute-start | bytes 1572872 | tf_op jit(solution)/shard_map/cotangent_3/ppermute | solution.py:355
  34.6 2.3 %backward_1.1 = (bf16[256,1024]{1,0:T(8,128)(2,1)S(1)}, bf16[256,384]{1,0:T(8,128)(2,1)S(1)}, bf16[256,384]{1,0:T(8,128)(2,1)S(1)}, bf16[128,1024]{1,0:T(8,128)(2,1)S(1)}, bf16[128,1024]{1,0:T(8,128)(2,1)S(1)}) custom-call(f32[16,128]{1,0:T(8,128)S(1)} %get-tuple-element.129.info_ref, f32[256,384]{1,0:T(8,128)S(1)} %get-tuple-element.133.slope, ...), custom_call_target="tpu_custom_call" | custom-call | flops 1073741824 | bytes 1024 | tf_op jit(solution)/shard_map/backward_1/pallas_call | solution.py:108
  38.7 2.5 %forward_2.1 = (f32[16,128]{1,0:T(8,128)S(1)}, bf16[256,1024]{1,0:T(8,128)(2,1)S(1)}, f32[256,384]{1,0:T(8,128)S(1)}, f32[256,384]{1,0:T(8,128)S(1)}, bf16[256,3...) custom-call(s32[2]{0:T(128)S(1)} %pad_add_fusion.expert_ref, ...), custom_call_target="tpu_custom_call" | custom-call | flops 2147483648 | bytes 1024 | tf_op jit(solution)/shard_map/forward_2/pallas_call | solution.py:108
  42.4 1.9 %collective-permute-start.22 = (bf16[128,1024]{1,0:T(8,128)(2,1)S(1)}, bf16[128,1024]{1,0:T(8,128)(2,1)S(1)}, u32[]{:S(2)}, u32[]{:S(2)}) collective-permute-start(bf16[128,1024]{1,0:T(8,128)(2,1)S(1)} %slice.7), channel_id=1, source_target_pairs={{0,4},{1,3},{4,8},{5,1},{8,12},{9,5},{12,14},{13,9},{14,10},{15,13... | collective-permute-start | bytes 786440 | tf_op jit(solution)/shard_map/cotangent_4/ppermute | solution.py:355
  44.4 2.0 %forward_3.1 = (f32[16,128]{1,0:T(8,128)S(1)}, bf16[256,1024]{1,0:T(8,128)(2,1)S(1)}, f32[256,384]{1,0:T(8,128)S(1)}, f32[256,384]{1,0:T(8,128)S(1)}, bf16[256,3...) custom-call(s32[2]{0:T(128)S(1)} %pad_add_fusion.expert_ref, ...), custom_call_target="tpu_custom_call" | custom-call | flops 1048576 | bytes 1024 | tf_op jit(solution)/shard_map/forward_3/pallas_call | solution.py:108
  46.3 2.2 %pair_forward.1 = (f32[16,128]{1,0:T(8,128)S(1)}, f32[128,384]{1,0:T(8,128)S(1)}, f32[128,384]{1,0:T(8,128)S(1)}, bf16[128,1024]{1,0:T(8,128)(2,1)S(1)}) custom-call(s32[2]{0:T(128)S(1)} %pad_add_fusion.expert_ref, bf16[144,1024]{1,0:T(8,128)(2,1)S(1)} %collective-permute-done.20.near, bf16[1024,384]{1,0:T(8,128)(2,1)S(1)} %get-tuple-element.139.w_gate.refs_0_, ...), custom_call_target="tpu_custom_call" | custom-call | flops 1073741824 | bytes 1024 | tf_op jit(solution)/shard_map/pair_forward/pallas_call | solution.py:108
  48.5 1.6 %collective-permute-start.21 = (bf16[128,1024]{1,0:T(8,128)(2,1)S(1)}, bf16[128,1024]{1,0:T(8,128)(2,1)S(1)}, u32[]{:S(2)}, u32[]{:S(2)}) collective-permute-start(bf16[128,1024]{1,0:T(8,128)(2,1)S(1)} %get-tuple-element.156), channel_id=1, source_target_pairs={{0,4},{1,3},{4,8},{5,1},{8,12},{9,5},{12,14},{13,9},{14,10},{15,13... | collective-permute-start | bytes 786440 | tf_op jit(solution)/shard_map/mixed_4/ppermute | solution.py:355
  50.1 1.8 %pair_backward.1 = bf16[128,1024]{1,0:T(8,128)(2,1)S(1)} custom-call(f32[16,128]{1,0:T(8,128)S(1)} %get-tuple-element.157.info_ref, f32[128,384]{1,0:T(8,128)S(1)} %get-tuple-element.158.slope_ref, f32[128,384]{1,0:T(8,128)S(1)} %get-tuple-element.159.act_ref, bf16[128,1024]{1,0:T(8,128)(2,1)S(1)} %collective-permute-done.22.near, ...), custom_call_target="tpu_custom_call" | custom-call | flops 1048576 | bytes 1024 | tf_op jit(solution)/shard_map/pair_backward/pallas_call | solution.py:108
  62.8 2.2 %weights_0.1 = bf16[1024,384]{1,0:T(8,128)(2,1)} custom-call(bf16[128,1024]{1,0:T(8,128)(2,1)S(1)} %get-tuple-element.182.refs_0_, bf16[256,1024]{1,0:T(8,128)(2,1)S(1)} %get-tuple-element.183.refs_1_, bf16[256,1024]{1,0:T(8,128)(2,1)S(1)} %get-tuple-element.184.refs_2_, bf16[256,1024]{1,0:T(8,128)(2,1)S(1)} %get-tuple-element.185.refs_3_, ...), custom_call_target="tpu_custom_call" | custom-call | flops 1048576 | bytes 1024 | tf_op jit(solution)/shard_map/weights_0/pallas_call | solution.py:108
  66.8 2.2 %weights_1.1 = bf16[1024,384]{1,0:T(8,128)(2,1)} custom-call(bf16[128,1024]{1,0:T(8,128)(2,1)S(1)} %get-tuple-element.182.refs_0_, bf16[256,1024]{1,0:T(8,128)(2,1)S(1)} %get-tuple-element.183.refs_1_, bf16[256,1024]{1,0:T(8,128)(2,1)S(1)} %get-tuple-element.184.refs_2_, bf16[256,1024]{1,0:T(8,128)(2,1)S(1)} %get-tuple-element.185.refs_3_, ...), custom_call_target="tpu_custom_call" | custom-call | flops 1048576 | bytes 1024 | tf_op jit(solution)/shard_map/weights_1/pallas_call | solution.py:108
  72.9 2.2 %weights_2.1 = bf16[1024,384]{1,0:T(8,128)(2,1)} custom-call(bf16[128,1024]{1,0:T(8,128)(2,1)S(1)} %get-tuple-element.196.refs_0_, bf16[256,1024]{1,0:T(8,128)(2,1)S(1)} %get-tuple-element.197.refs_1_, bf16[256,1024]{1,0:T(8,128)(2,1)S(1)} %get-tuple-element.198.refs_2_, bf16[256,1024]{1,0:T(8,128)(2,1)S(1)} %get-tuple-element.199.refs_3_, ...), custom_call_target="tpu_custom_call" | custom-call | flops 1048576 | bytes 1024 | tf_op jit(solution)/shard_map/weights_2/pallas_call | solution.py:108
  78.0 3.9 %collective-permute-done.36.refs_0_ = bf16[256,1024]{1,0:T(8,128)(2,1)S(1)} collective-permute-done((bf16[256,1024]{1,0:T(8,128)(2,1)S(1)}, bf16[256,1024]{1,0:T(8,128)(2,1)S(1)}, u32[]{:S(2)}, u32[]{:S(2)}) %collective-permute-start.36) | collective-permute-done | bytes 524320 | tf_op jit(solution)/shard_map/grad_2/ppermute | solution.py:355
  84.7 2.1 %collective-permute-done.34.refs_1_ = bf16[128,1024]{1,0:T(8,128)(2,1)S(1)} collective-permute-done((bf16[128,1024]{1,0:T(8,128)(2,1)S(1)}, bf16[128,1024]{1,0:T(8,128)(2,1)S(1)}, u32[]{:S(2)}, u32[]{:S(2)}) %collective-permute-start.34) | collective-permute-done | bytes 262176 | tf_op jit(solution)/shard_map/mixed_1_crossing/ppermute | solution.py:355
  87.7 2.6 %collective-permute-done.38.refs_0_ = bf16[128,1024]{1,0:T(8,128)(2,1)S(1)} collective-permute-done((bf16[128,1024]{1,0:T(8,128)(2,1)S(1)}, bf16[128,1024]{1,0:T(8,128)(2,1)S(1)}, u32[]{:S(2)}, u32[]{:S(2)}) %collective-permute-start.38) | collective-permute-done | bytes 262176 | tf_op jit(solution)/shard_map/grad_1/ppermute | solution.py:355
  90.3 2.1 %collective-permute-done.39.refs_1_ = bf16[128,1024]{1,0:T(8,128)(2,1)S(1)} collective-permute-done((bf16[128,1024]{1,0:T(8,128)(2,1)S(1)}, bf16[128,1024]{1,0:T(8,128)(2,1)S(1)}, u32[]{:S(2)}, u32[]{:S(2)}) %collective-permute-start.39) | collective-permute-done | bytes 262176 | tf_op jit(solution)/shard_map/grad_1_crossing/ppermute | solution.py:355
  (94 shorter events, 37.3 us)
Async XLA Ops:
  1.7 9.5 %collective-permute-start = (bf16[144,1024]{1,0:T(8,128)(2,1)S(1)}, bf16[144,1024]{1,0:T(8,128)(2,1)S(1)}, u32[]{:S(2)}, u32[]{:S(2)}) collective-permute-start(bf16[144,1024]{1,0:T(8,128)(2,1)S(1)} %payload.1.near), channel_id=1, source_target_pairs={{0,4},{1,3},{4,8},{5,1},{8,12},{9,5},{12,14},{13,9},{14,10},{15,13... | collective-permute-start | bytes 884744 | tf_op jit(solution)/shard_map/tokens_1/ppermute | solution.py:355
  6.5 9.8 %collective-permute-start.2 = (bf16[144,1024]{1,0:T(8,128)(2,1)S(1)}, bf16[144,1024]{1,0:T(8,128)(2,1)}, u32[]{:S(2)}, u32[]{:S(2)}) collective-permute-start(bf16[144,1024]{1,0:T(8,128)(2,1)S(1)} %payload.1.near), channel_id=1, source_target_pairs={{0,1},{1,0},{2,3},{3,2},{4,5},{5,4},{6,7},{7,6},{8,9},{9,8},{10,11... | collective-permute-start | bytes 884744 | tf_op jit(solution)/shard_map/tokens_0_swap/ppermute | solution.py:355
  9.0 9.5 %collective-permute-start.6 = (bf16[256,1024]{1,0:T(8,128)(2,1)}, bf16[256,1024]{1,0:T(8,128)(2,1)}, u32[]{:S(2)}, u32[]{:S(2)}) collective-permute-start(bf16[256,1024]{1,0:T(8,128)(2,1)} %join_0.1), channel_id=1, source_target_pairs={{0,4},{1,3},{4,8},{5,1},{8,12},{9,5},{12,14},{13,9},{14,10},{15,13... | collective-permute-start | bytes 1572872 | tf_op jit(solution)/shard_map/cotangent_1/ppermute | solution.py:355
  13.4 11.1 %collective-permute-start.4 = (bf16[272,1024]{1,0:T(8,128)(2,1)}, bf16[272,1024]{1,0:T(8,128)(2,1)}, u32[]{:S(2)}, u32[]{:S(2)}) collective-permute-start(bf16[272,1024]{1,0:T(8,128)(2,1)} %join_1.1.near), channel_id=1, source_target_pairs={{0,4},{1,3},{4,8},{5,1},{8,12},{9,5},{12,14},{13,9},{14,10},{15,13... | collective-permute-start | bytes 1671176 | tf_op jit(solution)/shard_map/tokens_2/ppermute | solution.py:355
  15.7 10.3 %collective-permute-start.12 = (bf16[1024,384]{1,0:T(8,128)(2,1)S(1)}, bf16[1024,384]{1,0:T(8,128)(2,1)S(1)}, u32[]{:S(2)}, u32[]{:S(2)}) collective-permute-start(bf16[1024,384]{1,0:T(8,128)(2,1)S(1)} %get-tuple-element.139.w_gate.refs_0_), channel_id=1, source_target_pairs={{0,1},{1,0},{2,3},{3,2},{4,5},{5,4},{6,7},{7,6},{8,9},{9,8},{10,11... | collective-permute-start | bytes 2359304 | tf_op jit(solution)/shard_map/weights_swap/ppermute | solution.py:355
  15.7 8.7 %collective-permute-start.7 = (bf16[272,1024]{1,0:T(8,128)(2,1)}, bf16[272,1024]{1,0:T(8,128)(2,1)}, u32[]{:S(2)}, u32[]{:S(2)}) collective-permute-start(bf16[272,1024]{1,0:T(8,128)(2,1)} %join_1.1.near), channel_id=1, source_target_pairs={{0,1},{1,0},{2,3},{3,2},{4,5},{5,4},{6,7},{7,6},{8,9},{9,8},{10,11... | collective-permute-start | bytes 1671176 | tf_op jit(solution)/shard_map/tokens_1_swap/ppermute | solution.py:355
  18.5 11.5 %collective-permute-start.10 = (bf16[256,1024]{1,0:T(8,128)(2,1)}, bf16[256,1024]{1,0:T(8,128)(2,1)S(1)}, u32[]{:S(2)}, u32[]{:S(2)}) collective-permute-start(bf16[256,1024]{1,0:T(8,128)(2,1)} %collective-permute-done.6.near), channel_id=1, source_target_pairs={{0,4},{1,3},{4,8},{5,1},{8,12},{9,5},{12,14},{13,9},{14,10},{15,13... | collective-permute-start | bytes 1572872 | tf_op jit(solution)/shard_map/cotangent_2/ppermute | solution.py:355
  20.4 16.5 %collective-permute-start.13 = (bf16[1024,384]{1,0:T(8,128)(2,1)S(1)}, bf16[1024,384]{1,0:T(8,128)(2,1)S(1)}, u32[]{:S(2)}, u32[]{:S(2)}) collective-permute-start(bf16[1024,384]{1,0:T(8,128)(2,1)S(1)} %get-tuple-element.140.w_up.refs_1_), channel_id=1, source_target_pairs={{0,1},{1,0},{2,3},{3,2},{4,5},{5,4},{6,7},{7,6},{8,9},{9,8},{10,11... | collective-permute-start | bytes 2359304 | tf_op jit(solution)/shard_map/weights_swap/ppermute | solution.py:355
  24.5 12.5 %collective-permute-start.14 = (bf16[1024,384]{1,0:T(8,128)(2,1)S(1)}, bf16[1024,384]{1,0:T(8,128)(2,1)S(1)}, u32[]{:S(2)}, u32[]{:S(2)}) collective-permute-start(bf16[1024,384]{1,0:T(8,128)(2,1)S(1)} %get-tuple-element.141.w_down.refs_2_), channel_id=1, source_target_pairs={{0,1},{1,0},{2,3},{3,2},{4,5},{5,4},{6,7},{7,6},{8,9},{9,8},{10,11... | collective-permute-start | bytes 2359304 | tf_op jit(solution)/shard_map/weights_swap/ppermute | solution.py:355
  24.5 8.2 %collective-permute-start.11 = (bf16[256,1024]{1,0:T(8,128)(2,1)}, bf16[256,1024]{1,0:T(8,128)(2,1)S(1)}, u32[]{:S(2)}, u32[]{:S(2)}) collective-permute-start(bf16[256,1024]{1,0:T(8,128)(2,1)} %collective-permute-done.6.near), channel_id=1, source_target_pairs={{0,1},{1,0},{2,3},{3,2},{4,5},{5,4},{6,7},{7,6},{8,9},{9,8},{10,11... | collective-permute-start | bytes 1572872 | tf_op jit(solution)/shard_map/cotangent_1_swap/ppermute | solution.py:355
  26.0 10.9 %collective-permute-start.9 = (bf16[272,1024]{1,0:T(8,128)(2,1)}, bf16[272,1024]{1,0:T(8,128)(2,1)S(1)}, u32[]{:S(2)}, u32[]{:S(2)}) collective-permute-start(bf16[272,1024]{1,0:T(8,128)(2,1)} %collective-permute-done.4.near), channel_id=1, source_target_pairs={{0,4},{1,3},{4,8},{5,1},{8,12},{9,5},{12,14},{13,9},{14,10},{15,13... | collective-permute-start | bytes 1671176 | tf_op jit(solution)/shard_map/tokens_3/ppermute | solution.py:355
  30.0 8.7 %collective-permute-start.15 = (bf16[272,1024]{1,0:T(8,128)(2,1)}, bf16[272,1024]{1,0:T(8,128)(2,1)S(1)}, u32[]{:S(2)}, u32[]{:S(2)}) collective-permute-start(bf16[272,1024]{1,0:T(8,128)(2,1)} %collective-permute-done.4.near), channel_id=1, source_target_pairs={{0,1},{1,0},{2,3},{3,2},{4,5},{5,4},{6,7},{7,6},{8,9},{9,8},{10,11... | collective-permute-start | bytes 1671176 | tf_op jit(solution)/shard_map/tokens_2_swap/ppermute | solution.py:355
  32.7 9.2 %collective-permute-start.17 = (bf16[256,1024]{1,0:T(8,128)(2,1)S(1)}, bf16[256,1024]{1,0:T(8,128)(2,1)S(1)}, u32[]{:S(2)}, u32[]{:S(2)}) collective-permute-start(bf16[256,1024]{1,0:T(8,128)(2,1)S(1)} %collective-permute-done.10.near), channel_id=1, source_target_pairs={{0,4},{1,3},{4,8},{5,1},{8,12},{9,5},{12,14},{13,9},{14,10},{15,13... | collective-permute-start | bytes 1572872 | tf_op jit(solution)/shard_map/cotangent_3/ppermute | solution.py:355
  37.2 9.2 %collective-permute-start.20 = (bf16[144,1024]{1,0:T(8,128)(2,1)S(1)}, bf16[144,1024]{1,0:T(8,128)(2,1)S(1)}, u32[]{:S(2)}, u32[]{:S(2)}) collective-permute-start(bf16[144,1024]{1,0:T(8,128)(2,1)S(1)} %slice.6), channel_id=1, source_target_pairs={{0,4},{1,3},{4,8},{5,1},{8,12},{9,5},{12,14},{13,9},{14,10},{15,13... | collective-permute-start | bytes 884744 | tf_op jit(solution)/shard_map/tokens_4/ppermute | solution.py:355
  41.9 11.6 %collective-permute-start.23 = (bf16[256,1024]{1,0:T(8,128)(2,1)S(1)}, bf16[256,1024]{1,0:T(8,128)(2,1)S(1)}, u32[]{:S(2)}, u32[]{:S(2)}) collective-permute-start(bf16[256,1024]{1,0:T(8,128)(2,1)S(1)} %collective-permute-done.17.near), channel_id=1, source_target_pairs={{0,1},{1,0},{2,3},{3,2},{4,5},{5,4},{6,7},{7,6},{8,9},{9,8},{10,11... | collective-permute-start | bytes 1572872 | tf_op jit(solution)/shard_map/cotangent_3_swap/ppermute | solution.py:355
  41.9 15.3 %collective-permute-start.27 = (bf16[256,1024]{1,0:T(8,128)(2,1)S(1)}, bf16[256,1024]{1,0:T(8,128)(2,1)S(1)}, u32[]{:S(2)}, u32[]{:S(2)}) collective-permute-start(bf16[256,1024]{1,0:T(8,128)(2,1)S(1)} %collective-permute-done.10.near), channel_id=1, source_target_pairs={{0,1},{1,0},{2,3},{3,2},{4,5},{5,4},{6,7},{7,6},{8,9},{9,8},{10,11... | collective-permute-start | bytes 1572872 | tf_op jit(solution)/shard_map/cotangent_2_swap/ppermute | solution.py:355
  55.8 9.2 %collective-permute-start.24 = (bf16[256,1024]{1,0:T(8,128)(2,1)S(1)}, bf16[256,1024]{1,0:T(8,128)(2,1)S(1)}, u32[]{:S(2)}, u32[]{:S(2)}) collective-permute-start(bf16[256,1024]{1,0:T(8,128)(2,1)S(1)} %mixed_sums_3.1), channel_id=1, source_target_pairs={{0,4},{1,3},{4,8},{5,1},{8,12},{9,5},{12,14},{13,9},{14,10},{15,13... | collective-permute-start | bytes 1572872 | tf_op jit(solution)/shard_map/mixed_3/ppermute | solution.py:355
  58.8 11.8 %collective-permute-start.32 = (bf16[256,1024]{1,0:T(8,128)(2,1)S(1)}, bf16[256,1024]{1,0:T(8,128)(2,1)S(1)}, u32[]{:S(2)}, u32[]{:S(2)}) collective-permute-start(bf16[256,1024]{1,0:T(8,128)(2,1)S(1)} %grad_sums_3.1), channel_id=1, source_target_pairs={{0,4},{1,3},{4,8},{5,1},{8,12},{9,5},{12,14},{13,9},{14,10},{15,13... | collective-permute-start | bytes 1572872 | tf_op jit(solution)/shard_map/grad_3/ppermute | solution.py:355
  60.9 9.7 %collective-permute-start.31 = (bf16[128,1024]{1,0:T(8,128)(2,1)S(1)}, bf16[128,1024]{1,0:T(8,128)(2,1)S(1)}, u32[]{:S(2)}, u32[]{:S(2)}) collective-permute-start(bf16[128,1024]{1,0:T(8,128)(2,1)S(1)} %get-tuple-element.189), channel_id=1, source_target_pairs={{0,1},{1,0},{2,3},{3,2},{4,5},{5,4},{6,7},{7,6},{8,9},{9,8},{10,11... | collective-permute-start | bytes 786440 | tf_op jit(solution)/shard_map/grad_2_swap/ppermute | solution.py:355
  65.4 10.9 %collective-permute-start.30 = (bf16[256,1024]{1,0:T(8,128)(2,1)S(1)}, bf16[256,1024]{1,0:T(8,128)(2,1)S(1)}, u32[]{:S(2)}, u32[]{:S(2)}) collective-permute-start(bf16[256,1024]{1,0:T(8,128)(2,1)S(1)} %mixed_sums_2.1), channel_id=1, source_target_pairs={{0,4},{1,3},{4,8},{5,1},{8,12},{9,5},{12,14},{13,9},{14,10},{15,13... | collective-permute-start | bytes 1572872 | tf_op jit(solution)/shard_map/mixed_2/ppermute | solution.py:355
  71.0 10.9 %collective-permute-start.36 = (bf16[256,1024]{1,0:T(8,128)(2,1)S(1)}, bf16[256,1024]{1,0:T(8,128)(2,1)S(1)}, u32[]{:S(2)}, u32[]{:S(2)}) collective-permute-start(bf16[256,1024]{1,0:T(8,128)(2,1)S(1)} %grad_sums_2.1), channel_id=1, source_target_pairs={{0,4},{1,3},{4,8},{5,1},{8,12},{9,5},{12,14},{13,9},{14,10},{15,13... | collective-permute-start | bytes 1572872 | tf_op jit(solution)/shard_map/grad_2/ppermute | solution.py:355
  72.4 9.5 %collective-permute-start.35 = (bf16[128,1024]{1,0:T(8,128)(2,1)S(1)}, bf16[128,1024]{1,0:T(8,128)(2,1)S(1)}, u32[]{:S(2)}, u32[]{:S(2)}) collective-permute-start(bf16[128,1024]{1,0:T(8,128)(2,1)S(1)} %get-tuple-element.205), channel_id=1, source_target_pairs={{0,1},{1,0},{2,3},{3,2},{4,5},{5,4},{6,7},{7,6},{8,9},{9,8},{10,11... | collective-permute-start | bytes 786440 | tf_op jit(solution)/shard_map/grad_1_swap/ppermute | solution.py:355
  78.0 8.8 %collective-permute-start.34 = (bf16[128,1024]{1,0:T(8,128)(2,1)S(1)}, bf16[128,1024]{1,0:T(8,128)(2,1)S(1)}, u32[]{:S(2)}, u32[]{:S(2)}) collective-permute-start(bf16[128,1024]{1,0:T(8,128)(2,1)S(1)} %get-tuple-element.203), channel_id=1, source_target_pairs={{0,5},{1,2},{4,9},{5,0},{8,13},{9,4},{12,15},{13,8},{14,11},{15,12... | collective-permute-start | bytes 786440 | tf_op jit(solution)/shard_map/mixed_1_crossing/ppermute | solution.py:355
  83.6 8.8 %collective-permute-start.39 = (bf16[128,1024]{1,0:T(8,128)(2,1)S(1)}, bf16[128,1024]{1,0:T(8,128)(2,1)S(1)}, u32[]{:S(2)}, u32[]{:S(2)}) collective-permute-start(bf16[128,1024]{1,0:T(8,128)(2,1)S(1)} %get-tuple-element.208), channel_id=1, source_target_pairs={{0,5},{1,2},{4,9},{5,0},{8,13},{9,4},{12,15},{13,8},{14,11},{15,12... | collective-permute-start | bytes 786440 | tf_op jit(solution)/shard_map/grad_1_crossing/ppermute | solution.py:355
  (20 other events, 113.1 us)

commit v6 on v5

--- a/solution.py
+++ b/solution.py
@@ -95,8 +95,22 @@
 LIMIT = 14 * 1024 * 1024
 
 
-K = {'far0': 0, 'mate': 'T3', 'mate_after': 'T1', 'f3': 't4', 'b2': 'm3', 'b3': 'm4', 'force': 0, 'cot1': 'join'}
-COST = {'pair_forward': 30, 'forward_0': 31, 'forward_4': 32, 'backward_0': 31, 'grad_sums_0': 29, 'forward_2': 31, 'grad_sums_1': 30, 'stage': 30, 'mixed_sums_2': 29, 'backward_1': 30, 'join_1': 30}
+COST = {
+    "pair_forward": 30,
+    "forward_0": 32,
+    "backward_0": 31,
+    "grad_sums_0": 29,
+    "forward_2": 32,
+    "grad_sums_1": 30,
+    "stage": 30,
+    "pair_backward": 28,
+    "mixed_sums_2": 29,
+    "backward_1": 30,
+    "join_1": 30,
+    "grad_sums_2": 28,
+    "payload": 31,
+    "mixed_sums_3": 32,
+}
 
 
 def call(name, body, outs, operands, smem=0, scratch=(), near=True, far=False):
@@ -454,39 +468,20 @@
     token_fly = [hop(payload, "tokens_1"), hop(payload, "tokens_1_crossing", crossing)]
     token_far = {0: swap(payload, "tokens_0_swap")}
     cot_far = {0: swap(after(cotangent, payload), "cotangent_0_swap")}
-    if K["cot1"] == "join":
-        cot_fly = [hop(join([cotangent, cot_far[0]], 0, "join_0"), "cotangent_1")]
-    else:
-        late = after(cotangent, payload)
-        cot_fly = [hop(late, "cotangent_1"), hop(late, "cotangent_1_crossing", crossing)]
-
-    def mates(where):
-        return mate_w if K["mate"] == where else []
-
+    cot_fly = [hop(join([cotangent, cot_far[0]], 0, "join_0"), "cotangent_1")]
     mate_w = []
     for step in range(1, reach):
         before = [backward[step - 2][1]] if step > 1 else [gate_w]
-        if step == 1 and K["far0"]:
-            before.append(token_far[0])
-        if K["force"] and step > 1:
-            before.append(cot_far[step - 1])
         *arrived, token_near[step - 1] = land(
-            [*token_fly, token_near[step - 1]], *before, *mates(f"T{step}")
+            [*token_fly, token_near[step - 1]], *before, *(mate_w if step == 3 else [])
         )
         token_near[step] = join(arrived, head, "join_1")
         token_fly = onward(token_near[step], step + 1, head, "tokens")
         token_far[step] = swap(token_near[step], f"tokens_{step}_swap")
         if step == 1:
-            first = {"T1": token_near[1], "P": payload, "T0": token_far[0]}[K["mate_after"]]
-            mate_w = [swap(after(w, first), "weights_swap") for w in (gate_w, up_w, down_w)]
-        before = [run_forward(step - 1)]
-        if step == reach - 1 and K["f3"] == "c3":
-            before.append(run_forward(step))
-        if K["force"]:
-            before.append(token_far[step])
-        *arrived, cot_near[step - 1] = land(
-            [*cot_fly, cot_near[step - 1]], *before, *mates(f"C{step}")
-        )
+            mate_w = [swap(after(w, token_near[1]), "weights_swap") for w in (gate_w, up_w, down_w)]
+        done = run_forward(step - 1)
+        *arrived, cot_near[step - 1] = land([*cot_fly, cot_near[step - 1]], done)
         cot_near[step] = join(arrived, 0, "join_2")
         cot_fly = onward(cot_near[step], step + 1, 0, "cotangent")
         cot_far[step] = swap(cot_near[step], f"cotangent_{step}_swap")
@@ -495,14 +490,8 @@
 
     last = reach - 1
     both_w = [gate_w, up_w, down_w, *mate_w]
-    before = []
-    if K["b2"] == "t4":
-        before.append(run_backward(last - 1))
-    if K["f3"] == "t4":
-        before.append(run_after(run_forward, token_near, last, cot_near[last]))
-    if K["force"]:
-        before.append(cot_far[last])
-    token_near[reach] = land(token_fly, *(before or [cot_near[last]]), *mates(f"T{reach}"))[0]
+    done = run_after(run_forward, token_near, last, cot_near[last])
+    token_near[reach] = land(token_fly, done)[0]
     info, slope, act, mixed_left = call(
         "pair_forward",
         functools.partial(pair_forward_body, cap, top),
@@ -516,12 +505,7 @@
         smem=1,
     )
     mixed_left, mixed_fly = [mixed_left], [hop(mixed_left, f"mixed_{reach}")]
-    before = [mixed_left[0]]
-    if K["f3"] == "late":
-        before.append(run_after(run_forward, token_near, last, *mixed_left))
-    if K["b2"] == "c4":
-        before.append(run_after(run_backward, cot_near, last - 1, *mixed_left))
-    cot_near[reach] = land(cot_fly, *before)[0]
+    cot_near[reach] = land(cot_fly, *mixed_left)[0]
     grad_left = call(
         "pair_backward",
         functools.partial(pair_backward_body, cap),
@@ -529,13 +513,7 @@
         [info, slope, act, cot_near[reach], *both_w],
     )
     grad_fly = [hop(grad_left[0], f"grad_{reach}")]
-    before = [*grad_left]
-    if K["f3"] == "y":
-        before.append(run_after(run_forward, token_near, last, *grad_left))
-    if K["b2"] == "m4":
-        before.append(run_after(run_backward, cot_near, last - 1, *grad_left))
-    if K["b3"] == "m4":
-        before.append(run_after(run_backward, cot_near, last, *grad_left))
+    before = [*grad_left, run_after(run_backward, cot_near, last, *grad_left)]
 
     def back_from(step, what, kept, given, values):
         outs = {0: (tok,), 1: (tok, tok)}.get(step, (2 * tok,))
@@ -573,13 +551,15 @@
         if len(grads) == len(jobs):
             return []
         lefts, rights = jobs[len(grads)]
-        grads.extend(call(
-            f"weights_{len(grads)}",
-            functools.partial(weights_body, len(lefts), 256),
-            [struct((width, units), BF16)],
-            [*lefts, *rights],
-            near=False,
-        ))
+        grads.extend(
+            call(
+                f"weights_{len(grads)}",
+                functools.partial(weights_body, len(lefts), 256),
+                [struct((width, units), BF16)],
+                [*lefts, *rights],
+                near=False,
+            )
+        )
         return grads[-1:]
 
     for step in range(last, 0, -1):
@@ -588,10 +568,7 @@
         mixed_fly = send_back(mixed_left, step, "mixed")
         before = [*mixed_left]
         if step == last:
-            if K["b3"] == "m3":
-                before.append(run_after(run_backward, cot_near, last, *mixed_left))
-            if K["b2"] == "m3":
-                before.append(run_after(run_backward, cot_near, last - 1, *mixed_left))
+            before.append(run_after(run_backward, cot_near, last - 1, *mixed_left))
             token_near[reach] = after(token_near[reach], *mixed_left)
             token_far[reach] = swap(token_near[reach], f"tokens_{reach}_swap")
             cot_far[reach] = swap(after(cot_near[reach], *mixed_left), f"cotangent_{reach}_swap")
@@ -602,8 +579,6 @@
         grad_fly = send_back(grad_left, step, "grad")
         before = [*grad_left]
         if step == last:
-            if K["b2"] == "g3":
-                before.append(run_after(run_backward, cot_near, last - 1, *grad_left))
             cot_near[reach] = after(cot_near[reach], *grad_left)
             before += [run_forward(reach), run_backward(reach)]
         before += some_job()
@@ -624,7 +599,7 @@
         lax.axis_size("dp") == 1
         and w_gate.shape[0] == 1
         and n % 4 == 0
-        and n >= 8
+        and n >= 16
         and n <= 2 * top
         and tok % 128 == 0
         and top % 8 == 0

time: 93.7 us -> 93.2 us (level)
  Pallas kernels: 35.7 us -> 31.3 us
  waiting for transfers between devices: 22.7 us -> 26.4 us
    pallas_call x27, Pallas kernels: 35.7 us -> 31.3 us  [call(): pl.pallas_call(body, out_shape=[pltpu.VMEM(a.shape, a.dtype) if near else...]
    ppermute x40, waiting for transfers between devices: 22.7 us -> 26.4 us  [hop(): return lax.ppermute(value, 'expert', moves)]
  transfers between devices with their start and end apart: 40 -> 40, of which waited for: 14 -> 15; matrix products, arithmetic and copies ran while one was open for 0% -> 0% of each run, Pallas kernels for 36% -> 31%
where the time goes in v6:
time: 93.2 us; the launch traced here: 93.1 us
  starting transfers between devices  34.3 us (37%)
  Pallas kernels  31.3 us (34%)
  waiting for transfers between devices  26.4 us (28%)
    ppermute x40, starting transfers between devices, hop(): return lax.ppermute(value, 'expert', moves)  34.3 us
    pallas_call x27, Pallas kernels, call(): pl.pallas_call(body, out_shape=[pltpu.VMEM(a.shape, a.dtype) if near else...  31.3 us
    ppermute x40, waiting for transfers between devices, hop(): return lax.ppermute(value, 'expert', moves)  26.4 us
  transfers between devices with their start and end apart: 40, of which 15 were waited for; matrix products, arithmetic and copies ran while one was open for 0% of the time, Pallas kernels for 31%

profile of v6, /device:TPU:0, one launch (start us, length us, event | category | flops | bytes accessed | tf_op | source)
XLA Modules:
  0.0 93.1 jit_solution(2906314990705394979)
XLA Ops:
  2.2 2.6 %collective-permute-start = (bf16[144,1024]{1,0:T(8,128)(2,1)S(1)}, bf16[144,1024]{1,0:T(8,128)(2,1)S(1)}, u32[]{:S(2)}, u32[]{:S(2)}) collective-permute-start(bf16[144,1024]{1,0:T(8,128)(2,1)S(1)} %payload.1.near), channel_id=1, source_target_pairs={{0,4},{1,3},{4,8},{5,1},{8,12},{9,5},{12,14},{13,9},{14,10},{15,13... | collective-permute-start | bytes 884744 | tf_op jit(solution)/shard_map/tokens_1/ppermute | solution.py:369
  6.7 1.6 %collective-permute-start.6 = (bf16[256,1024]{1,0:T(8,128)(2,1)S(1)}, bf16[256,1024]{1,0:T(8,128)(2,1)S(1)}, u32[]{:S(2)}, u32[]{:S(2)}) collective-permute-start(bf16[256,1024]{1,0:T(8,128)(2,1)S(1)} %join_0.1), channel_id=1, source_target_pairs={{0,4},{1,3},{4,8},{5,1},{8,12},{9,5},{12,14},{13,9},{14,10},{15,13... | collective-permute-start | bytes 1572872 | tf_op jit(solution)/shard_map/cotangent_1/ppermute | solution.py:369
  8.3 1.6 %stage.1 = (bf16[1024,384]{1,0:T(8,128)(2,1)S(1)}, bf16[1024,384]{1,0:T(8,128)(2,1)S(1)}, bf16[1024,384]{1,0:T(8,128)(2,1)S(1)}) custom-call(bf16[1024,384]{1,0:T(8,128)(2,1)} %bitcast.13, bf16[1024,384]{1,0:T(8,128)(2,1)} %bitcast.14, bf16[1024,384]{1,0:T(8,128)(2,1)} %bitcast.15), custom_call_target="tpu_custom_call" | custom-call | flops 1073741824 | bytes 1024 | tf_op jit(solution)/shard_map/stage/pallas_call | solution.py:122
  11.3 3.0 %collective-permute-done.1.second = bf16[144,1024]{1,0:T(8,128)(2,1)S(1)} collective-permute-done((bf16[144,1024]{1,0:T(8,128)(2,1)S(1)}, bf16[144,1024]{1,0:T(8,128)(2,1)S(1)}, u32[]{:S(2)}, u32[]{:S(2)}) %collective-permute-start.1) | collective-permute-done | bytes 294944 | tf_op jit(solution)/shard_map/tokens_1_crossing/ppermute | solution.py:369
  18.3 2.1 %collective-permute-start.10 = (bf16[256,1024]{1,0:T(8,128)(2,1)S(1)}, bf16[256,1024]{1,0:T(8,128)(2,1)S(1)}, u32[]{:S(2)}, u32[]{:S(2)}) collective-permute-start(bf16[256,1024]{1,0:T(8,128)(2,1)S(1)} %collective-permute-done.6.near), channel_id=1, source_target_pairs={{0,4},{1,3},{4,8},{5,1},{8,12},{9,5},{12,14},{13,9},{14,10},{15,13... | collective-permute-start | bytes 1572872 | tf_op jit(solution)/shard_map/cotangent_2/ppermute | solution.py:369
  20.4 3.9 %collective-permute-done.4.near = bf16[272,1024]{1,0:T(8,128)(2,1)S(1)} collective-permute-done((bf16[272,1024]{1,0:T(8,128)(2,1)S(1)}, bf16[272,1024]{1,0:T(8,128)(2,1)S(1)}, u32[]{:S(2)}, u32[]{:S(2)}) %collective-permute-start.4) | collective-permute-done | bytes 557088 | tf_op jit(solution)/shard_map/tokens_2/ppermute | solution.py:369
  25.8 2.2 %collective-permute-start.9 = (bf16[272,1024]{1,0:T(8,128)(2,1)S(1)}, bf16[272,1024]{1,0:T(8,128)(2,1)S(1)}, u32[]{:S(2)}, u32[]{:S(2)}) collective-permute-start(bf16[272,1024]{1,0:T(8,128)(2,1)S(1)} %collective-permute-done.4.near), channel_id=1, source_target_pairs={{0,4},{1,3},{4,8},{5,1},{8,12},{9,5},{12,14},{13,9},{14,10},{15,13... | collective-permute-start | bytes 1671176 | tf_op jit(solution)/shard_map/tokens_3/ppermute | solution.py:369
  27.9 1.9 %collective-permute-done.10.near = bf16[256,1024]{1,0:T(8,128)(2,1)S(1)} collective-permute-done((bf16[256,1024]{1,0:T(8,128)(2,1)S(1)}, bf16[256,1024]{1,0:T(8,128)(2,1)S(1)}, u32[]{:S(2)}, u32[]{:S(2)}) %collective-permute-start.10) | collective-permute-done | bytes 524320 | tf_op jit(solution)/shard_map/cotangent_2/ppermute | solution.py:369
  29.9 2.0 %forward_1.1 = (f32[16,128]{1,0:T(8,128)S(1)}, bf16[256,1024]{1,0:T(8,128)(2,1)S(1)}, f32[256,384]{1,0:T(8,128)S(1)}, f32[256,384]{1,0:T(8,128)S(1)}, bf16[256,3...) custom-call(s32[2]{0:T(128)S(1)} %pad_add_fusion.expert_ref, ...), custom_call_target="tpu_custom_call" | custom-call | flops 1048576 | bytes 1024 | tf_op jit(solution)/shard_map/forward_1/pallas_call | solution.py:122
  31.8 2.2 %collective-permute-start.17 = (bf16[256,1024]{1,0:T(8,128)(2,1)S(1)}, bf16[256,1024]{1,0:T(8,128)(2,1)S(1)}, u32[]{:S(2)}, u32[]{:S(2)}) collective-permute-start(bf16[256,1024]{1,0:T(8,128)(2,1)S(1)} %collective-permute-done.10.near), channel_id=1, source_target_pairs={{0,4},{1,3},{4,8},{5,1},{8,12},{9,5},{12,14},{13,9},{14,10},{15,13... | collective-permute-start | bytes 1572872 | tf_op jit(solution)/shard_map/cotangent_3/ppermute | solution.py:369
  35.8 2.2 %collective-permute-start.20 = (bf16[144,1024]{1,0:T(8,128)(2,1)S(1)}, bf16[144,1024]{1,0:T(8,128)(2,1)S(1)}, u32[]{:S(2)}, u32[]{:S(2)}) collective-permute-start(bf16[144,1024]{1,0:T(8,128)(2,1)S(1)} %slice.6), channel_id=1, source_target_pairs={{0,4},{1,3},{4,8},{5,1},{8,12},{9,5},{12,14},{13,9},{14,10},{15,13... | collective-permute-start | bytes 884744 | tf_op jit(solution)/shard_map/tokens_4/ppermute | solution.py:369
  38.0 2.0 %forward_2.1 = (f32[16,128]{1,0:T(8,128)S(1)}, bf16[256,1024]{1,0:T(8,128)(2,1)S(1)}, f32[256,384]{1,0:T(8,128)S(1)}, f32[256,384]{1,0:T(8,128)S(1)}, bf16[256,3...) custom-call(s32[2]{0:T(128)S(1)} %pad_add_fusion.expert_ref, ...), custom_call_target="tpu_custom_call" | custom-call | flops 4294967296 | bytes 1024 | tf_op jit(solution)/shard_map/forward_2/pallas_call | solution.py:122
  41.5 2.2 %collective-permute-start.22 = (bf16[128,1024]{1,0:T(8,128)(2,1)S(1)}, bf16[128,1024]{1,0:T(8,128)(2,1)S(1)}, u32[]{:S(2)}, u32[]{:S(2)}) collective-permute-start(bf16[128,1024]{1,0:T(8,128)(2,1)S(1)} %slice.7), channel_id=1, source_target_pairs={{0,4},{1,3},{4,8},{5,1},{8,12},{9,5},{12,14},{13,9},{14,10},{15,13... | collective-permute-start | bytes 786440 | tf_op jit(solution)/shard_map/cotangent_4/ppermute | solution.py:369
  43.6 2.0 %forward_3.1 = (f32[16,128]{1,0:T(8,128)S(1)}, bf16[256,1024]{1,0:T(8,128)(2,1)S(1)}, f32[256,384]{1,0:T(8,128)S(1)}, f32[256,384]{1,0:T(8,128)S(1)}, bf16[256,3...) custom-call(s32[2]{0:T(128)S(1)} %pad_add_fusion.expert_ref, ...), custom_call_target="tpu_custom_call" | custom-call | flops 1048576 | bytes 1024 | tf_op jit(solution)/shard_map/forward_3/pallas_call | solution.py:122
  45.6 2.2 %pair_forward.1 = (f32[16,128]{1,0:T(8,128)S(1)}, f32[128,384]{1,0:T(8,128)S(1)}, f32[128,384]{1,0:T(8,128)S(1)}, bf16[128,1024]{1,0:T(8,128)(2,1)S(1)}) custom-call(s32[2]{0:T(128)S(1)} %pad_add_fusion.expert_ref, bf16[144,1024]{1,0:T(8,128)(2,1)S(1)} %collective-permute-done.20.near, bf16[1024,384]{1,0:T(8,128)(2,1)S(1)} %get-tuple-element.139.w_gate.refs_0_, ...), custom_call_target="tpu_custom_call" | custom-call | flops 1073741824 | bytes 1024 | tf_op jit(solution)/shard_map/pair_forward/pallas_call | solution.py:122
  47.8 1.6 %collective-permute-start.21 = (bf16[128,1024]{1,0:T(8,128)(2,1)S(1)}, bf16[128,1024]{1,0:T(8,128)(2,1)S(1)}, u32[]{:S(2)}, u32[]{:S(2)}) collective-permute-start(bf16[128,1024]{1,0:T(8,128)(2,1)S(1)} %get-tuple-element.156), channel_id=1, source_target_pairs={{0,4},{1,3},{4,8},{5,1},{8,12},{9,5},{12,14},{13,9},{14,10},{15,13... | collective-permute-start | bytes 786440 | tf_op jit(solution)/shard_map/mixed_4/ppermute | solution.py:369
  49.9 1.8 %pair_backward.1 = bf16[128,1024]{1,0:T(8,128)(2,1)S(1)} custom-call(f32[16,128]{1,0:T(8,128)S(1)} %get-tuple-element.157.info_ref, f32[128,384]{1,0:T(8,128)S(1)} %get-tuple-element.158.slope_ref, f32[128,384]{1,0:T(8,128)S(1)} %get-tuple-element.159.act_ref, bf16[128,1024]{1,0:T(8,128)(2,1)S(1)} %collective-permute-done.22.near, ...), custom_call_target="tpu_custom_call" | custom-call | flops 268435456 | bytes 1024 | tf_op jit(solution)/shard_map/pair_backward/pallas_call | solution.py:122
  62.4 2.2 %weights_0.1 = bf16[1024,384]{1,0:T(8,128)(2,1)} custom-call(bf16[128,1024]{1,0:T(8,128)(2,1)S(1)} %get-tuple-element.182.refs_0_, bf16[256,1024]{1,0:T(8,128)(2,1)S(1)} %get-tuple-element.183.refs_1_, bf16[256,1024]{1,0:T(8,128)(2,1)S(1)} %get-tuple-element.184.refs_2_, bf16[256,1024]{1,0:T(8,128)(2,1)S(1)} %get-tuple-element.185.refs_3_, ...), custom_call_target="tpu_custom_call" | custom-call | flops 1048576 | bytes 1024 | tf_op jit(solution)/shard_map/weights_0/pallas_call | solution.py:122
  66.4 2.2 %weights_1.1 = bf16[1024,384]{1,0:T(8,128)(2,1)} custom-call(bf16[128,1024]{1,0:T(8,128)(2,1)S(1)} %get-tuple-element.182.refs_0_, bf16[256,1024]{1,0:T(8,128)(2,1)S(1)} %get-tuple-element.183.refs_1_, bf16[256,1024]{1,0:T(8,128)(2,1)S(1)} %get-tuple-element.184.refs_2_, bf16[256,1024]{1,0:T(8,128)(2,1)S(1)} %get-tuple-element.185.refs_3_, ...), custom_call_target="tpu_custom_call" | custom-call | flops 1048576 | bytes 1024 | tf_op jit(solution)/shard_map/weights_1/pallas_call | solution.py:122
  72.4 2.2 %weights_2.1 = bf16[1024,384]{1,0:T(8,128)(2,1)} custom-call(bf16[128,1024]{1,0:T(8,128)(2,1)S(1)} %get-tuple-element.196.refs_0_, bf16[256,1024]{1,0:T(8,128)(2,1)S(1)} %get-tuple-element.197.refs_1_, bf16[256,1024]{1,0:T(8,128)(2,1)S(1)} %get-tuple-element.198.refs_2_, bf16[256,1024]{1,0:T(8,128)(2,1)S(1)} %get-tuple-element.199.refs_3_, ...), custom_call_target="tpu_custom_call" | custom-call | flops 1048576 | bytes 1024 | tf_op jit(solution)/shard_map/weights_2/pallas_call | solution.py:122
  77.5 3.9 %collective-permute-done.36.refs_0_ = bf16[256,1024]{1,0:T(8,128)(2,1)S(1)} collective-permute-done((bf16[256,1024]{1,0:T(8,128)(2,1)S(1)}, bf16[256,1024]{1,0:T(8,128)(2,1)S(1)}, u32[]{:S(2)}, u32[]{:S(2)}) %collective-permute-start.36) | collective-permute-done | bytes 524320 | tf_op jit(solution)/shard_map/grad_2/ppermute | solution.py:369
  84.1 2.3 %collective-permute-done.34.refs_1_ = bf16[128,1024]{1,0:T(8,128)(2,1)S(1)} collective-permute-done((bf16[128,1024]{1,0:T(8,128)(2,1)S(1)}, bf16[128,1024]{1,0:T(8,128)(2,1)S(1)}, u32[]{:S(2)}, u32[]{:S(2)}) %collective-permute-start.34) | collective-permute-done | bytes 262176 | tf_op jit(solution)/shard_map/mixed_1_crossing/ppermute | solution.py:369
  87.4 2.3 %collective-permute-done.38.refs_0_ = bf16[128,1024]{1,0:T(8,128)(2,1)S(1)} collective-permute-done((bf16[128,1024]{1,0:T(8,128)(2,1)S(1)}, bf16[128,1024]{1,0:T(8,128)(2,1)S(1)}, u32[]{:S(2)}, u32[]{:S(2)}) %collective-permute-start.38) | collective-permute-done | bytes 262176 | tf_op jit(solution)/shard_map/grad_1/ppermute | solution.py:369
  89.7 2.3 %collective-permute-done.39.refs_1_ = bf16[128,1024]{1,0:T(8,128)(2,1)S(1)} collective-permute-done((bf16[128,1024]{1,0:T(8,128)(2,1)S(1)}, bf16[128,1024]{1,0:T(8,128)(2,1)S(1)}, u32[]{:S(2)}, u32[]{:S(2)}) %collective-permute-start.39) | collective-permute-done | bytes 262176 | tf_op jit(solution)/shard_map/grad_1_crossing/ppermute | solution.py:369
  (88 shorter events, 37.7 us)
Async XLA Ops:
  2.2 9.0 %collective-permute-start = (bf16[144,1024]{1,0:T(8,128)(2,1)S(1)}, bf16[144,1024]{1,0:T(8,128)(2,1)S(1)}, u32[]{:S(2)}, u32[]{:S(2)}) collective-permute-start(bf16[144,1024]{1,0:T(8,128)(2,1)S(1)} %payload.1.near), channel_id=1, source_target_pairs={{0,4},{1,3},{4,8},{5,1},{8,12},{9,5},{12,14},{13,9},{14,10},{15,13... | collective-permute-start | bytes 884744 | tf_op jit(solution)/shard_map/tokens_1/ppermute | solution.py:369
  4.9 9.4 %collective-permute-start.1 = (bf16[144,1024]{1,0:T(8,128)(2,1)S(1)}, bf16[144,1024]{1,0:T(8,128)(2,1)S(1)}, u32[]{:S(2)}, u32[]{:S(2)}) collective-permute-start(bf16[144,1024]{1,0:T(8,128)(2,1)S(1)} %payload.1.near), channel_id=1, source_target_pairs={{0,3},{1,4},{4,1},{5,8},{8,5},{9,12},{12,9},{13,14},{14,13},{15,10... | collective-permute-start | bytes 884744 | tf_op jit(solution)/shard_map/tokens_1_crossing/ppermute | solution.py:369
  6.1 10.2 %collective-permute-start.2 = (bf16[144,1024]{1,0:T(8,128)(2,1)S(1)}, bf16[144,1024]{1,0:T(8,128)(2,1)S(1)}, u32[]{:S(2)}, u32[]{:S(2)}) collective-permute-start(bf16[144,1024]{1,0:T(8,128)(2,1)S(1)} %payload.1.near), channel_id=1, source_target_pairs={{0,1},{1,0},{2,3},{3,2},{4,5},{5,4},{6,7},{7,6},{8,9},{9,8},{10,11... | collective-permute-start | bytes 884744 | tf_op jit(solution)/shard_map/tokens_0_swap/ppermute | solution.py:369
  6.7 11.6 %collective-permute-start.6 = (bf16[256,1024]{1,0:T(8,128)(2,1)S(1)}, bf16[256,1024]{1,0:T(8,128)(2,1)S(1)}, u32[]{:S(2)}, u32[]{:S(2)}) collective-permute-start(bf16[256,1024]{1,0:T(8,128)(2,1)S(1)} %join_0.1), channel_id=1, source_target_pairs={{0,4},{1,3},{4,8},{5,1},{8,12},{9,5},{12,14},{13,9},{14,10},{15,13... | collective-permute-start | bytes 1572872 | tf_op jit(solution)/shard_map/cotangent_1/ppermute | solution.py:369
  14.3 9.9 %collective-permute-start.4 = (bf16[272,1024]{1,0:T(8,128)(2,1)S(1)}, bf16[272,1024]{1,0:T(8,128)(2,1)S(1)}, u32[]{:S(2)}, u32[]{:S(2)}) collective-permute-start(bf16[272,1024]{1,0:T(8,128)(2,1)S(1)} %join_1.1.near), channel_id=1, source_target_pairs={{0,4},{1,3},{4,8},{5,1},{8,12},{9,5},{12,14},{13,9},{14,10},{15,13... | collective-permute-start | bytes 1671176 | tf_op jit(solution)/shard_map/tokens_2/ppermute | solution.py:369
  15.8 8.4 %collective-permute-start.7 = (bf16[272,1024]{1,0:T(8,128)(2,1)S(1)}, bf16[272,1024]{1,0:T(8,128)(2,1)S(1)}, u32[]{:S(2)}, u32[]{:S(2)}) collective-permute-start(bf16[272,1024]{1,0:T(8,128)(2,1)S(1)} %join_1.1.near), channel_id=1, source_target_pairs={{0,1},{1,0},{2,3},{3,2},{4,5},{5,4},{6,7},{7,6},{8,9},{9,8},{10,11... | collective-permute-start | bytes 1671176 | tf_op jit(solution)/shard_map/tokens_1_swap/ppermute | solution.py:369
  16.0 9.7 %collective-permute-start.12 = (bf16[1024,384]{1,0:T(8,128)(2,1)S(1)}, bf16[1024,384]{1,0:T(8,128)(2,1)S(1)}, u32[]{:S(2)}, u32[]{:S(2)}) collective-permute-start(bf16[1024,384]{1,0:T(8,128)(2,1)S(1)} %get-tuple-element.139.w_gate.refs_0_), channel_id=1, source_target_pairs={{0,1},{1,0},{2,3},{3,2},{4,5},{5,4},{6,7},{7,6},{8,9},{9,8},{10,11... | collective-permute-start | bytes 2359304 | tf_op jit(solution)/shard_map/weights_swap/ppermute | solution.py:369
  18.3 11.6 %collective-permute-start.10 = (bf16[256,1024]{1,0:T(8,128)(2,1)S(1)}, bf16[256,1024]{1,0:T(8,128)(2,1)S(1)}, u32[]{:S(2)}, u32[]{:S(2)}) collective-permute-start(bf16[256,1024]{1,0:T(8,128)(2,1)S(1)} %collective-permute-done.6.near), channel_id=1, source_target_pairs={{0,4},{1,3},{4,8},{5,1},{8,12},{9,5},{12,14},{13,9},{14,10},{15,13... | collective-permute-start | bytes 1572872 | tf_op jit(solution)/shard_map/cotangent_2/ppermute | solution.py:369
  20.4 14.9 %collective-permute-start.13 = (bf16[1024,384]{1,0:T(8,128)(2,1)S(1)}, bf16[1024,384]{1,0:T(8,128)(2,1)S(1)}, u32[]{:S(2)}, u32[]{:S(2)}) collective-permute-start(bf16[1024,384]{1,0:T(8,128)(2,1)S(1)} %get-tuple-element.140.w_up.refs_1_), channel_id=1, source_target_pairs={{0,1},{1,0},{2,3},{3,2},{4,5},{5,4},{6,7},{7,6},{8,9},{9,8},{10,11... | collective-permute-start | bytes 2359304 | tf_op jit(solution)/shard_map/weights_swap/ppermute | solution.py:369
  24.2 11.1 %collective-permute-start.14 = (bf16[1024,384]{1,0:T(8,128)(2,1)S(1)}, bf16[1024,384]{1,0:T(8,128)(2,1)S(1)}, u32[]{:S(2)}, u32[]{:S(2)}) collective-permute-start(bf16[1024,384]{1,0:T(8,128)(2,1)S(1)} %get-tuple-element.141.w_down.refs_2_), channel_id=1, source_target_pairs={{0,1},{1,0},{2,3},{3,2},{4,5},{5,4},{6,7},{7,6},{8,9},{9,8},{10,11... | collective-permute-start | bytes 2359304 | tf_op jit(solution)/shard_map/weights_swap/ppermute | solution.py:369
  25.8 10.1 %collective-permute-start.9 = (bf16[272,1024]{1,0:T(8,128)(2,1)S(1)}, bf16[272,1024]{1,0:T(8,128)(2,1)S(1)}, u32[]{:S(2)}, u32[]{:S(2)}) collective-permute-start(bf16[272,1024]{1,0:T(8,128)(2,1)S(1)} %collective-permute-done.4.near), channel_id=1, source_target_pairs={{0,4},{1,3},{4,8},{5,1},{8,12},{9,5},{12,14},{13,9},{14,10},{15,13... | collective-permute-start | bytes 1671176 | tf_op jit(solution)/shard_map/tokens_3/ppermute | solution.py:369
  29.8 8.2 %collective-permute-start.15 = (bf16[272,1024]{1,0:T(8,128)(2,1)S(1)}, bf16[272,1024]{1,0:T(8,128)(2,1)S(1)}, u32[]{:S(2)}, u32[]{:S(2)}) collective-permute-start(bf16[272,1024]{1,0:T(8,128)(2,1)S(1)} %collective-permute-done.4.near), channel_id=1, source_target_pairs={{0,1},{1,0},{2,3},{3,2},{4,5},{5,4},{6,7},{7,6},{8,9},{9,8},{10,11... | collective-permute-start | bytes 1671176 | tf_op jit(solution)/shard_map/tokens_2_swap/ppermute | solution.py:369
  31.8 9.6 %collective-permute-start.17 = (bf16[256,1024]{1,0:T(8,128)(2,1)S(1)}, bf16[256,1024]{1,0:T(8,128)(2,1)S(1)}, u32[]{:S(2)}, u32[]{:S(2)}) collective-permute-start(bf16[256,1024]{1,0:T(8,128)(2,1)S(1)} %collective-permute-done.10.near), channel_id=1, source_target_pairs={{0,4},{1,3},{4,8},{5,1},{8,12},{9,5},{12,14},{13,9},{14,10},{15,13... | collective-permute-start | bytes 1572872 | tf_op jit(solution)/shard_map/cotangent_3/ppermute | solution.py:369
  35.8 9.8 %collective-permute-start.20 = (bf16[144,1024]{1,0:T(8,128)(2,1)S(1)}, bf16[144,1024]{1,0:T(8,128)(2,1)S(1)}, u32[]{:S(2)}, u32[]{:S(2)}) collective-permute-start(bf16[144,1024]{1,0:T(8,128)(2,1)S(1)} %slice.6), channel_id=1, source_target_pairs={{0,4},{1,3},{4,8},{5,1},{8,12},{9,5},{12,14},{13,9},{14,10},{15,13... | collective-permute-start | bytes 884744 | tf_op jit(solution)/shard_map/tokens_4/ppermute | solution.py:369
  41.4 11.9 %collective-permute-start.23 = (bf16[256,1024]{1,0:T(8,128)(2,1)S(1)}, bf16[256,1024]{1,0:T(8,128)(2,1)S(1)}, u32[]{:S(2)}, u32[]{:S(2)}) collective-permute-start(bf16[256,1024]{1,0:T(8,128)(2,1)S(1)} %collective-permute-done.17.near), channel_id=1, source_target_pairs={{0,1},{1,0},{2,3},{3,2},{4,5},{5,4},{6,7},{7,6},{8,9},{9,8},{10,11... | collective-permute-start | bytes 1572872 | tf_op jit(solution)/shard_map/cotangent_3_swap/ppermute | solution.py:369
  41.5 8.5 %collective-permute-start.22 = (bf16[128,1024]{1,0:T(8,128)(2,1)S(1)}, bf16[128,1024]{1,0:T(8,128)(2,1)S(1)}, u32[]{:S(2)}, u32[]{:S(2)}) collective-permute-start(bf16[128,1024]{1,0:T(8,128)(2,1)S(1)} %slice.7), channel_id=1, source_target_pairs={{0,4},{1,3},{4,8},{5,1},{8,12},{9,5},{12,14},{13,9},{14,10},{15,13... | collective-permute-start | bytes 786440 | tf_op jit(solution)/shard_map/cotangent_4/ppermute | solution.py:369
  55.1 9.6 %collective-permute-start.24 = (bf16[256,1024]{1,0:T(8,128)(2,1)S(1)}, bf16[256,1024]{1,0:T(8,128)(2,1)S(1)}, u32[]{:S(2)}, u32[]{:S(2)}) collective-permute-start(bf16[256,1024]{1,0:T(8,128)(2,1)S(1)} %mixed_sums_3.1), channel_id=1, source_target_pairs={{0,4},{1,3},{4,8},{5,1},{8,12},{9,5},{12,14},{13,9},{14,10},{15,13... | collective-permute-start | bytes 1572872 | tf_op jit(solution)/shard_map/mixed_3/ppermute | solution.py:369
  58.5 11.6 %collective-permute-start.32 = (bf16[256,1024]{1,0:T(8,128)(2,1)S(1)}, bf16[256,1024]{1,0:T(8,128)(2,1)S(1)}, u32[]{:S(2)}, u32[]{:S(2)}) collective-permute-start(bf16[256,1024]{1,0:T(8,128)(2,1)S(1)} %grad_sums_3.1), channel_id=1, source_target_pairs={{0,4},{1,3},{4,8},{5,1},{8,12},{9,5},{12,14},{13,9},{14,10},{15,13... | collective-permute-start | bytes 1572872 | tf_op jit(solution)/shard_map/grad_3/ppermute | solution.py:369
  60.6 9.5 %collective-permute-start.31 = (bf16[128,1024]{1,0:T(8,128)(2,1)S(1)}, bf16[128,1024]{1,0:T(8,128)(2,1)S(1)}, u32[]{:S(2)}, u32[]{:S(2)}) collective-permute-start(bf16[128,1024]{1,0:T(8,128)(2,1)S(1)} %get-tuple-element.189), channel_id=1, source_target_pairs={{0,1},{1,0},{2,3},{3,2},{4,5},{5,4},{6,7},{7,6},{8,9},{9,8},{10,11... | collective-permute-start | bytes 786440 | tf_op jit(solution)/shard_map/grad_2_swap/ppermute | solution.py:369
  65.0 10.8 %collective-permute-start.30 = (bf16[256,1024]{1,0:T(8,128)(2,1)S(1)}, bf16[256,1024]{1,0:T(8,128)(2,1)S(1)}, u32[]{:S(2)}, u32[]{:S(2)}) collective-permute-start(bf16[256,1024]{1,0:T(8,128)(2,1)S(1)} %mixed_sums_2.1), channel_id=1, source_target_pairs={{0,4},{1,3},{4,8},{5,1},{8,12},{9,5},{12,14},{13,9},{14,10},{15,13... | collective-permute-start | bytes 1572872 | tf_op jit(solution)/shard_map/mixed_2/ppermute | solution.py:369
  70.4 10.9 %collective-permute-start.36 = (bf16[256,1024]{1,0:T(8,128)(2,1)S(1)}, bf16[256,1024]{1,0:T(8,128)(2,1)S(1)}, u32[]{:S(2)}, u32[]{:S(2)}) collective-permute-start(bf16[256,1024]{1,0:T(8,128)(2,1)S(1)} %grad_sums_2.1), channel_id=1, source_target_pairs={{0,4},{1,3},{4,8},{5,1},{8,12},{9,5},{12,14},{13,9},{14,10},{15,13... | collective-permute-start | bytes 1572872 | tf_op jit(solution)/shard_map/grad_2/ppermute | solution.py:369
  71.8 9.5 %collective-permute-start.35 = (bf16[128,1024]{1,0:T(8,128)(2,1)S(1)}, bf16[128,1024]{1,0:T(8,128)(2,1)S(1)}, u32[]{:S(2)}, u32[]{:S(2)}) collective-permute-start(bf16[128,1024]{1,0:T(8,128)(2,1)S(1)} %get-tuple-element.205), channel_id=1, source_target_pairs={{0,1},{1,0},{2,3},{3,2},{4,5},{5,4},{6,7},{7,6},{8,9},{9,8},{10,11... | collective-permute-start | bytes 786440 | tf_op jit(solution)/shard_map/grad_1_swap/ppermute | solution.py:369
  77.5 9.0 %collective-permute-start.34 = (bf16[128,1024]{1,0:T(8,128)(2,1)S(1)}, bf16[128,1024]{1,0:T(8,128)(2,1)S(1)}, u32[]{:S(2)}, u32[]{:S(2)}) collective-permute-start(bf16[128,1024]{1,0:T(8,128)(2,1)S(1)} %get-tuple-element.203), channel_id=1, source_target_pairs={{0,5},{1,2},{4,9},{5,0},{8,13},{9,4},{12,15},{13,8},{14,11},{15,12... | collective-permute-start | bytes 786440 | tf_op jit(solution)/shard_map/mixed_1_crossing/ppermute | solution.py:369
  83.1 9.0 %collective-permute-start.39 = (bf16[128,1024]{1,0:T(8,128)(2,1)S(1)}, bf16[128,1024]{1,0:T(8,128)(2,1)S(1)}, u32[]{:S(2)}, u32[]{:S(2)}) collective-permute-start(bf16[128,1024]{1,0:T(8,128)(2,1)S(1)} %get-tuple-element.208), channel_id=1, source_target_pairs={{0,5},{1,2},{4,9},{5,0},{8,13},{9,4},{12,15},{13,8},{14,11},{15,12... | collective-permute-start | bytes 786440 | tf_op jit(solution)/shard_map/grad_1_crossing/ppermute | solution.py:369
  (17 other events, 92.4 us)

commit v7 on v6

--- a/solution.py
+++ b/solution.py
@@ -329,7 +329,11 @@
         for j in range(ref.shape[0] // tok):
             sums[j] = sums[j] + ref[j * tok : (j + 1) * tok].astype(F32)
     for out, total in zip(outs, sums if count > 1 else [joined(sums)]):
-        out[...] = total.astype(BF16)
+        out[...] = total.astype(out.dtype)
+
+
+def last_body(own, first, second, out):
+    out[...] = (own[...] + first[...].astype(F32) + second[...].astype(F32)).astype(BF16)
 
 
 def weights_body(steps, cols, *refs):
@@ -586,8 +590,17 @@
         pass
     arrived = land(mixed_fly, *before, *grads)
     mixed = mixed_back(0, arrived)[0]
-    arrived = land(grad_fly, mixed)
-    grad_tokens = grad_back(0, arrived)[0]
+    given = swap(backward[0][4], "grad_0_swap")
+    (own,) = call(
+        "grad_sums_0",
+        functools.partial(return_body, cap, blocks_of(0)[1], 1),
+        [struct((tok, width), F32)],
+        [forward[0][0], backward[0][3], given],
+    )
+    arrived = land(grad_fly, mixed, own)
+    (grad_tokens,) = call(
+        "grad_last", last_body, [struct((tok, width), BF16)], [own, *arrived], near=False
+    )
     return (mixed, grad_tokens, *[g[None] for g in grads])
 
 

time: 93.2 us -> 93.7 us (level)
    pallas_call x27 -> x28, Pallas kernels: 31.3 us -> 31.4 us  [call(): pl.pallas_call(body, out_shape=[pltpu.VMEM(a.shape, a.dtype) if near else...]
  transfers between devices with their start and end apart: 40 -> 40, of which waited for: 15 -> 14; matrix products, arithmetic and copies ran while one was open for 0% -> 0% of each run, Pallas kernels for 31% -> 32%
where the time goes in v7:
time: 93.7 us; the launch traced here: 93.6 us
  starting transfers between devices  34.3 us (37%)
  Pallas kernels  31.4 us (34%)
  waiting for transfers between devices  26.8 us (29%)
    ppermute x40, starting transfers between devices, hop(): return lax.ppermute(value, 'expert', moves)  34.3 us
    pallas_call x28, Pallas kernels, call(): pl.pallas_call(body, out_shape=[pltpu.VMEM(a.shape, a.dtype) if near else...  31.4 us
    ppermute x40, waiting for transfers between devices, hop(): return lax.ppermute(value, 'expert', moves)  26.8 us
  transfers between devices with their start and end apart: 40, of which 14 were waited for; matrix products, arithmetic and copies ran while one was open for 0% of the time, Pallas kernels for 32%

profile of v7, /device:TPU:0, one launch (start us, length us, event | category | flops | bytes accessed | tf_op | source)
XLA Modules:
  0.0 93.6 jit_solution(4717609065633956174)
XLA Ops:
  2.2 2.6 %collective-permute-start = (bf16[144,1024]{1,0:T(8,128)(2,1)S(1)}, bf16[144,1024]{1,0:T(8,128)(2,1)S(1)}, u32[]{:S(2)}, u32[]{:S(2)}) collective-permute-start(bf16[144,1024]{1,0:T(8,128)(2,1)S(1)} %payload.1.near), channel_id=1, source_target_pairs={{0,4},{1,3},{4,8},{5,1},{8,12},{9,5},{12,14},{13,9},{14,10},{15,13... | collective-permute-start | bytes 884744 | tf_op jit(solution)/shard_map/tokens_1/ppermute | solution.py:373
  6.7 1.6 %collective-permute-start.6 = (bf16[256,1024]{1,0:T(8,128)(2,1)S(1)}, bf16[256,1024]{1,0:T(8,128)(2,1)S(1)}, u32[]{:S(2)}, u32[]{:S(2)}) collective-permute-start(bf16[256,1024]{1,0:T(8,128)(2,1)S(1)} %join_0.1), channel_id=1, source_target_pairs={{0,4},{1,3},{4,8},{5,1},{8,12},{9,5},{12,14},{13,9},{14,10},{15,13... | collective-permute-start | bytes 1572872 | tf_op jit(solution)/shard_map/cotangent_1/ppermute | solution.py:373
  8.3 1.6 %stage.1 = (bf16[1024,384]{1,0:T(8,128)(2,1)S(1)}, bf16[1024,384]{1,0:T(8,128)(2,1)S(1)}, bf16[1024,384]{1,0:T(8,128)(2,1)S(1)}) custom-call(bf16[1024,384]{1,0:T(8,128)(2,1)} %bitcast.13, bf16[1024,384]{1,0:T(8,128)(2,1)} %bitcast.14, bf16[1024,384]{1,0:T(8,128)(2,1)} %bitcast.15), custom_call_target="tpu_custom_call" | custom-call | flops 1073741824 | bytes 1024 | tf_op jit(solution)/shard_map/stage/pallas_call | solution.py:122
  11.3 3.0 %collective-permute-done.1.second = bf16[144,1024]{1,0:T(8,128)(2,1)S(1)} collective-permute-done((bf16[144,1024]{1,0:T(8,128)(2,1)S(1)}, bf16[144,1024]{1,0:T(8,128)(2,1)S(1)}, u32[]{:S(2)}, u32[]{:S(2)}) %collective-permute-start.1) | collective-permute-done | bytes 294944 | tf_op jit(solution)/shard_map/tokens_1_crossing/ppermute | solution.py:373
  18.3 2.1 %collective-permute-start.10 = (bf16[256,1024]{1,0:T(8,128)(2,1)S(1)}, bf16[256,1024]{1,0:T(8,128)(2,1)S(1)}, u32[]{:S(2)}, u32[]{:S(2)}) collective-permute-start(bf16[256,1024]{1,0:T(8,128)(2,1)S(1)} %collective-permute-done.6.near), channel_id=1, source_target_pairs={{0,4},{1,3},{4,8},{5,1},{8,12},{9,5},{12,14},{13,9},{14,10},{15,13... | collective-permute-start | bytes 1572872 | tf_op jit(solution)/shard_map/cotangent_2/ppermute | solution.py:373
  20.4 3.9 %collective-permute-done.4.near = bf16[272,1024]{1,0:T(8,128)(2,1)S(1)} collective-permute-done((bf16[272,1024]{1,0:T(8,128)(2,1)S(1)}, bf16[272,1024]{1,0:T(8,128)(2,1)S(1)}, u32[]{:S(2)}, u32[]{:S(2)}) %collective-permute-start.4) | collective-permute-done | bytes 557088 | tf_op jit(solution)/shard_map/tokens_2/ppermute | solution.py:373
  25.8 2.2 %collective-permute-start.9 = (bf16[272,1024]{1,0:T(8,128)(2,1)S(1)}, bf16[272,1024]{1,0:T(8,128)(2,1)S(1)}, u32[]{:S(2)}, u32[]{:S(2)}) collective-permute-start(bf16[272,1024]{1,0:T(8,128)(2,1)S(1)} %collective-permute-done.4.near), channel_id=1, source_target_pairs={{0,4},{1,3},{4,8},{5,1},{8,12},{9,5},{12,14},{13,9},{14,10},{15,13... | collective-permute-start | bytes 1671176 | tf_op jit(solution)/shard_map/tokens_3/ppermute | solution.py:373
  27.9 1.9 %collective-permute-done.10.near = bf16[256,1024]{1,0:T(8,128)(2,1)S(1)} collective-permute-done((bf16[256,1024]{1,0:T(8,128)(2,1)S(1)}, bf16[256,1024]{1,0:T(8,128)(2,1)S(1)}, u32[]{:S(2)}, u32[]{:S(2)}) %collective-permute-start.10) | collective-permute-done | bytes 524320 | tf_op jit(solution)/shard_map/cotangent_2/ppermute | solution.py:373
  29.9 2.0 %forward_1.1 = (f32[16,128]{1,0:T(8,128)S(1)}, bf16[256,1024]{1,0:T(8,128)(2,1)S(1)}, f32[256,384]{1,0:T(8,128)S(1)}, f32[256,384]{1,0:T(8,128)S(1)}, bf16[256,3...) custom-call(s32[2]{0:T(128)S(1)} %pad_add_fusion.expert_ref, ...), custom_call_target="tpu_custom_call" | custom-call | flops 1048576 | bytes 1024 | tf_op jit(solution)/shard_map/forward_1/pallas_call | solution.py:122
  31.8 2.2 %collective-permute-start.17 = (bf16[256,1024]{1,0:T(8,128)(2,1)S(1)}, bf16[256,1024]{1,0:T(8,128)(2,1)S(1)}, u32[]{:S(2)}, u32[]{:S(2)}) collective-permute-start(bf16[256,1024]{1,0:T(8,128)(2,1)S(1)} %collective-permute-done.10.near), channel_id=1, source_target_pairs={{0,4},{1,3},{4,8},{5,1},{8,12},{9,5},{12,14},{13,9},{14,10},{15,13... | collective-permute-start | bytes 1572872 | tf_op jit(solution)/shard_map/cotangent_3/ppermute | solution.py:373
  35.8 2.2 %collective-permute-start.20 = (bf16[144,1024]{1,0:T(8,128)(2,1)S(1)}, bf16[144,1024]{1,0:T(8,128)(2,1)S(1)}, u32[]{:S(2)}, u32[]{:S(2)}) collective-permute-start(bf16[144,1024]{1,0:T(8,128)(2,1)S(1)} %slice.6), channel_id=1, source_target_pairs={{0,4},{1,3},{4,8},{5,1},{8,12},{9,5},{12,14},{13,9},{14,10},{15,13... | collective-permute-start | bytes 884744 | tf_op jit(solution)/shard_map/tokens_4/ppermute | solution.py:373
  38.0 2.0 %forward_2.1 = (f32[16,128]{1,0:T(8,128)S(1)}, bf16[256,1024]{1,0:T(8,128)(2,1)S(1)}, f32[256,384]{1,0:T(8,128)S(1)}, f32[256,384]{1,0:T(8,128)S(1)}, bf16[256,3...) custom-call(s32[2]{0:T(128)S(1)} %pad_add_fusion.expert_ref, ...), custom_call_target="tpu_custom_call" | custom-call | flops 4294967296 | bytes 1024 | tf_op jit(solution)/shard_map/forward_2/pallas_call | solution.py:122
  41.5 2.2 %collective-permute-start.22 = (bf16[128,1024]{1,0:T(8,128)(2,1)S(1)}, bf16[128,1024]{1,0:T(8,128)(2,1)S(1)}, u32[]{:S(2)}, u32[]{:S(2)}) collective-permute-start(bf16[128,1024]{1,0:T(8,128)(2,1)S(1)} %slice.7), channel_id=1, source_target_pairs={{0,4},{1,3},{4,8},{5,1},{8,12},{9,5},{12,14},{13,9},{14,10},{15,13... | collective-permute-start | bytes 786440 | tf_op jit(solution)/shard_map/cotangent_4/ppermute | solution.py:373
  43.6 2.0 %forward_3.1 = (f32[16,128]{1,0:T(8,128)S(1)}, bf16[256,1024]{1,0:T(8,128)(2,1)S(1)}, f32[256,384]{1,0:T(8,128)S(1)}, f32[256,384]{1,0:T(8,128)S(1)}, bf16[256,3...) custom-call(s32[2]{0:T(128)S(1)} %pad_add_fusion.expert_ref, ...), custom_call_target="tpu_custom_call" | custom-call | flops 1048576 | bytes 1024 | tf_op jit(solution)/shard_map/forward_3/pallas_call | solution.py:122
  45.6 2.2 %pair_forward.1 = (f32[16,128]{1,0:T(8,128)S(1)}, f32[128,384]{1,0:T(8,128)S(1)}, f32[128,384]{1,0:T(8,128)S(1)}, bf16[128,1024]{1,0:T(8,128)(2,1)S(1)}) custom-call(s32[2]{0:T(128)S(1)} %pad_add_fusion.expert_ref, bf16[144,1024]{1,0:T(8,128)(2,1)S(1)} %collective-permute-done.20.near, bf16[1024,384]{1,0:T(8,128)(2,1)S(1)} %get-tuple-element.139.w_gate.refs_0_, ...), custom_call_target="tpu_custom_call" | custom-call | flops 1073741824 | bytes 1024 | tf_op jit(solution)/shard_map/pair_forward/pallas_call | solution.py:122
  49.9 1.8 %pair_backward.1 = bf16[128,1024]{1,0:T(8,128)(2,1)S(1)} custom-call(f32[16,128]{1,0:T(8,128)S(1)} %get-tuple-element.157.info_ref, f32[128,384]{1,0:T(8,128)S(1)} %get-tuple-element.158.slope_ref, f32[128,384]{1,0:T(8,128)S(1)} %get-tuple-element.159.act_ref, bf16[128,1024]{1,0:T(8,128)(2,1)S(1)} %collective-permute-done.22.near, ...), custom_call_target="tpu_custom_call" | custom-call | flops 268435456 | bytes 1024 | tf_op jit(solution)/shard_map/pair_backward/pallas_call | solution.py:122
  62.4 2.2 %weights_0.1 = bf16[1024,384]{1,0:T(8,128)(2,1)} custom-call(bf16[128,1024]{1,0:T(8,128)(2,1)S(1)} %get-tuple-element.182.refs_0_, bf16[256,1024]{1,0:T(8,128)(2,1)S(1)} %get-tuple-element.183.refs_1_, bf16[256,1024]{1,0:T(8,128)(2,1)S(1)} %get-tuple-element.184.refs_2_, bf16[256,1024]{1,0:T(8,128)(2,1)S(1)} %get-tuple-element.185.refs_3_, ...), custom_call_target="tpu_custom_call" | custom-call | flops 1048576 | bytes 1024 | tf_op jit(solution)/shard_map/weights_0/pallas_call | solution.py:122
  64.6 2.2 %weights_1.1 = bf16[1024,384]{1,0:T(8,128)(2,1)} custom-call(bf16[128,1024]{1,0:T(8,128)(2,1)S(1)} %get-tuple-element.182.refs_0_, bf16[256,1024]{1,0:T(8,128)(2,1)S(1)} %get-tuple-element.183.refs_1_, bf16[256,1024]{1,0:T(8,128)(2,1)S(1)} %get-tuple-element.184.refs_2_, bf16[256,1024]{1,0:T(8,128)(2,1)S(1)} %get-tuple-element.185.refs_3_, ...), custom_call_target="tpu_custom_call" | custom-call | flops 1048576 | bytes 1024 | tf_op jit(solution)/shard_map/weights_1/pallas_call | solution.py:122
  72.4 2.2 %weights_2.1 = bf16[1024,384]{1,0:T(8,128)(2,1)} custom-call(bf16[128,1024]{1,0:T(8,128)(2,1)S(1)} %get-tuple-element.196.refs_0_, bf16[256,1024]{1,0:T(8,128)(2,1)S(1)} %get-tuple-element.197.refs_1_, bf16[256,1024]{1,0:T(8,128)(2,1)S(1)} %get-tuple-element.198.refs_2_, bf16[256,1024]{1,0:T(8,128)(2,1)S(1)} %get-tuple-element.199.refs_3_, ...), custom_call_target="tpu_custom_call" | custom-call | flops 1048576 | bytes 1024 | tf_op jit(solution)/shard_map/weights_2/pallas_call | solution.py:122
  74.6 1.8 %collective-permute-done.30.refs_0_ = bf16[256,1024]{1,0:T(8,128)(2,1)S(1)} collective-permute-done((bf16[256,1024]{1,0:T(8,128)(2,1)S(1)}, bf16[256,1024]{1,0:T(8,128)(2,1)S(1)}, u32[]{:S(2)}, u32[]{:S(2)}) %collective-permute-start.30) | collective-permute-done | bytes 524320 | tf_op jit(solution)/shard_map/mixed_2/ppermute | solution.py:373
  78.2 3.9 %collective-permute-done.36.refs_0_ = bf16[256,1024]{1,0:T(8,128)(2,1)S(1)} collective-permute-done((bf16[256,1024]{1,0:T(8,128)(2,1)S(1)}, bf16[256,1024]{1,0:T(8,128)(2,1)S(1)}, u32[]{:S(2)}, u32[]{:S(2)}) %collective-permute-start.36) | collective-permute-done | bytes 524320 | tf_op jit(solution)/shard_map/grad_2/ppermute | solution.py:373
  84.8 2.3 %collective-permute-done.34.refs_1_ = bf16[128,1024]{1,0:T(8,128)(2,1)S(1)} collective-permute-done((bf16[128,1024]{1,0:T(8,128)(2,1)S(1)}, bf16[128,1024]{1,0:T(8,128)(2,1)S(1)}, u32[]{:S(2)}, u32[]{:S(2)}) %collective-permute-start.34) | collective-permute-done | bytes 262176 | tf_op jit(solution)/shard_map/mixed_1_crossing/ppermute | solution.py:373
  88.1 2.3 %collective-permute-done.38.first = bf16[128,1024]{1,0:T(8,128)(2,1)S(1)} collective-permute-done((bf16[128,1024]{1,0:T(8,128)(2,1)S(1)}, bf16[128,1024]{1,0:T(8,128)(2,1)S(1)}, u32[]{:S(2)}, u32[]{:S(2)}) %collective-permute-start.38) | collective-permute-done | bytes 262176 | tf_op jit(solution)/shard_map/grad_1/ppermute | solution.py:373
  90.5 2.3 %collective-permute-done.39.second = bf16[128,1024]{1,0:T(8,128)(2,1)S(1)} collective-permute-done((bf16[128,1024]{1,0:T(8,128)(2,1)S(1)}, bf16[128,1024]{1,0:T(8,128)(2,1)S(1)}, u32[]{:S(2)}, u32[]{:S(2)}) %collective-permute-start.39) | collective-permute-done | bytes 262176 | tf_op jit(solution)/shard_map/grad_1_crossing/ppermute | solution.py:373
  (89 shorter events, 38.0 us)
Async XLA Ops:
  2.2 9.0 %collective-permute-start = (bf16[144,1024]{1,0:T(8,128)(2,1)S(1)}, bf16[144,1024]{1,0:T(8,128)(2,1)S(1)}, u32[]{:S(2)}, u32[]{:S(2)}) collective-permute-start(bf16[144,1024]{1,0:T(8,128)(2,1)S(1)} %payload.1.near), channel_id=1, source_target_pairs={{0,4},{1,3},{4,8},{5,1},{8,12},{9,5},{12,14},{13,9},{14,10},{15,13... | collective-permute-start | bytes 884744 | tf_op jit(solution)/shard_map/tokens_1/ppermute | solution.py:373
  4.9 9.4 %collective-permute-start.1 = (bf16[144,1024]{1,0:T(8,128)(2,1)S(1)}, bf16[144,1024]{1,0:T(8,128)(2,1)S(1)}, u32[]{:S(2)}, u32[]{:S(2)}) collective-permute-start(bf16[144,1024]{1,0:T(8,128)(2,1)S(1)} %payload.1.near), channel_id=1, source_target_pairs={{0,3},{1,4},{4,1},{5,8},{8,5},{9,12},{12,9},{13,14},{14,13},{15,10... | collective-permute-start | bytes 884744 | tf_op jit(solution)/shard_map/tokens_1_crossing/ppermute | solution.py:373
  6.1 10.2 %collective-permute-start.2 = (bf16[144,1024]{1,0:T(8,128)(2,1)S(1)}, bf16[144,1024]{1,0:T(8,128)(2,1)S(1)}, u32[]{:S(2)}, u32[]{:S(2)}) collective-permute-start(bf16[144,1024]{1,0:T(8,128)(2,1)S(1)} %payload.1.near), channel_id=1, source_target_pairs={{0,1},{1,0},{2,3},{3,2},{4,5},{5,4},{6,7},{7,6},{8,9},{9,8},{10,11... | collective-permute-start | bytes 884744 | tf_op jit(solution)/shard_map/tokens_0_swap/ppermute | solution.py:373
  6.7 11.6 %collective-permute-start.6 = (bf16[256,1024]{1,0:T(8,128)(2,1)S(1)}, bf16[256,1024]{1,0:T(8,128)(2,1)S(1)}, u32[]{:S(2)}, u32[]{:S(2)}) collective-permute-start(bf16[256,1024]{1,0:T(8,128)(2,1)S(1)} %join_0.1), channel_id=1, source_target_pairs={{0,4},{1,3},{4,8},{5,1},{8,12},{9,5},{12,14},{13,9},{14,10},{15,13... | collective-permute-start | bytes 1572872 | tf_op jit(solution)/shard_map/cotangent_1/ppermute | solution.py:373
  14.3 9.9 %collective-permute-start.4 = (bf16[272,1024]{1,0:T(8,128)(2,1)S(1)}, bf16[272,1024]{1,0:T(8,128)(2,1)S(1)}, u32[]{:S(2)}, u32[]{:S(2)}) collective-permute-start(bf16[272,1024]{1,0:T(8,128)(2,1)S(1)} %join_1.1.near), channel_id=1, source_target_pairs={{0,4},{1,3},{4,8},{5,1},{8,12},{9,5},{12,14},{13,9},{14,10},{15,13... | collective-permute-start | bytes 1671176 | tf_op jit(solution)/shard_map/tokens_2/ppermute | solution.py:373
  15.8 8.4 %collective-permute-start.7 = (bf16[272,1024]{1,0:T(8,128)(2,1)S(1)}, bf16[272,1024]{1,0:T(8,128)(2,1)S(1)}, u32[]{:S(2)}, u32[]{:S(2)}) collective-permute-start(bf16[272,1024]{1,0:T(8,128)(2,1)S(1)} %join_1.1.near), channel_id=1, source_target_pairs={{0,1},{1,0},{2,3},{3,2},{4,5},{5,4},{6,7},{7,6},{8,9},{9,8},{10,11... | collective-permute-start | bytes 1671176 | tf_op jit(solution)/shard_map/tokens_1_swap/ppermute | solution.py:373
  16.0 9.7 %collective-permute-start.12 = (bf16[1024,384]{1,0:T(8,128)(2,1)S(1)}, bf16[1024,384]{1,0:T(8,128)(2,1)S(1)}, u32[]{:S(2)}, u32[]{:S(2)}) collective-permute-start(bf16[1024,384]{1,0:T(8,128)(2,1)S(1)} %get-tuple-element.139.w_gate.refs_0_), channel_id=1, source_target_pairs={{0,1},{1,0},{2,3},{3,2},{4,5},{5,4},{6,7},{7,6},{8,9},{9,8},{10,11... | collective-permute-start | bytes 2359304 | tf_op jit(solution)/shard_map/weights_swap/ppermute | solution.py:373
  18.3 11.6 %collective-permute-start.10 = (bf16[256,1024]{1,0:T(8,128)(2,1)S(1)}, bf16[256,1024]{1,0:T(8,128)(2,1)S(1)}, u32[]{:S(2)}, u32[]{:S(2)}) collective-permute-start(bf16[256,1024]{1,0:T(8,128)(2,1)S(1)} %collective-permute-done.6.near), channel_id=1, source_target_pairs={{0,4},{1,3},{4,8},{5,1},{8,12},{9,5},{12,14},{13,9},{14,10},{15,13... | collective-permute-start | bytes 1572872 | tf_op jit(solution)/shard_map/cotangent_2/ppermute | solution.py:373
  20.4 14.9 %collective-permute-start.13 = (bf16[1024,384]{1,0:T(8,128)(2,1)S(1)}, bf16[1024,384]{1,0:T(8,128)(2,1)S(1)}, u32[]{:S(2)}, u32[]{:S(2)}) collective-permute-start(bf16[1024,384]{1,0:T(8,128)(2,1)S(1)} %get-tuple-element.140.w_up.refs_1_), channel_id=1, source_target_pairs={{0,1},{1,0},{2,3},{3,2},{4,5},{5,4},{6,7},{7,6},{8,9},{9,8},{10,11... | collective-permute-start | bytes 2359304 | tf_op jit(solution)/shard_map/weights_swap/ppermute | solution.py:373
  24.2 11.1 %collective-permute-start.14 = (bf16[1024,384]{1,0:T(8,128)(2,1)S(1)}, bf16[1024,384]{1,0:T(8,128)(2,1)S(1)}, u32[]{:S(2)}, u32[]{:S(2)}) collective-permute-start(bf16[1024,384]{1,0:T(8,128)(2,1)S(1)} %get-tuple-element.141.w_down.refs_2_), channel_id=1, source_target_pairs={{0,1},{1,0},{2,3},{3,2},{4,5},{5,4},{6,7},{7,6},{8,9},{9,8},{10,11... | collective-permute-start | bytes 2359304 | tf_op jit(solution)/shard_map/weights_swap/ppermute | solution.py:373
  25.8 10.1 %collective-permute-start.9 = (bf16[272,1024]{1,0:T(8,128)(2,1)S(1)}, bf16[272,1024]{1,0:T(8,128)(2,1)S(1)}, u32[]{:S(2)}, u32[]{:S(2)}) collective-permute-start(bf16[272,1024]{1,0:T(8,128)(2,1)S(1)} %collective-permute-done.4.near), channel_id=1, source_target_pairs={{0,4},{1,3},{4,8},{5,1},{8,12},{9,5},{12,14},{13,9},{14,10},{15,13... | collective-permute-start | bytes 1671176 | tf_op jit(solution)/shard_map/tokens_3/ppermute | solution.py:373
  31.8 9.6 %collective-permute-start.17 = (bf16[256,1024]{1,0:T(8,128)(2,1)S(1)}, bf16[256,1024]{1,0:T(8,128)(2,1)S(1)}, u32[]{:S(2)}, u32[]{:S(2)}) collective-permute-start(bf16[256,1024]{1,0:T(8,128)(2,1)S(1)} %collective-permute-done.10.near), channel_id=1, source_target_pairs={{0,4},{1,3},{4,8},{5,1},{8,12},{9,5},{12,14},{13,9},{14,10},{15,13... | collective-permute-start | bytes 1572872 | tf_op jit(solution)/shard_map/cotangent_3/ppermute | solution.py:373
  35.8 9.8 %collective-permute-start.20 = (bf16[144,1024]{1,0:T(8,128)(2,1)S(1)}, bf16[144,1024]{1,0:T(8,128)(2,1)S(1)}, u32[]{:S(2)}, u32[]{:S(2)}) collective-permute-start(bf16[144,1024]{1,0:T(8,128)(2,1)S(1)} %slice.6), channel_id=1, source_target_pairs={{0,4},{1,3},{4,8},{5,1},{8,12},{9,5},{12,14},{13,9},{14,10},{15,13... | collective-permute-start | bytes 884744 | tf_op jit(solution)/shard_map/tokens_4/ppermute | solution.py:373
  41.4 11.9 %collective-permute-start.23 = (bf16[256,1024]{1,0:T(8,128)(2,1)S(1)}, bf16[256,1024]{1,0:T(8,128)(2,1)S(1)}, u32[]{:S(2)}, u32[]{:S(2)}) collective-permute-start(bf16[256,1024]{1,0:T(8,128)(2,1)S(1)} %collective-permute-done.17.near), channel_id=1, source_target_pairs={{0,1},{1,0},{2,3},{3,2},{4,5},{5,4},{6,7},{7,6},{8,9},{9,8},{10,11... | collective-permute-start | bytes 1572872 | tf_op jit(solution)/shard_map/cotangent_3_swap/ppermute | solution.py:373
  41.5 8.5 %collective-permute-start.22 = (bf16[128,1024]{1,0:T(8,128)(2,1)S(1)}, bf16[128,1024]{1,0:T(8,128)(2,1)S(1)}, u32[]{:S(2)}, u32[]{:S(2)}) collective-permute-start(bf16[128,1024]{1,0:T(8,128)(2,1)S(1)} %slice.7), channel_id=1, source_target_pairs={{0,4},{1,3},{4,8},{5,1},{8,12},{9,5},{12,14},{13,9},{14,10},{15,13... | collective-permute-start | bytes 786440 | tf_op jit(solution)/shard_map/cotangent_4/ppermute | solution.py:373
  55.1 11.8 %collective-permute-start.24 = (bf16[256,1024]{1,0:T(8,128)(2,1)S(1)}, bf16[256,1024]{1,0:T(8,128)(2,1)S(1)}, u32[]{:S(2)}, u32[]{:S(2)}) collective-permute-start(bf16[256,1024]{1,0:T(8,128)(2,1)S(1)} %mixed_sums_3.1), channel_id=1, source_target_pairs={{0,4},{1,3},{4,8},{5,1},{8,12},{9,5},{12,14},{13,9},{14,10},{15,13... | collective-permute-start | bytes 1572872 | tf_op jit(solution)/shard_map/mixed_3/ppermute | solution.py:373
  58.5 11.6 %collective-permute-start.32 = (bf16[256,1024]{1,0:T(8,128)(2,1)S(1)}, bf16[256,1024]{1,0:T(8,128)(2,1)S(1)}, u32[]{:S(2)}, u32[]{:S(2)}) collective-permute-start(bf16[256,1024]{1,0:T(8,128)(2,1)S(1)} %grad_sums_3.1), channel_id=1, source_target_pairs={{0,4},{1,3},{4,8},{5,1},{8,12},{9,5},{12,14},{13,9},{14,10},{15,13... | collective-permute-start | bytes 1572872 | tf_op jit(solution)/shard_map/grad_3/ppermute | solution.py:373
  60.6 9.5 %collective-permute-start.31 = (bf16[128,1024]{1,0:T(8,128)(2,1)S(1)}, bf16[128,1024]{1,0:T(8,128)(2,1)S(1)}, u32[]{:S(2)}, u32[]{:S(2)}) collective-permute-start(bf16[128,1024]{1,0:T(8,128)(2,1)S(1)} %get-tuple-element.189), channel_id=1, source_target_pairs={{0,1},{1,0},{2,3},{3,2},{4,5},{5,4},{6,7},{7,6},{8,9},{9,8},{10,11... | collective-permute-start | bytes 786440 | tf_op jit(solution)/shard_map/grad_2_swap/ppermute | solution.py:373
  67.2 9.2 %collective-permute-start.30 = (bf16[256,1024]{1,0:T(8,128)(2,1)S(1)}, bf16[256,1024]{1,0:T(8,128)(2,1)S(1)}, u32[]{:S(2)}, u32[]{:S(2)}) collective-permute-start(bf16[256,1024]{1,0:T(8,128)(2,1)S(1)} %mixed_sums_2.1), channel_id=1, source_target_pairs={{0,4},{1,3},{4,8},{5,1},{8,12},{9,5},{12,14},{13,9},{14,10},{15,13... | collective-permute-start | bytes 1572872 | tf_op jit(solution)/shard_map/mixed_2/ppermute | solution.py:373
  70.4 11.6 %collective-permute-start.36 = (bf16[256,1024]{1,0:T(8,128)(2,1)S(1)}, bf16[256,1024]{1,0:T(8,128)(2,1)S(1)}, u32[]{:S(2)}, u32[]{:S(2)}) collective-permute-start(bf16[256,1024]{1,0:T(8,128)(2,1)S(1)} %grad_sums_2.1), channel_id=1, source_target_pairs={{0,4},{1,3},{4,8},{5,1},{8,12},{9,5},{12,14},{13,9},{14,10},{15,13... | collective-permute-start | bytes 1572872 | tf_op jit(solution)/shard_map/grad_2/ppermute | solution.py:373
  71.8 10.2 %collective-permute-start.35 = (bf16[128,1024]{1,0:T(8,128)(2,1)S(1)}, bf16[128,1024]{1,0:T(8,128)(2,1)S(1)}, u32[]{:S(2)}, u32[]{:S(2)}) collective-permute-start(bf16[128,1024]{1,0:T(8,128)(2,1)S(1)} %get-tuple-element.205), channel_id=1, source_target_pairs={{0,1},{1,0},{2,3},{3,2},{4,5},{5,4},{6,7},{7,6},{8,9},{9,8},{10,11... | collective-permute-start | bytes 786440 | tf_op jit(solution)/shard_map/grad_1_swap/ppermute | solution.py:373
  72.4 11.4 %collective-permute-start.37 = (bf16[64,1024]{1,0:T(8,128)(2,1)S(1)}, bf16[64,1024]{1,0:T(8,128)(2,1)S(1)}, u32[]{:S(2)}, u32[]{:S(2)}) collective-permute-start(bf16[64,1024]{1,0:T(8,128)(2,1)S(1)} %get-tuple-element.212), channel_id=1, source_target_pairs={{0,1},{1,0},{2,3},{3,2},{4,5},{5,4},{6,7},{7,6},{8,9},{9,8},{10,11... | collective-permute-start | bytes 393224 | tf_op jit(solution)/shard_map/grad_0_swap/ppermute | solution.py:373
  78.2 9.0 %collective-permute-start.34 = (bf16[128,1024]{1,0:T(8,128)(2,1)S(1)}, bf16[128,1024]{1,0:T(8,128)(2,1)S(1)}, u32[]{:S(2)}, u32[]{:S(2)}) collective-permute-start(bf16[128,1024]{1,0:T(8,128)(2,1)S(1)} %get-tuple-element.203), channel_id=1, source_target_pairs={{0,5},{1,2},{4,9},{5,0},{8,13},{9,4},{12,15},{13,8},{14,11},{15,12... | collective-permute-start | bytes 786440 | tf_op jit(solution)/shard_map/mixed_1_crossing/ppermute | solution.py:373
  83.8 9.0 %collective-permute-start.39 = (bf16[128,1024]{1,0:T(8,128)(2,1)S(1)}, bf16[128,1024]{1,0:T(8,128)(2,1)S(1)}, u32[]{:S(2)}, u32[]{:S(2)}) collective-permute-start(bf16[128,1024]{1,0:T(8,128)(2,1)S(1)} %get-tuple-element.208), channel_id=1, source_target_pairs={{0,5},{1,2},{4,9},{5,0},{8,13},{9,4},{12,15},{13,8},{14,11},{15,12... | collective-permute-start | bytes 786440 | tf_op jit(solution)/shard_map/grad_1_crossing/ppermute | solution.py:373
  (17 other events, 95.5 us)

commit v8 on v6

--- a/solution.py
+++ b/solution.py
@@ -581,7 +581,8 @@
         if step == last:
             cot_near[reach] = after(cot_near[reach], *grad_left)
             before += [run_forward(reach), run_backward(reach)]
-        before += some_job()
+        else:
+            before += some_job()
     while some_job():
         pass
     arrived = land(mixed_fly, *before, *grads)

time: 93.2 us -> 93.2 us (level)
  transfers between devices with their start and end apart: 40 -> 40, of which waited for: 15 -> 16; matrix products, arithmetic and copies ran while one was open for 0% -> 0% of each run, Pallas kernels for 31% -> 31%
where the time goes in v8:
time: 93.2 us; the launch traced here: 93 us
  starting transfers between devices  34.3 us (37%)
  Pallas kernels  31.3 us (34%)
  waiting for transfers between devices  26.4 us (28%)
    ppermute x40, starting transfers between devices, hop(): return lax.ppermute(value, 'expert', moves)  34.3 us
    pallas_call x27, Pallas kernels, call(): pl.pallas_call(body, out_shape=[pltpu.VMEM(a.shape, a.dtype) if near else...  31.3 us
    ppermute x40, waiting for transfers between devices, hop(): return lax.ppermute(value, 'expert', moves)  26.4 us
  transfers between devices with their start and end apart: 40, of which 16 were waited for; matrix products, arithmetic and copies ran while one was open for 0% of the time, Pallas kernels for 31%

profile of v8, /device:TPU:0, one launch (start us, length us, event | category | flops | bytes accessed | tf_op | source)
XLA Modules:
  0.0 93.0 jit_solution(3128543893865457854)
XLA Ops:
  2.2 2.6 %collective-permute-start = (bf16[144,1024]{1,0:T(8,128)(2,1)S(1)}, bf16[144,1024]{1,0:T(8,128)(2,1)S(1)}, u32[]{:S(2)}, u32[]{:S(2)}) collective-permute-start(bf16[144,1024]{1,0:T(8,128)(2,1)S(1)} %payload.1.near), channel_id=1, source_target_pairs={{0,4},{1,3},{4,8},{5,1},{8,12},{9,5},{12,14},{13,9},{14,10},{15,13... | collective-permute-start | bytes 884744 | tf_op jit(solution)/shard_map/tokens_1/ppermute | solution.py:369
  8.3 1.6 %stage.1 = (bf16[1024,384]{1,0:T(8,128)(2,1)S(1)}, bf16[1024,384]{1,0:T(8,128)(2,1)S(1)}, bf16[1024,384]{1,0:T(8,128)(2,1)S(1)}) custom-call(bf16[1024,384]{1,0:T(8,128)(2,1)} %bitcast.13, bf16[1024,384]{1,0:T(8,128)(2,1)} %bitcast.14, bf16[1024,384]{1,0:T(8,128)(2,1)} %bitcast.15), custom_call_target="tpu_custom_call" | custom-call | flops 1073741824 | bytes 1024 | tf_op jit(solution)/shard_map/stage/pallas_call | solution.py:122
  11.3 3.0 %collective-permute-done.1.second = bf16[144,1024]{1,0:T(8,128)(2,1)S(1)} collective-permute-done((bf16[144,1024]{1,0:T(8,128)(2,1)S(1)}, bf16[144,1024]{1,0:T(8,128)(2,1)S(1)}, u32[]{:S(2)}, u32[]{:S(2)}) %collective-permute-start.1) | collective-permute-done | bytes 294944 | tf_op jit(solution)/shard_map/tokens_1_crossing/ppermute | solution.py:369
  18.3 2.1 %collective-permute-start.10 = (bf16[256,1024]{1,0:T(8,128)(2,1)S(1)}, bf16[256,1024]{1,0:T(8,128)(2,1)S(1)}, u32[]{:S(2)}, u32[]{:S(2)}) collective-permute-start(bf16[256,1024]{1,0:T(8,128)(2,1)S(1)} %collective-permute-done.6.near), channel_id=1, source_target_pairs={{0,4},{1,3},{4,8},{5,1},{8,12},{9,5},{12,14},{13,9},{14,10},{15,13... | collective-permute-start | bytes 1572872 | tf_op jit(solution)/shard_map/cotangent_2/ppermute | solution.py:369
  20.4 3.9 %collective-permute-done.4.near = bf16[272,1024]{1,0:T(8,128)(2,1)S(1)} collective-permute-done((bf16[272,1024]{1,0:T(8,128)(2,1)S(1)}, bf16[272,1024]{1,0:T(8,128)(2,1)S(1)}, u32[]{:S(2)}, u32[]{:S(2)}) %collective-permute-start.4) | collective-permute-done | bytes 557088 | tf_op jit(solution)/shard_map/tokens_2/ppermute | solution.py:369
  25.8 2.2 %collective-permute-start.9 = (bf16[272,1024]{1,0:T(8,128)(2,1)S(1)}, bf16[272,1024]{1,0:T(8,128)(2,1)S(1)}, u32[]{:S(2)}, u32[]{:S(2)}) collective-permute-start(bf16[272,1024]{1,0:T(8,128)(2,1)S(1)} %collective-permute-done.4.near), channel_id=1, source_target_pairs={{0,4},{1,3},{4,8},{5,1},{8,12},{9,5},{12,14},{13,9},{14,10},{15,13... | collective-permute-start | bytes 1671176 | tf_op jit(solution)/shard_map/tokens_3/ppermute | solution.py:369
  27.9 1.9 %collective-permute-done.10.near = bf16[256,1024]{1,0:T(8,128)(2,1)S(1)} collective-permute-done((bf16[256,1024]{1,0:T(8,128)(2,1)S(1)}, bf16[256,1024]{1,0:T(8,128)(2,1)S(1)}, u32[]{:S(2)}, u32[]{:S(2)}) %collective-permute-start.10) | collective-permute-done | bytes 524320 | tf_op jit(solution)/shard_map/cotangent_2/ppermute | solution.py:369
  29.9 2.0 %forward_1.1 = (f32[16,128]{1,0:T(8,128)S(1)}, bf16[256,1024]{1,0:T(8,128)(2,1)S(1)}, f32[256,384]{1,0:T(8,128)S(1)}, f32[256,384]{1,0:T(8,128)S(1)}, bf16[256,3...) custom-call(s32[2]{0:T(128)S(1)} %pad_add_fusion.expert_ref, ...), custom_call_target="tpu_custom_call" | custom-call | flops 1048576 | bytes 1024 | tf_op jit(solution)/shard_map/forward_1/pallas_call | solution.py:122
  31.8 2.2 %collective-permute-start.17 = (bf16[256,1024]{1,0:T(8,128)(2,1)S(1)}, bf16[256,1024]{1,0:T(8,128)(2,1)S(1)}, u32[]{:S(2)}, u32[]{:S(2)}) collective-permute-start(bf16[256,1024]{1,0:T(8,128)(2,1)S(1)} %collective-permute-done.10.near), channel_id=1, source_target_pairs={{0,4},{1,3},{4,8},{5,1},{8,12},{9,5},{12,14},{13,9},{14,10},{15,13... | collective-permute-start | bytes 1572872 | tf_op jit(solution)/shard_map/cotangent_3/ppermute | solution.py:369
  35.8 2.2 %collective-permute-start.20 = (bf16[144,1024]{1,0:T(8,128)(2,1)S(1)}, bf16[144,1024]{1,0:T(8,128)(2,1)S(1)}, u32[]{:S(2)}, u32[]{:S(2)}) collective-permute-start(bf16[144,1024]{1,0:T(8,128)(2,1)S(1)} %slice.6), channel_id=1, source_target_pairs={{0,4},{1,3},{4,8},{5,1},{8,12},{9,5},{12,14},{13,9},{14,10},{15,13... | collective-permute-start | bytes 884744 | tf_op jit(solution)/shard_map/tokens_4/ppermute | solution.py:369
  38.0 2.0 %forward_2.1 = (f32[16,128]{1,0:T(8,128)S(1)}, bf16[256,1024]{1,0:T(8,128)(2,1)S(1)}, f32[256,384]{1,0:T(8,128)S(1)}, f32[256,384]{1,0:T(8,128)S(1)}, bf16[256,3...) custom-call(s32[2]{0:T(128)S(1)} %pad_add_fusion.expert_ref, ...), custom_call_target="tpu_custom_call" | custom-call | flops 4294967296 | bytes 1024 | tf_op jit(solution)/shard_map/forward_2/pallas_call | solution.py:122
  41.5 2.2 %collective-permute-start.22 = (bf16[128,1024]{1,0:T(8,128)(2,1)S(1)}, bf16[128,1024]{1,0:T(8,128)(2,1)S(1)}, u32[]{:S(2)}, u32[]{:S(2)}) collective-permute-start(bf16[128,1024]{1,0:T(8,128)(2,1)S(1)} %slice.7), channel_id=1, source_target_pairs={{0,4},{1,3},{4,8},{5,1},{8,12},{9,5},{12,14},{13,9},{14,10},{15,13... | collective-permute-start | bytes 786440 | tf_op jit(solution)/shard_map/cotangent_4/ppermute | solution.py:369
  43.6 2.0 %forward_3.1 = (f32[16,128]{1,0:T(8,128)S(1)}, bf16[256,1024]{1,0:T(8,128)(2,1)S(1)}, f32[256,384]{1,0:T(8,128)S(1)}, f32[256,384]{1,0:T(8,128)S(1)}, bf16[256,3...) custom-call(s32[2]{0:T(128)S(1)} %pad_add_fusion.expert_ref, ...), custom_call_target="tpu_custom_call" | custom-call | flops 1048576 | bytes 1024 | tf_op jit(solution)/shard_map/forward_3/pallas_call | solution.py:122
  45.6 2.2 %pair_forward.1 = (f32[16,128]{1,0:T(8,128)S(1)}, f32[128,384]{1,0:T(8,128)S(1)}, f32[128,384]{1,0:T(8,128)S(1)}, bf16[128,1024]{1,0:T(8,128)(2,1)S(1)}) custom-call(s32[2]{0:T(128)S(1)} %pad_add_fusion.expert_ref, bf16[144,1024]{1,0:T(8,128)(2,1)S(1)} %collective-permute-done.20.near, bf16[1024,384]{1,0:T(8,128)(2,1)S(1)} %get-tuple-element.139.w_gate.refs_0_, ...), custom_call_target="tpu_custom_call" | custom-call | flops 1073741824 | bytes 1024 | tf_op jit(solution)/shard_map/pair_forward/pallas_call | solution.py:122
  49.9 1.8 %pair_backward.1 = bf16[128,1024]{1,0:T(8,128)(2,1)S(1)} custom-call(f32[16,128]{1,0:T(8,128)S(1)} %get-tuple-element.157.info_ref, f32[128,384]{1,0:T(8,128)S(1)} %get-tuple-element.158.slope_ref, f32[128,384]{1,0:T(8,128)S(1)} %get-tuple-element.159.act_ref, bf16[128,1024]{1,0:T(8,128)(2,1)S(1)} %collective-permute-done.22.near, ...), custom_call_target="tpu_custom_call" | custom-call | flops 268435456 | bytes 1024 | tf_op jit(solution)/shard_map/pair_backward/pallas_call | solution.py:122
  62.4 2.1 %collective-permute-done.24.refs_0_ = bf16[256,1024]{1,0:T(8,128)(2,1)S(1)} collective-permute-done((bf16[256,1024]{1,0:T(8,128)(2,1)S(1)}, bf16[256,1024]{1,0:T(8,128)(2,1)S(1)}, u32[]{:S(2)}, u32[]{:S(2)}) %collective-permute-start.24) | collective-permute-done | bytes 524320 | tf_op jit(solution)/shard_map/mixed_3/ppermute | solution.py:369
  66.2 2.2 %weights_0.1 = bf16[1024,384]{1,0:T(8,128)(2,1)} custom-call(bf16[128,1024]{1,0:T(8,128)(2,1)S(1)} %get-tuple-element.185.refs_0_, bf16[256,1024]{1,0:T(8,128)(2,1)S(1)} %get-tuple-element.186.refs_1_, bf16[256,1024]{1,0:T(8,128)(2,1)S(1)} %get-tuple-element.187.refs_2_, bf16[256,1024]{1,0:T(8,128)(2,1)S(1)} %get-tuple-element.188.refs_3_, ...), custom_call_target="tpu_custom_call" | custom-call | flops 1048576 | bytes 1024 | tf_op jit(solution)/shard_map/weights_0/pallas_call | solution.py:122
  68.4 1.6 %collective-permute-done.32.refs_0_ = bf16[256,1024]{1,0:T(8,128)(2,1)S(1)} collective-permute-done((bf16[256,1024]{1,0:T(8,128)(2,1)S(1)}, bf16[256,1024]{1,0:T(8,128)(2,1)S(1)}, u32[]{:S(2)}, u32[]{:S(2)}) %collective-permute-start.32) | collective-permute-done | bytes 524320 | tf_op jit(solution)/shard_map/grad_3/ppermute | solution.py:369
  72.3 2.2 %weights_1.1 = bf16[1024,384]{1,0:T(8,128)(2,1)} custom-call(bf16[128,1024]{1,0:T(8,128)(2,1)S(1)} %get-tuple-element.185.refs_0_, bf16[256,1024]{1,0:T(8,128)(2,1)S(1)} %get-tuple-element.186.refs_1_, bf16[256,1024]{1,0:T(8,128)(2,1)S(1)} %get-tuple-element.187.refs_2_, bf16[256,1024]{1,0:T(8,128)(2,1)S(1)} %get-tuple-element.188.refs_3_, ...), custom_call_target="tpu_custom_call" | custom-call | flops 1048576 | bytes 1024 | tf_op jit(solution)/shard_map/weights_1/pallas_call | solution.py:122
  77.5 2.2 %weights_2.1 = bf16[1024,384]{1,0:T(8,128)(2,1)} custom-call(bf16[128,1024]{1,0:T(8,128)(2,1)S(1)} %get-tuple-element.201.refs_0_, bf16[256,1024]{1,0:T(8,128)(2,1)S(1)} %get-tuple-element.202.refs_1_, bf16[256,1024]{1,0:T(8,128)(2,1)S(1)} %get-tuple-element.203.refs_2_, bf16[256,1024]{1,0:T(8,128)(2,1)S(1)} %get-tuple-element.204.refs_3_, ...), custom_call_target="tpu_custom_call" | custom-call | flops 1048576 | bytes 1024 | tf_op jit(solution)/shard_map/weights_2/pallas_call | solution.py:122
  79.7 1.6 %collective-permute-done.36.refs_0_ = bf16[256,1024]{1,0:T(8,128)(2,1)S(1)} collective-permute-done((bf16[256,1024]{1,0:T(8,128)(2,1)S(1)}, bf16[256,1024]{1,0:T(8,128)(2,1)S(1)}, u32[]{:S(2)}, u32[]{:S(2)}) %collective-permute-start.36) | collective-permute-done | bytes 524320 | tf_op jit(solution)/shard_map/grad_2/ppermute | solution.py:369
  84.1 2.3 %collective-permute-done.34.refs_1_ = bf16[128,1024]{1,0:T(8,128)(2,1)S(1)} collective-permute-done((bf16[128,1024]{1,0:T(8,128)(2,1)S(1)}, bf16[128,1024]{1,0:T(8,128)(2,1)S(1)}, u32[]{:S(2)}, u32[]{:S(2)}) %collective-permute-start.34) | collective-permute-done | bytes 262176 | tf_op jit(solution)/shard_map/mixed_1_crossing/ppermute | solution.py:369
  87.4 2.3 %collective-permute-done.38.refs_0_ = bf16[128,1024]{1,0:T(8,128)(2,1)S(1)} collective-permute-done((bf16[128,1024]{1,0:T(8,128)(2,1)S(1)}, bf16[128,1024]{1,0:T(8,128)(2,1)S(1)}, u32[]{:S(2)}, u32[]{:S(2)}) %collective-permute-start.38) | collective-permute-done | bytes 262176 | tf_op jit(solution)/shard_map/grad_1/ppermute | solution.py:369
  89.7 2.3 %collective-permute-done.39.refs_1_ = bf16[128,1024]{1,0:T(8,128)(2,1)S(1)} collective-permute-done((bf16[128,1024]{1,0:T(8,128)(2,1)S(1)}, bf16[128,1024]{1,0:T(8,128)(2,1)S(1)}, u32[]{:S(2)}, u32[]{:S(2)}) %collective-permute-start.39) | collective-permute-done | bytes 262176 | tf_op jit(solution)/shard_map/grad_1_crossing/ppermute | solution.py:369
  (88 shorter events, 39.5 us)
Async XLA Ops:
  2.2 9.0 %collective-permute-start = (bf16[144,1024]{1,0:T(8,128)(2,1)S(1)}, bf16[144,1024]{1,0:T(8,128)(2,1)S(1)}, u32[]{:S(2)}, u32[]{:S(2)}) collective-permute-start(bf16[144,1024]{1,0:T(8,128)(2,1)S(1)} %payload.1.near), channel_id=1, source_target_pairs={{0,4},{1,3},{4,8},{5,1},{8,12},{9,5},{12,14},{13,9},{14,10},{15,13... | collective-permute-start | bytes 884744 | tf_op jit(solution)/shard_map/tokens_1/ppermute | solution.py:369
  4.9 9.4 %collective-permute-start.1 = (bf16[144,1024]{1,0:T(8,128)(2,1)S(1)}, bf16[144,1024]{1,0:T(8,128)(2,1)S(1)}, u32[]{:S(2)}, u32[]{:S(2)}) collective-permute-start(bf16[144,1024]{1,0:T(8,128)(2,1)S(1)} %payload.1.near), channel_id=1, source_target_pairs={{0,3},{1,4},{4,1},{5,8},{8,5},{9,12},{12,9},{13,14},{14,13},{15,10... | collective-permute-start | bytes 884744 | tf_op jit(solution)/shard_map/tokens_1_crossing/ppermute | solution.py:369
  6.1 10.2 %collective-permute-start.2 = (bf16[144,1024]{1,0:T(8,128)(2,1)S(1)}, bf16[144,1024]{1,0:T(8,128)(2,1)S(1)}, u32[]{:S(2)}, u32[]{:S(2)}) collective-permute-start(bf16[144,1024]{1,0:T(8,128)(2,1)S(1)} %payload.1.near), channel_id=1, source_target_pairs={{0,1},{1,0},{2,3},{3,2},{4,5},{5,4},{6,7},{7,6},{8,9},{9,8},{10,11... | collective-permute-start | bytes 884744 | tf_op jit(solution)/shard_map/tokens_0_swap/ppermute | solution.py:369
  6.7 11.6 %collective-permute-start.6 = (bf16[256,1024]{1,0:T(8,128)(2,1)S(1)}, bf16[256,1024]{1,0:T(8,128)(2,1)S(1)}, u32[]{:S(2)}, u32[]{:S(2)}) collective-permute-start(bf16[256,1024]{1,0:T(8,128)(2,1)S(1)} %join_0.1), channel_id=1, source_target_pairs={{0,4},{1,3},{4,8},{5,1},{8,12},{9,5},{12,14},{13,9},{14,10},{15,13... | collective-permute-start | bytes 1572872 | tf_op jit(solution)/shard_map/cotangent_1/ppermute | solution.py:369
  14.3 9.9 %collective-permute-start.4 = (bf16[272,1024]{1,0:T(8,128)(2,1)S(1)}, bf16[272,1024]{1,0:T(8,128)(2,1)S(1)}, u32[]{:S(2)}, u32[]{:S(2)}) collective-permute-start(bf16[272,1024]{1,0:T(8,128)(2,1)S(1)} %join_1.1.near), channel_id=1, source_target_pairs={{0,4},{1,3},{4,8},{5,1},{8,12},{9,5},{12,14},{13,9},{14,10},{15,13... | collective-permute-start | bytes 1671176 | tf_op jit(solution)/shard_map/tokens_2/ppermute | solution.py:369
  15.8 8.4 %collective-permute-start.7 = (bf16[272,1024]{1,0:T(8,128)(2,1)S(1)}, bf16[272,1024]{1,0:T(8,128)(2,1)S(1)}, u32[]{:S(2)}, u32[]{:S(2)}) collective-permute-start(bf16[272,1024]{1,0:T(8,128)(2,1)S(1)} %join_1.1.near), channel_id=1, source_target_pairs={{0,1},{1,0},{2,3},{3,2},{4,5},{5,4},{6,7},{7,6},{8,9},{9,8},{10,11... | collective-permute-start | bytes 1671176 | tf_op jit(solution)/shard_map/tokens_1_swap/ppermute | solution.py:369
  16.0 9.7 %collective-permute-start.12 = (bf16[1024,384]{1,0:T(8,128)(2,1)S(1)}, bf16[1024,384]{1,0:T(8,128)(2,1)S(1)}, u32[]{:S(2)}, u32[]{:S(2)}) collective-permute-start(bf16[1024,384]{1,0:T(8,128)(2,1)S(1)} %get-tuple-element.139.w_gate.refs_0_), channel_id=1, source_target_pairs={{0,1},{1,0},{2,3},{3,2},{4,5},{5,4},{6,7},{7,6},{8,9},{9,8},{10,11... | collective-permute-start | bytes 2359304 | tf_op jit(solution)/shard_map/weights_swap/ppermute | solution.py:369
  18.3 11.6 %collective-permute-start.10 = (bf16[256,1024]{1,0:T(8,128)(2,1)S(1)}, bf16[256,1024]{1,0:T(8,128)(2,1)S(1)}, u32[]{:S(2)}, u32[]{:S(2)}) collective-permute-start(bf16[256,1024]{1,0:T(8,128)(2,1)S(1)} %collective-permute-done.6.near), channel_id=1, source_target_pairs={{0,4},{1,3},{4,8},{5,1},{8,12},{9,5},{12,14},{13,9},{14,10},{15,13... | collective-permute-start | bytes 1572872 | tf_op jit(solution)/shard_map/cotangent_2/ppermute | solution.py:369
  20.4 14.9 %collective-permute-start.13 = (bf16[1024,384]{1,0:T(8,128)(2,1)S(1)}, bf16[1024,384]{1,0:T(8,128)(2,1)S(1)}, u32[]{:S(2)}, u32[]{:S(2)}) collective-permute-start(bf16[1024,384]{1,0:T(8,128)(2,1)S(1)} %get-tuple-element.140.w_up.refs_1_), channel_id=1, source_target_pairs={{0,1},{1,0},{2,3},{3,2},{4,5},{5,4},{6,7},{7,6},{8,9},{9,8},{10,11... | collective-permute-start | bytes 2359304 | tf_op jit(solution)/shard_map/weights_swap/ppermute | solution.py:369
  24.2 11.1 %collective-permute-start.14 = (bf16[1024,384]{1,0:T(8,128)(2,1)S(1)}, bf16[1024,384]{1,0:T(8,128)(2,1)S(1)}, u32[]{:S(2)}, u32[]{:S(2)}) collective-permute-start(bf16[1024,384]{1,0:T(8,128)(2,1)S(1)} %get-tuple-element.141.w_down.refs_2_), channel_id=1, source_target_pairs={{0,1},{1,0},{2,3},{3,2},{4,5},{5,4},{6,7},{7,6},{8,9},{9,8},{10,11... | collective-permute-start | bytes 2359304 | tf_op jit(solution)/shard_map/weights_swap/ppermute | solution.py:369
  25.8 10.1 %collective-permute-start.9 = (bf16[272,1024]{1,0:T(8,128)(2,1)S(1)}, bf16[272,1024]{1,0:T(8,128)(2,1)S(1)}, u32[]{:S(2)}, u32[]{:S(2)}) collective-permute-start(bf16[272,1024]{1,0:T(8,128)(2,1)S(1)} %collective-permute-done.4.near), channel_id=1, source_target_pairs={{0,4},{1,3},{4,8},{5,1},{8,12},{9,5},{12,14},{13,9},{14,10},{15,13... | collective-permute-start | bytes 1671176 | tf_op jit(solution)/shard_map/tokens_3/ppermute | solution.py:369
  29.8 8.2 %collective-permute-start.15 = (bf16[272,1024]{1,0:T(8,128)(2,1)S(1)}, bf16[272,1024]{1,0:T(8,128)(2,1)S(1)}, u32[]{:S(2)}, u32[]{:S(2)}) collective-permute-start(bf16[272,1024]{1,0:T(8,128)(2,1)S(1)} %collective-permute-done.4.near), channel_id=1, source_target_pairs={{0,1},{1,0},{2,3},{3,2},{4,5},{5,4},{6,7},{7,6},{8,9},{9,8},{10,11... | collective-permute-start | bytes 1671176 | tf_op jit(solution)/shard_map/tokens_2_swap/ppermute | solution.py:369
  31.8 9.6 %collective-permute-start.17 = (bf16[256,1024]{1,0:T(8,128)(2,1)S(1)}, bf16[256,1024]{1,0:T(8,128)(2,1)S(1)}, u32[]{:S(2)}, u32[]{:S(2)}) collective-permute-start(bf16[256,1024]{1,0:T(8,128)(2,1)S(1)} %collective-permute-done.10.near), channel_id=1, source_target_pairs={{0,4},{1,3},{4,8},{5,1},{8,12},{9,5},{12,14},{13,9},{14,10},{15,13... | collective-permute-start | bytes 1572872 | tf_op jit(solution)/shard_map/cotangent_3/ppermute | solution.py:369
  35.8 9.8 %collective-permute-start.20 = (bf16[144,1024]{1,0:T(8,128)(2,1)S(1)}, bf16[144,1024]{1,0:T(8,128)(2,1)S(1)}, u32[]{:S(2)}, u32[]{:S(2)}) collective-permute-start(bf16[144,1024]{1,0:T(8,128)(2,1)S(1)} %slice.6), channel_id=1, source_target_pairs={{0,4},{1,3},{4,8},{5,1},{8,12},{9,5},{12,14},{13,9},{14,10},{15,13... | collective-permute-start | bytes 884744 | tf_op jit(solution)/shard_map/tokens_4/ppermute | solution.py:369
  41.4 11.9 %collective-permute-start.23 = (bf16[256,1024]{1,0:T(8,128)(2,1)S(1)}, bf16[256,1024]{1,0:T(8,128)(2,1)S(1)}, u32[]{:S(2)}, u32[]{:S(2)}) collective-permute-start(bf16[256,1024]{1,0:T(8,128)(2,1)S(1)} %collective-permute-done.17.near), channel_id=1, source_target_pairs={{0,1},{1,0},{2,3},{3,2},{4,5},{5,4},{6,7},{7,6},{8,9},{9,8},{10,11... | collective-permute-start | bytes 1572872 | tf_op jit(solution)/shard_map/cotangent_3_swap/ppermute | solution.py:369
  41.5 8.5 %collective-permute-start.22 = (bf16[128,1024]{1,0:T(8,128)(2,1)S(1)}, bf16[128,1024]{1,0:T(8,128)(2,1)S(1)}, u32[]{:S(2)}, u32[]{:S(2)}) collective-permute-start(bf16[128,1024]{1,0:T(8,128)(2,1)S(1)} %slice.7), channel_id=1, source_target_pairs={{0,4},{1,3},{4,8},{5,1},{8,12},{9,5},{12,14},{13,9},{14,10},{15,13... | collective-permute-start | bytes 786440 | tf_op jit(solution)/shard_map/cotangent_4/ppermute | solution.py:369
  55.0 9.4 %collective-permute-start.24 = (bf16[256,1024]{1,0:T(8,128)(2,1)S(1)}, bf16[256,1024]{1,0:T(8,128)(2,1)S(1)}, u32[]{:S(2)}, u32[]{:S(2)}) collective-permute-start(bf16[256,1024]{1,0:T(8,128)(2,1)S(1)} %mixed_sums_3.1), channel_id=1, source_target_pairs={{0,4},{1,3},{4,8},{5,1},{8,12},{9,5},{12,14},{13,9},{14,10},{15,13... | collective-permute-start | bytes 1572872 | tf_op jit(solution)/shard_map/mixed_3/ppermute | solution.py:369
  58.5 11.6 %collective-permute-start.32 = (bf16[256,1024]{1,0:T(8,128)(2,1)S(1)}, bf16[256,1024]{1,0:T(8,128)(2,1)S(1)}, u32[]{:S(2)}, u32[]{:S(2)}) collective-permute-start(bf16[256,1024]{1,0:T(8,128)(2,1)S(1)} %grad_sums_3.1), channel_id=1, source_target_pairs={{0,4},{1,3},{4,8},{5,1},{8,12},{9,5},{12,14},{13,9},{14,10},{15,13... | collective-permute-start | bytes 1572872 | tf_op jit(solution)/shard_map/grad_3/ppermute | solution.py:369
  60.6 9.5 %collective-permute-start.31 = (bf16[128,1024]{1,0:T(8,128)(2,1)S(1)}, bf16[128,1024]{1,0:T(8,128)(2,1)S(1)}, u32[]{:S(2)}, u32[]{:S(2)}) collective-permute-start(bf16[128,1024]{1,0:T(8,128)(2,1)S(1)} %get-tuple-element.184), channel_id=1, source_target_pairs={{0,1},{1,0},{2,3},{3,2},{4,5},{5,4},{6,7},{7,6},{8,9},{9,8},{10,11... | collective-permute-start | bytes 786440 | tf_op jit(solution)/shard_map/grad_2_swap/ppermute | solution.py:369
  64.8 10.9 %collective-permute-start.30 = (bf16[256,1024]{1,0:T(8,128)(2,1)S(1)}, bf16[256,1024]{1,0:T(8,128)(2,1)S(1)}, u32[]{:S(2)}, u32[]{:S(2)}) collective-permute-start(bf16[256,1024]{1,0:T(8,128)(2,1)S(1)} %mixed_sums_2.1), channel_id=1, source_target_pairs={{0,4},{1,3},{4,8},{5,1},{8,12},{9,5},{12,14},{13,9},{14,10},{15,13... | collective-permute-start | bytes 1572872 | tf_op jit(solution)/shard_map/mixed_2/ppermute | solution.py:369
  70.4 10.9 %collective-permute-start.36 = (bf16[256,1024]{1,0:T(8,128)(2,1)S(1)}, bf16[256,1024]{1,0:T(8,128)(2,1)S(1)}, u32[]{:S(2)}, u32[]{:S(2)}) collective-permute-start(bf16[256,1024]{1,0:T(8,128)(2,1)S(1)} %grad_sums_2.1), channel_id=1, source_target_pairs={{0,4},{1,3},{4,8},{5,1},{8,12},{9,5},{12,14},{13,9},{14,10},{15,13... | collective-permute-start | bytes 1572872 | tf_op jit(solution)/shard_map/grad_2/ppermute | solution.py:369
  71.8 9.5 %collective-permute-start.35 = (bf16[128,1024]{1,0:T(8,128)(2,1)S(1)}, bf16[128,1024]{1,0:T(8,128)(2,1)S(1)}, u32[]{:S(2)}, u32[]{:S(2)}) collective-permute-start(bf16[128,1024]{1,0:T(8,128)(2,1)S(1)} %get-tuple-element.200), channel_id=1, source_target_pairs={{0,1},{1,0},{2,3},{3,2},{4,5},{5,4},{6,7},{7,6},{8,9},{9,8},{10,11... | collective-permute-start | bytes 786440 | tf_op jit(solution)/shard_map/grad_1_swap/ppermute | solution.py:369
  76.0 8.1 %collective-permute-start.33 = (bf16[128,1024]{1,0:T(8,128)(2,1)S(1)}, bf16[128,1024]{1,0:T(8,128)(2,1)S(1)}, u32[]{:S(2)}, u32[]{:S(2)}) collective-permute-start(bf16[128,1024]{1,0:T(8,128)(2,1)S(1)} %get-tuple-element.197), channel_id=1, source_target_pairs={{0,4},{1,3},{4,8},{5,1},{8,12},{9,5},{12,14},{13,9},{14,10},{15,13... | collective-permute-start | bytes 786440 | tf_op jit(solution)/shard_map/mixed_1/ppermute | solution.py:369
  83.1 9.0 %collective-permute-start.39 = (bf16[128,1024]{1,0:T(8,128)(2,1)S(1)}, bf16[128,1024]{1,0:T(8,128)(2,1)S(1)}, u32[]{:S(2)}, u32[]{:S(2)}) collective-permute-start(bf16[128,1024]{1,0:T(8,128)(2,1)S(1)} %get-tuple-element.208), channel_id=1, source_target_pairs={{0,5},{1,2},{4,9},{5,0},{8,13},{9,4},{12,15},{13,8},{14,11},{15,12... | collective-permute-start | bytes 786440 | tf_op jit(solution)/shard_map/grad_1_crossing/ppermute | solution.py:369
  (17 other events, 90.9 us)
